TPU v7x, 32 devices: a whole 2x2x4 slice. The times are simulated.
32 devices in a mesh: slab: 4 (over y, x), row: 8 (over z, core).
Axes of the slice: x: 2, y: 2, z: 4, core: 2. Of those that a mesh axis runs over, the one named last changes fastest.
Arguments:
- forcing: bfloat16 [4, 4096, 64], P('slab', 'row'), may hold values from -6 to 6
- inflow: bfloat16 [4096, 64], P('row'), may hold values from -6 to 6
- self_solve: bfloat16 [4, 8, 512, 512], P('slab', 'row'), may hold values from -0.25 to 0.25
- greens: bfloat16 [4, 8, 8, 512, 512], P('slab', 'row'), may hold values from -0.125 to 0.125
- kept_cols: int32 [4, 8, 8], P('slab', 'row'), may hold values from 0 to 7, as said below
- counts: int32 [4, 8], P('slab', 'row'), may hold values from 2 to 8, as said below
Outputs:
- traces: bfloat16 [4, 4096, 64], P('slab', 'row')
Inputs may be any that keep to these rules, and one draw needn't show every extreme that they name: `kept_cols`: for each slab and tile row the 8 entries name distinct column tiles. `counts`: in every slab some tile row uses all 8 slots.
All inputs are finite; a program needn't handle non-finite values.
Results may differ from a plain program's by a relative error of at most 0.012.
Values may be sent and summed in bfloat16 or wider, within the bound.
No kernel may reach another device: no remote copies, remote signals or barrier semaphores. Data moves between devices by JAX's collectives and lax.ppermute only.
A program may use at most 64 MiB of HBM per device.

v0:
```python
import jax
import jax.numpy as jnp
from jax import lax
from jax.sharding import PartitionSpec as P

TILE = 512


def shifted(array, axis, by):
    size = lax.axis_size(axis)
    pairs = [(i, i + by) for i in range(size) if 0 <= i + by < size]
    return lax.ppermute(array, axis, pairs)


def advance(previous, inflow_cols, forcing_cols, green_row, cols_row, count_row, solve_row):
    arrived = shifted(previous, "slab", 1)
    first_slab = lax.axis_index("slab") == 0
    incoming = jnp.where(first_slab, inflow_cols, arrived)
    gathered = lax.all_gather(incoming, "row", axis=0, tiled=True)
    width = incoming.shape[1]
    tiles = gathered.reshape(-1, TILE, width)
    chosen = tiles[cols_row]
    slot_ids = jnp.arange(green_row.shape[0], dtype=jnp.int32)
    valid = slot_ids < count_row
    chosen = jnp.where(valid[:, None, None], chosen, jnp.zeros((), chosen.dtype))
    total = jnp.einsum("kij,kjw->iw", green_row, chosen, preferred_element_type=jnp.float32)
    coupled = (total + forcing_cols.astype(jnp.float32)).astype(jnp.bfloat16)
    return jnp.dot(solve_row, coupled, preferred_element_type=jnp.float32).astype(jnp.bfloat16)


def shards(forcing, inflow, self_solve, greens, kept_cols, counts):
    slab_count = lax.axis_size("slab")
    green_row = greens[0, 0]
    cols_row = kept_cols[0, 0]
    count_row = counts[0, 0]
    solve_row = self_solve[0, 0]
    source = forcing[0]
    columns = source.shape[1]
    previous = jnp.zeros((TILE, columns), jnp.bfloat16)
    for section in range(slab_count):
        previous = advance(previous, inflow, source, green_row, cols_row, count_row, solve_row)
    return previous[None]


def solution(mesh):
    placed = (
        P("slab", "row", None),
        P("row", None),
        P("slab", "row", None, None),
        P("slab", "row", None, None, None),
        P("slab", "row", None),
        P("slab", "row"),
    )
    return jax.shard_map(
        shards, mesh=mesh, in_specs=placed, out_specs=P("slab", "row", None), check_vma=False
    )
```

profile of v0, /device:TPU:13, one launch (start us, length us, event | category | flops | bytes accessed | tf_op | source)
XLA Modules:
  0.0 107.6 jit_solution(15627340045828583116)
XLA Ops:
  0.0 0.0 copy-start
  0.0 3.3 %collective-permute-start = (bf16[512,64]{0,1:T(8,128)(2,1)S(1)}, bf16[512,64]{0,1:T(8,128)(2,1)S(1)}, u32[]{:S(2)}, u32[]{:S(2)}) collective-permute-start(bf16[512,64]{0,1:T(8,128)(2,1)S(1)} %broadcast_in_dim.39), channel_id=1, source_target_pairs={{0,8},{8,16},{16,24},{1,9},{9,17},{17,25},{2,10},{10,18},{18,26},{... | collective-permute-start | bytes 196616 | tf_op jit(solution)/shard_map/ppermute | solution.py:12
  3.9 0.7 fusion.100
  4.6 1.5 %collective-permute-done = bf16[512,64]{0,1:T(8,128)(2,1)S(1)} collective-permute-done((bf16[512,64]{0,1:T(8,128)(2,1)S(1)}, bf16[512,64]{0,1:T(8,128)(2,1)S(1)}, u32[]{:S(2)}, u32[]{:S(2)}) %collective-permute-start) | collective-permute-done | bytes 65568 | tf_op jit(solution)/shard_map/ppermute | solution.py:12
  6.1 16.7 %all_gather.12 = bf16[4096,64]{0,1:T(8,128)(2,1)S(1)} all-gather(bf16[512,64]{0,1:T(8,128)(2,1)S(1)} %broadcast_select_fusion.3), channel_id=1, replica_groups=mesh['slab'=4,'row'=8] {'row'}, dimensions={0}, use_global_device_ids=true | all-gather | bytes 589824 | tf_op jit(solution)/shard_map/all_gather | solution.py:19
  22.8 0.6 gather_fusion
  23.4 0.0 copy-done
  23.4 0.0 copy-start.1
  23.4 3.8 %fusion.61 = bf16[512,64]{0,1:T(8,128)(2,1)S(1)} fusion(bf16[1,1,8,512,512]{4,3,2,1,0:T(8,128)(2,1)} %param.9, bf16[1,1,512,512]{3,2,1,0:T(8,128)(2,1)S(1)} %copy-done, bf16[8,512,64]{1,2,0:T(8,128)(2,1)S(1)} %gather_fusion, pred[8]{0:T(512)(128)(4,1)S(1)} %iota_compare_fusion, bf16[1,512,64]{1,2,0:T(8,128)(2,1)} %param.6), kind=kOutput, calls=%fused_computation.31 | convolution fusion | flops 302383104 | bytes 5373960 | tf_op jit(solution)/shard_map/dot_general | solution.py:28
  27.2 2.2 %collective-permute-start.1 = (bf16[512,64]{0,1:T(8,128)(2,1)S(1)}, bf16[512,64]{0,1:T(8,128)(2,1)S(1)}, u32[]{:S(2)}, u32[]{:S(2)}) collective-permute-start(bf16[512,64]{0,1:T(8,128)(2,1)S(1)} %fusion.61), channel_id=1, source_target_pairs={{0,8},{8,16},{16,24},{1,9},{9,17},{17,25},{2,10},{10,18},{18,26},{... | collective-permute-start | bytes 196616 | tf_op jit(solution)/shard_map/ppermute | solution.py:12
  29.5 4.1 %collective-permute-done.1 = bf16[512,64]{0,1:T(8,128)(2,1)S(1)} collective-permute-done((bf16[512,64]{0,1:T(8,128)(2,1)S(1)}, bf16[512,64]{0,1:T(8,128)(2,1)S(1)}, u32[]{:S(2)}, u32[]{:S(2)}) %collective-permute-start.1) | collective-permute-done | bytes 65568 | tf_op jit(solution)/shard_map/ppermute | solution.py:12
  33.6 15.8 %all_gather.13 = bf16[4096,64]{0,1:T(8,128)(2,1)S(1)} all-gather(bf16[512,64]{0,1:T(8,128)(2,1)S(1)} %broadcast_select_fusion.2), channel_id=1, replica_groups=mesh['slab'=4,'row'=8] {'row'}, dimensions={0}, use_global_device_ids=true | all-gather | bytes 589824 | tf_op jit(solution)/shard_map/all_gather | solution.py:19
  49.4 0.6 gather_fusion.1
  50.0 3.8 %fusion.56 = bf16[512,64]{0,1:T(8,128)(2,1)S(1)} fusion(bf16[1,1,8,512,512]{4,3,2,1,0:T(8,128)(2,1)} %param.9, bf16[1,1,512,512]{3,2,1,0:T(8,128)(2,1)S(1)} %copy-done, bf16[8,512,64]{1,2,0:T(8,128)(2,1)S(1)} %gather_fusion.1, pred[8]{0:T(512)(128)(4,1)S(1)} %iota_compare_fusion, bf16[1,512,64]{1,2,0:T(8,128)(2,1)S(1)} %copy-done.1), kind=kOutput, calls=%fused_computation.30 | convolution fusion | flops 302383104 | bytes 5373960 | tf_op jit(solution)/shard_map/dot_general | solution.py:28
  53.8 1.9 %collective-permute-start.2 = (bf16[512,64]{0,1:T(8,128)(2,1)S(1)}, bf16[512,64]{0,1:T(8,128)(2,1)S(1)}, u32[]{:S(2)}, u32[]{:S(2)}) collective-permute-start(bf16[512,64]{0,1:T(8,128)(2,1)S(1)} %fusion.56), channel_id=1, source_target_pairs={{0,8},{8,16},{16,24},{1,9},{9,17},{17,25},{2,10},{10,18},{18,26},{... | collective-permute-start | bytes 196616 | tf_op jit(solution)/shard_map/ppermute | solution.py:12
  55.7 4.4 %collective-permute-done.2 = bf16[512,64]{0,1:T(8,128)(2,1)S(1)} collective-permute-done((bf16[512,64]{0,1:T(8,128)(2,1)S(1)}, bf16[512,64]{0,1:T(8,128)(2,1)S(1)}, u32[]{:S(2)}, u32[]{:S(2)}) %collective-permute-start.2) | collective-permute-done | bytes 65568 | tf_op jit(solution)/shard_map/ppermute | solution.py:12
  60.2 15.8 %all_gather.14 = bf16[4096,64]{0,1:T(8,128)(2,1)S(1)} all-gather(bf16[512,64]{0,1:T(8,128)(2,1)S(1)} %broadcast_select_fusion.1), channel_id=1, replica_groups=mesh['slab'=4,'row'=8] {'row'}, dimensions={0}, use_global_device_ids=true | all-gather | bytes 589824 | tf_op jit(solution)/shard_map/all_gather | solution.py:19
  76.0 0.6 gather_fusion.2
  76.6 3.8 %fusion.51 = bf16[512,64]{0,1:T(8,128)(2,1)S(1)} fusion(bf16[1,1,8,512,512]{4,3,2,1,0:T(8,128)(2,1)} %param.9, bf16[1,1,512,512]{3,2,1,0:T(8,128)(2,1)S(1)} %copy-done, bf16[8,512,64]{1,2,0:T(8,128)(2,1)S(1)} %gather_fusion.2, pred[8]{0:T(512)(128)(4,1)S(1)} %iota_compare_fusion, bf16[1,512,64]{1,2,0:T(8,128)(2,1)S(1)} %copy-done.1), kind=kOutput, calls=%fused_computation.29 | convolution fusion | flops 302383104 | bytes 5373960 | tf_op jit(solution)/shard_map/dot_general | solution.py:28
  80.4 1.9 %collective-permute-start.3 = (bf16[512,64]{0,1:T(8,128)(2,1)S(1)}, bf16[512,64]{0,1:T(8,128)(2,1)S(1)}, u32[]{:S(2)}, u32[]{:S(2)}) collective-permute-start(bf16[512,64]{0,1:T(8,128)(2,1)S(1)} %fusion.51), channel_id=1, source_target_pairs={{0,8},{8,16},{16,24},{1,9},{9,17},{17,25},{2,10},{10,18},{18,26},{... | collective-permute-start | bytes 196616 | tf_op jit(solution)/shard_map/ppermute | solution.py:12
  82.3 4.4 %collective-permute-done.3 = bf16[512,64]{0,1:T(8,128)(2,1)S(1)} collective-permute-done((bf16[512,64]{0,1:T(8,128)(2,1)S(1)}, bf16[512,64]{0,1:T(8,128)(2,1)S(1)}, u32[]{:S(2)}, u32[]{:S(2)}) %collective-permute-start.3) | collective-permute-done | bytes 65568 | tf_op jit(solution)/shard_map/ppermute | solution.py:12
  86.7 15.8 %all_gather.15 = bf16[4096,64]{0,1:T(8,128)(2,1)S(1)} all-gather(bf16[512,64]{0,1:T(8,128)(2,1)S(1)} %broadcast_select_fusion), channel_id=1, replica_groups=mesh['slab'=4,'row'=8] {'row'}, dimensions={0}, use_global_device_ids=true | all-gather | bytes 589824 | tf_op jit(solution)/shard_map/all_gather | solution.py:19
  102.6 0.6 gather_fusion.3
  103.2 4.4 %fusion.46 = bf16[1,512,64]{1,2,0:T(8,128)(2,1)} fusion(bf16[1,1,8,512,512]{4,3,2,1,0:T(8,128)(2,1)} %param.9, bf16[1,1,512,512]{3,2,1,0:T(8,128)(2,1)S(1)} %copy-done, bf16[8,512,64]{1,2,0:T(8,128)(2,1)S(1)} %gather_fusion.3, pred[8]{0:T(512)(128)(4,1)S(1)} %iota_compare_fusion, bf16[1,512,64]{1,2,0:T(8,128)(2,1)S(1)} %copy-done.1), kind=kOutput, calls=%fused_computation.28 | convolution fusion | flops 302383104 | bytes 5373960 | tf_op jit(solution)/shard_map/dot_general | solution.py:28
  (14 shorter events, 0.2 us)
Async XLA Ops:
  0.0 23.4 %copy-start = (bf16[1,1,512,512]{3,2,1,0:T(8,128)(2,1)S(1)}, bf16[1,1,512,512]{3,2,1,0:T(8,128)(2,1)}, u32[]{:S(2)}) copy-start(bf16[1,1,512,512]{3,2,1,0:T(8,128)(2,1)} %param.8) | copy-start | bytes 1572868
  0.0 6.0 %collective-permute-start = (bf16[512,64]{0,1:T(8,128)(2,1)S(1)}, bf16[512,64]{0,1:T(8,128)(2,1)S(1)}, u32[]{:S(2)}, u32[]{:S(2)}) collective-permute-start(bf16[512,64]{0,1:T(8,128)(2,1)S(1)} %broadcast_in_dim.39), channel_id=1, source_target_pairs={{0,8},{8,16},{16,24},{1,9},{9,17},{17,25},{2,10},{10,18},{18,26},{... | collective-permute-start | bytes 196616 | tf_op jit(solution)/shard_map/ppermute | solution.py:12
  22.8 10.8 %copy-start.2 = (bf16[512,64]{0,1:T(8,128)(2,1)S(1)}, bf16[512,64]{0,1:T(8,128)(2,1)}, u32[]{:S(2)}) copy-start(bf16[512,64]{0,1:T(8,128)(2,1)} %param.7) | copy-start | bytes 196612
  23.4 26.6 %copy-start.1 = (bf16[1,512,64]{1,2,0:T(8,128)(2,1)S(1)}, bf16[1,512,64]{1,2,0:T(8,128)(2,1)}, u32[]{:S(2)}) copy-start(bf16[1,512,64]{1,2,0:T(8,128)(2,1)} %param.6) | copy-start | bytes 196612
  27.2 6.3 %collective-permute-start.1 = (bf16[512,64]{0,1:T(8,128)(2,1)S(1)}, bf16[512,64]{0,1:T(8,128)(2,1)S(1)}, u32[]{:S(2)}, u32[]{:S(2)}) collective-permute-start(bf16[512,64]{0,1:T(8,128)(2,1)S(1)} %fusion.61), channel_id=1, source_target_pairs={{0,8},{8,16},{16,24},{1,9},{9,17},{17,25},{2,10},{10,18},{18,26},{... | collective-permute-start | bytes 196616 | tf_op jit(solution)/shard_map/ppermute | solution.py:12
  53.8 6.3 %collective-permute-start.2 = (bf16[512,64]{0,1:T(8,128)(2,1)S(1)}, bf16[512,64]{0,1:T(8,128)(2,1)S(1)}, u32[]{:S(2)}, u32[]{:S(2)}) collective-permute-start(bf16[512,64]{0,1:T(8,128)(2,1)S(1)} %fusion.56), channel_id=1, source_target_pairs={{0,8},{8,16},{16,24},{1,9},{9,17},{17,25},{2,10},{10,18},{18,26},{... | collective-permute-start | bytes 196616 | tf_op jit(solution)/shard_map/ppermute | solution.py:12
  80.4 6.3 %collective-permute-start.3 = (bf16[512,64]{0,1:T(8,128)(2,1)S(1)}, bf16[512,64]{0,1:T(8,128)(2,1)S(1)}, u32[]{:S(2)}, u32[]{:S(2)}) collective-permute-start(bf16[512,64]{0,1:T(8,128)(2,1)S(1)} %fusion.51), channel_id=1, source_target_pairs={{0,8},{8,16},{16,24},{1,9},{9,17},{17,25},{2,10},{10,18},{18,26},{... | collective-permute-start | bytes 196616 | tf_op jit(solution)/shard_map/ppermute | solution.py:12
where the time goes:
time: 108 us
  blocking collectives  64.1 us (59%)
  matrix products  15.7 us (15%)
  waiting for transfers between devices  14.4 us (13%)
  starting transfers between devices  9.31 us (9%)
  local copies, waits for them, and re-layouts  2.49 us (2%)
    all_gather x4, blocking collectives, advance(): gathered = lax.all_gather(incoming, 'row', axis=0, tiled=True)  64.1 us
    dot_general x4, matrix products, advance(): jnp.dot(solve_row, coupled, preferred_element_type=jnp.float32)  15.7 us
    ppermute x4, waiting for transfers between devices, shifted(): return lax.ppermute(array, axis, pairs)  14.4 us
    ppermute x4, starting transfers between devices, shifted(): return lax.ppermute(array, axis, pairs)  9.31 us
    gather x4, local copies, waits for them, and re-layouts, advance(): chosen = tiles[cols_row]  2.32 us
  transfers between devices with their start and end apart: 4, of which 4 were waited for; matrix products, arithmetic and copies ran while one was open for 1% of the time, Pallas kernels for 0%

commit v1 on v0

v1 whole, which is shorter than its diff:
```python
import functools

import jax
import jax.numpy as jnp
from jax import lax
from jax.experimental import pallas as pl
from jax.experimental.pallas import tpu as pltpu
from jax.sharding import PartitionSpec as P

CORES = 2
VMEM_LIMIT = 48 * 2**20
CONTRACT_LAST = (((1,), (1,)), ((), ()))
IN_VMEM = pl.BlockSpec(memory_space=pltpu.VMEM)
IN_SMEM = pl.BlockSpec(memory_space=pltpu.SMEM)
ANYWHERE = pl.BlockSpec(memory_space=pl.ANY)


def params():
    return pltpu.CompilerParams(vmem_limit_bytes=VMEM_LIMIT)


def place_kernel(chips, cols_ref, count_ref, greens_ref, placed_ref, sems):
    slots, positions = greens_ref.shape[0], placed_ref.shape[0]
    me = lax.axis_index("row")
    chip, core = me // CORES, me % CORES
    if positions > slots:
        placed_ref[...] = jnp.zeros_like(placed_ref)
    copies = []
    for slot in range(slots):
        column = cols_ref[slot]
        hop = lax.rem(chip - column // CORES + chips, chips)
        position = jnp.where(column % CORES == core, 0, chips) + hop
        copy = pltpu.make_async_copy(greens_ref.at[slot], placed_ref.at[position], sems.at[slot])
        used = slot < count_ref[0]
        copies.append((used, copy))

        @pl.when(used)
        def _():
            copy.start()

        if positions == slots:

            @pl.when(jnp.logical_not(used))
            def _():
                placed_ref[position] = jnp.zeros(placed_ref.shape[1:], placed_ref.dtype)

    for used, copy in copies:

        @pl.when(used)
        def _():
            copy.wait()


def place(chips, cols, count, greens):
    slots, rows, depth = greens.shape
    return pl.pallas_call(
        functools.partial(place_kernel, chips),
        out_shape=pltpu.VMEM((chips * CORES, rows, depth), greens.dtype),
        in_specs=[IN_SMEM, IN_SMEM, ANYWHERE],
        out_specs=IN_VMEM,
        scratch_shapes=[pltpu.SemaphoreType.DMA((slots,))],
        compiler_params=params(),
        name="place",
    )(cols, count, greens)


def products(tiles, placed_ref, first):
    total = None
    for offset, tile in enumerate(tiles):
        term = lax.dot_general(
            tile[...], placed_ref[first + offset], CONTRACT_LAST, preferred_element_type=jnp.float32
        )
        total = term if total is None else total + term
    return total


def early_kernel(section, placed_ref, *refs):
    tiles, total_ref = refs[:-1], refs[-1]

    @pl.when(lax.axis_index("slab") == section)
    def _():
        total_ref[...] = products(tiles, placed_ref, 0)


def early(section, placed, tiles):
    return pl.pallas_call(
        functools.partial(early_kernel, section),
        out_shape=pltpu.VMEM(tiles[0].shape, jnp.float32),
        in_specs=[IN_VMEM] * (1 + len(tiles)),
        out_specs=IN_VMEM,
        compiler_params=params(),
        name="early_tiles",
    )(placed, *tiles)


def late_kernel(section, placed_ref, total_ref, tile_ref, source_ref, solve_ref, trace_in, trace_ref):
    @pl.when(lax.axis_index("slab") == section)
    def _():
        total = total_ref[...] + products([tile_ref], placed_ref, placed_ref.shape[0] - 1)
        coupled = (total + source_ref[...].astype(jnp.float32)).astype(jnp.bfloat16)
        trace_ref[...] = lax.dot_general(
            coupled, solve_ref[...], CONTRACT_LAST, preferred_element_type=jnp.float32
        ).astype(trace_ref.dtype)


def late(section, placed, total, tile, source, solve, trace):
    return pl.pallas_call(
        functools.partial(late_kernel, section),
        out_shape=pltpu.VMEM(trace.shape, trace.dtype),
        in_specs=[IN_VMEM] * 6,
        out_specs=IN_VMEM,
        input_output_aliases={5: 0},
        compiler_params=params(),
        name="late_tile_and_solve",
    )(placed, total, tile, source, solve, trace)


def swapped(tile, rows):
    return lax.ppermute(tile, "row", [(r, r ^ 1) for r in range(rows)])


def direct(forcing, inflow, self_solve, greens, kept_cols, counts):
    slabs, rows = lax.axis_size("slab"), lax.axis_size("row")
    chips = rows // CORES
    placed = place(chips, kept_cols[0, 0], counts[0], greens[0, 0])
    source = forcing[0].T
    solve = self_solve[0, 0]
    trace = inflow.T
    own = [trace]
    for hop in range(1, chips):
        own.append(lax.ppermute(trace, "row", [(r, (r + hop * CORES) % rows) for r in range(rows)]))
    for section in range(slabs):
        if section > 0:
            before, now = (section - 1) * rows, section * rows
            own = [
                lax.ppermute(
                    trace, ("slab", "row"), [(before + r, now + (r + hop * CORES) % rows) for r in range(rows)]
                )
                for hop in range(chips)
            ]
        other = [swapped(tile, rows) for tile in own]
        total = early(section, placed, own + other[:-1])
        trace = late(section, placed, total, other[-1], source, solve, trace)
    return trace.T[None]


def shifted(array, axis, by):
    size = lax.axis_size(axis)
    return lax.ppermute(array, axis, [(i, i + by) for i in range(size) if 0 <= i + by < size])


def gathering(forcing, inflow, self_solve, greens, kept_cols, counts):
    source, green_row, solve = forcing[0], greens[0, 0], self_solve[0, 0]
    valid = jnp.arange(green_row.shape[0], dtype=jnp.int32) < counts[0, 0]
    incoming = inflow
    for section in range(lax.axis_size("slab")):
        if section > 0:
            arrived = shifted(trace, "slab", 1)
            incoming = jnp.where(lax.axis_index("slab") == 0, inflow, arrived)
        gathered = lax.all_gather(incoming, "row", axis=0)
        chosen = gathered[kept_cols[0, 0]]
        chosen = jnp.where(valid[:, None, None], chosen, jnp.zeros((), chosen.dtype))
        total = jnp.einsum("kij,kjw->iw", green_row, chosen, preferred_element_type=jnp.float32)
        coupled = (total + source.astype(jnp.float32)).astype(jnp.bfloat16)
        trace = jnp.dot(solve, coupled, preferred_element_type=jnp.float32).astype(jnp.bfloat16)
    return trace[None]


def shards(forcing, inflow, self_solve, greens, kept_cols, counts):
    rows, slots = lax.axis_size("row"), greens.shape[2]
    if rows % CORES == 0 and rows <= 2 * slots:
        return direct(forcing, inflow, self_solve, greens, kept_cols, counts)
    return gathering(forcing, inflow, self_solve, greens, kept_cols, counts)


def solution(mesh):
    placed = (
        P("slab", "row", None),
        P("row", None),
        P("slab", "row", None, None),
        P("slab", "row", None, None, None),
        P("slab", "row", None),
        P("slab", "row"),
    )
    return jax.shard_map(
        shards, mesh=mesh, in_specs=placed, out_specs=P("slab", "row", None), check_vma=False
    )
```

time: 108 us -> 58 us (0.54)
  the two profiles are of different devices: /device:TPU:13 before, /device:TPU:7 now
where the time goes in v1:
time: 58 us; the launch traced here: 57.6 us
  starting transfers between devices  24.9 us (43%)
  waiting for transfers between devices  24.4 us (42%)
  Pallas kernels  4.36 us (8%)
  local copies, waits for them, and re-layouts  3.09 us (5%)
  between operations  0.88 us (2%)
    ppermute x12, waiting for transfers between devices, direct(): lax.ppermute(trace, ('slab', 'row'), [(before + r, now + (r + hop * CORES...  20.8 us
    ppermute x12, starting transfers between devices, direct(): lax.ppermute(trace, ('slab', 'row'), [(before + r, now + (r + hop * CORES...  10.5 us
    ppermute x16, starting transfers between devices, swapped(): return lax.ppermute(tile, 'row', [(r, r ^ 1) for r in range(rows)])  9.78 us
    ppermute x3, starting transfers between devices, direct(): lax.ppermute(trace, 'row', [(r, (r + hop * CORES) % rows) for r in range(...  4.67 us
    unnamed x8, local copies, waits for them, and re-layouts  3.09 us
    ppermute x16, waiting for transfers between devices, swapped(): return lax.ppermute(tile, 'row', [(r, r ^ 1) for r in range(rows)])  2.84 us
    pallas_call x1, Pallas kernels, place(): pl.pallas_call(functools.partial(place_kernel, chips), out_shape=pltpu.VM...  2.64 us
    pallas_call x4, Pallas kernels, early(): pl.pallas_call(functools.partial(early_kernel, section), out_shape=pltpu....  1.23 us
  transfers between devices with their start and end apart: 31, of which 12 were waited for; matrix products, arithmetic and copies ran while one was open for 0% of the time, Pallas kernels for 7%

profile of v1, /device:TPU:7, one launch (start us, length us, event | category | flops | bytes accessed | tf_op | source)
XLA Modules:
  0.0 57.6 jit_solution(14534738278232740062)
XLA Ops:
  0.0 0.8 %copy.15 = bf16[512,64]{0,1:T(8,128)(2,1)S(1)} copy(bf16[512,64]{0,1:T(8,128)(2,1)} %param.7) | data formatting | bytes 131072
  0.8 1.3 %collective-permute-start = (bf16[64,512]{1,0:T(8,128)(2,1)S(1)}, bf16[64,512]{1,0:T(8,128)(2,1)S(1)}, u32[]{:S(2)}, u32[]{:S(2)}) collective-permute-start(bf16[64,512]{1,0:T(8,128)(2,1)S(1)} %bitcast.12), channel_id=1, source_target_pairs={{0,2},{1,3},{2,4},{3,5},{4,6},{5,7},{6,0},{7,1},{8,10},{9,11},{10,... | collective-permute-start | bytes 196616 | tf_op jit(solution)/shard_map/ppermute | solution.py:131
  2.1 2.3 %collective-permute-start.1 = (bf16[64,512]{1,0:T(8,128)(2,1)S(1)}, bf16[64,512]{1,0:T(8,128)(2,1)S(1)}, u32[]{:S(2)}, u32[]{:S(2)}) collective-permute-start(bf16[64,512]{1,0:T(8,128)(2,1)S(1)} %bitcast.13), channel_id=1, source_target_pairs={{0,4},{1,5},{2,6},{3,7},{4,0},{5,1},{6,2},{7,3},{8,12},{9,13},{10,... | collective-permute-start | bytes 196616 | tf_op jit(solution)/shard_map/ppermute | solution.py:131
  4.4 1.1 %collective-permute-start.2 = (bf16[64,512]{1,0:T(8,128)(2,1)S(1)}, bf16[64,512]{1,0:T(8,128)(2,1)S(1)}, u32[]{:S(2)}, u32[]{:S(2)}) collective-permute-start(bf16[64,512]{1,0:T(8,128)(2,1)S(1)} %bitcast.14), channel_id=1, source_target_pairs={{0,6},{1,7},{2,0},{3,1},{4,2},{5,3},{6,4},{7,5},{8,14},{9,15},{10,... | collective-permute-start | bytes 196616 | tf_op jit(solution)/shard_map/ppermute | solution.py:131
  5.5 1.5 %collective-permute-start.3 = (bf16[64,512]{1,0:T(8,128)(2,1)S(1)}, bf16[64,512]{1,0:T(8,128)(2,1)S(1)}, u32[]{:S(2)}, u32[]{:S(2)}) collective-permute-start(bf16[64,512]{1,0:T(8,128)(2,1)S(1)} %bitcast.15), channel_id=1, source_target_pairs={{0,1},{1,0},{2,3},{3,2},{4,5},{5,4},{6,7},{7,6},{8,9},{9,8},{10,11... | collective-permute-start | bytes 196616 | tf_op jit(solution)/shard_map/ppermute | solution.py:119
  7.0 1.0 %collective-permute-start.4 = (bf16[64,512]{1,0:T(8,128)(2,1)S(1)}, bf16[64,512]{1,0:T(8,128)(2,1)S(1)}, u32[]{:S(2)}, u32[]{:S(2)}) collective-permute-start(bf16[64,512]{1,0:T(8,128)(2,1)S(1)} %collective-permute-done.refs_1_), channel_id=1, source_target_pairs={{0,1},{1,0},{2,3},{3,2},{4,5},{5,4},{6,7},{7,6},{8,9},{9,8},{10,11... | collective-permute-start | bytes 196616 | tf_op jit(solution)/shard_map/ppermute | solution.py:119
  8.0 0.7 %collective-permute-done.1.refs_2_ = bf16[64,512]{1,0:T(8,128)(2,1)S(1)} collective-permute-done((bf16[64,512]{1,0:T(8,128)(2,1)S(1)}, bf16[64,512]{1,0:T(8,128)(2,1)S(1)}, u32[]{:S(2)}, u32[]{:S(2)}) %collective-permute-start.1) | collective-permute-done | bytes 65568 | tf_op jit(solution)/shard_map/ppermute | solution.py:131
  8.7 1.7 %collective-permute-start.5 = (bf16[64,512]{1,0:T(8,128)(2,1)S(1)}, bf16[64,512]{1,0:T(8,128)(2,1)S(1)}, u32[]{:S(2)}, u32[]{:S(2)}) collective-permute-start(bf16[64,512]{1,0:T(8,128)(2,1)S(1)} %collective-permute-done.1.refs_2_), channel_id=1, source_target_pairs={{0,1},{1,0},{2,3},{3,2},{4,5},{5,4},{6,7},{7,6},{8,9},{9,8},{10,11... | collective-permute-start | bytes 196616 | tf_op jit(solution)/shard_map/ppermute | solution.py:119
  11.8 2.6 %place.1.placed_ref = bf16[8,512,512]{2,1,0:T(8,128)(2,1)S(1)} custom-call(s32[8]{0:T(128)S(1)} %bitcast.27, s32[1]{0:T(128)} %bitcast.11.count_ref, bf16[8,512,512]{2,1,0:T(8,128)(2,1)} %bitcast.28), custom_call_target="tpu_custom_call" | custom-call | tf_op jit(solution)/shard_map/place/pallas_call | solution.py:56
  14.5 1.0 %copy-done = bf16[1,1,512,512]{3,2,1,0:T(8,128)(2,1)S(1)} copy-done((bf16[1,1,512,512]{3,2,1,0:T(8,128)(2,1)S(1)}, bf16[1,1,512,512]{3,2,1,0:T(8,128)(2,1)}, u32[]{:S(2)}) %copy-start) | copy-done | bytes 524312
  16.1 0.7 %collective-permute-start.8 = (bf16[64,512]{1,0:T(8,128)(2,1)S(1)}, bf16[64,512]{1,0:T(8,128)(2,1)S(1)}, u32[]{:S(2)}, u32[]{:S(2)}) collective-permute-start(bf16[64,512]{1,0:T(8,128)(2,1)S(1)} %late_tile_and_solve.4.trace_in), channel_id=1, source_target_pairs={{0,10},{1,11},{2,12},{3,13},{4,14},{5,15},{6,8},{7,9}} | collective-permute-start | bytes 196616 | tf_op jit(solution)/shard_map/ppermute | solution.py:136
  16.8 0.7 %collective-permute-start.9 = (bf16[64,512]{1,0:T(8,128)(2,1)S(1)}, bf16[64,512]{1,0:T(8,128)(2,1)S(1)}, u32[]{:S(2)}, u32[]{:S(2)}) collective-permute-start(bf16[64,512]{1,0:T(8,128)(2,1)S(1)} %late_tile_and_solve.4.trace_in), channel_id=1, source_target_pairs={{0,12},{1,13},{2,14},{3,15},{4,8},{5,9},{6,10},{7,11}} | collective-permute-start | bytes 196616 | tf_op jit(solution)/shard_map/ppermute | solution.py:136
  18.1 0.7 %collective-permute-start.11 = (bf16[64,512]{1,0:T(8,128)(2,1)S(1)}, bf16[64,512]{1,0:T(8,128)(2,1)S(1)}, u32[]{:S(2)}, u32[]{:S(2)}) collective-permute-start(bf16[64,512]{1,0:T(8,128)(2,1)S(1)} %collective-permute-done.7.refs_0_), channel_id=1, source_target_pairs={{0,1},{1,0},{2,3},{3,2},{4,5},{5,4},{6,7},{7,6},{8,9},{9,8},{10,11... | collective-permute-start | bytes 196616 | tf_op jit(solution)/shard_map/ppermute | solution.py:119
  25.4 1.3 %collective-permute-start.23 = (bf16[64,512]{1,0:T(8,128)(2,1)S(1)}, bf16[64,512]{1,0:T(8,128)(2,1)S(1)}, u32[]{:S(2)}, u32[]{:S(2)}) collective-permute-start(bf16[64,512]{1,0:T(8,128)(2,1)S(1)} %late_tile_and_solve.6.trace_in), channel_id=1, source_target_pairs={{16,24},{17,25},{18,26},{19,27},{20,28},{21,29},{22,30},{23,31}} | collective-permute-start | bytes 196616 | tf_op jit(solution)/shard_map/ppermute | solution.py:136
  26.6 1.3 %collective-permute-start.24 = (bf16[64,512]{1,0:T(8,128)(2,1)S(1)}, bf16[64,512]{1,0:T(8,128)(2,1)S(1)}, u32[]{:S(2)}, u32[]{:S(2)}) collective-permute-start(bf16[64,512]{1,0:T(8,128)(2,1)S(1)} %late_tile_and_solve.6.trace_in), channel_id=1, source_target_pairs={{16,26},{17,27},{18,28},{19,29},{20,30},{21,31},{22,24},{23,25}} | collective-permute-start | bytes 196616 | tf_op jit(solution)/shard_map/ppermute | solution.py:136
  27.9 1.3 %collective-permute-start.25 = (bf16[64,512]{1,0:T(8,128)(2,1)S(1)}, bf16[64,512]{1,0:T(8,128)(2,1)S(1)}, u32[]{:S(2)}, u32[]{:S(2)}) collective-permute-start(bf16[64,512]{1,0:T(8,128)(2,1)S(1)} %late_tile_and_solve.6.trace_in), channel_id=1, source_target_pairs={{16,28},{17,29},{18,30},{19,31},{20,24},{21,25},{22,26},{23,27}} | collective-permute-start | bytes 196616 | tf_op jit(solution)/shard_map/ppermute | solution.py:136
  29.2 1.3 %collective-permute-start.26 = (bf16[64,512]{1,0:T(8,128)(2,1)S(1)}, bf16[64,512]{1,0:T(8,128)(2,1)S(1)}, u32[]{:S(2)}, u32[]{:S(2)}) collective-permute-start(bf16[64,512]{1,0:T(8,128)(2,1)S(1)} %late_tile_and_solve.6.trace_in), channel_id=1, source_target_pairs={{16,30},{17,31},{18,24},{19,25},{20,26},{21,27},{22,28},{23,29}} | collective-permute-start | bytes 196616 | tf_op jit(solution)/shard_map/ppermute | solution.py:136
  30.5 17.4 %collective-permute-done.23.refs_0_ = bf16[64,512]{1,0:T(8,128)(2,1)S(1)} collective-permute-done((bf16[64,512]{1,0:T(8,128)(2,1)S(1)}, bf16[64,512]{1,0:T(8,128)(2,1)S(1)}, u32[]{:S(2)}, u32[]{:S(2)}) %collective-permute-start.23) | collective-permute-done | bytes 65568 | tf_op jit(solution)/shard_map/ppermute | solution.py:136
  48.0 0.9 %collective-permute-start.27 = (bf16[64,512]{1,0:T(8,128)(2,1)S(1)}, bf16[64,512]{1,0:T(8,128)(2,1)S(1)}, u32[]{:S(2)}, u32[]{:S(2)}) collective-permute-start(bf16[64,512]{1,0:T(8,128)(2,1)S(1)} %collective-permute-done.23.refs_0_), channel_id=1, source_target_pairs={{0,1},{1,0},{2,3},{3,2},{4,5},{5,4},{6,7},{7,6},{8,9},{9,8},{10,11... | collective-permute-start | bytes 196616 | tf_op jit(solution)/shard_map/ppermute | solution.py:119
  48.8 3.3 %collective-permute-done.24.refs_1_ = bf16[64,512]{1,0:T(8,128)(2,1)S(1)} collective-permute-done((bf16[64,512]{1,0:T(8,128)(2,1)S(1)}, bf16[64,512]{1,0:T(8,128)(2,1)S(1)}, u32[]{:S(2)}, u32[]{:S(2)}) %collective-permute-start.24) | collective-permute-done | bytes 65568 | tf_op jit(solution)/shard_map/ppermute | solution.py:136
  52.2 1.1 %collective-permute-start.28 = (bf16[64,512]{1,0:T(8,128)(2,1)S(1)}, bf16[64,512]{1,0:T(8,128)(2,1)S(1)}, u32[]{:S(2)}, u32[]{:S(2)}) collective-permute-start(bf16[64,512]{1,0:T(8,128)(2,1)S(1)} %collective-permute-done.24.refs_1_), channel_id=1, source_target_pairs={{0,1},{1,0},{2,3},{3,2},{4,5},{5,4},{6,7},{7,6},{8,9},{9,8},{10,11... | collective-permute-start | bytes 196616 | tf_op jit(solution)/shard_map/ppermute | solution.py:119
  53.3 1.0 %collective-permute-start.29 = (bf16[64,512]{1,0:T(8,128)(2,1)S(1)}, bf16[64,512]{1,0:T(8,128)(2,1)S(1)}, u32[]{:S(2)}, u32[]{:S(2)}) collective-permute-start(bf16[64,512]{1,0:T(8,128)(2,1)S(1)} %collective-permute-done.25.refs_2_), channel_id=1, source_target_pairs={{0,1},{1,0},{2,3},{3,2},{4,5},{5,4},{6,7},{7,6},{8,9},{9,8},{10,11... | collective-permute-start | bytes 196616 | tf_op jit(solution)/shard_map/ppermute | solution.py:119
  54.5 0.8 %collective-permute-done.29.refs_6_ = bf16[64,512]{1,0:T(8,128)(2,1)S(1)} collective-permute-done((bf16[64,512]{1,0:T(8,128)(2,1)S(1)}, bf16[64,512]{1,0:T(8,128)(2,1)S(1)}, u32[]{:S(2)}, u32[]{:S(2)}) %collective-permute-start.29) | collective-permute-done | bytes 65568 | tf_op jit(solution)/shard_map/ppermute | solution.py:119
  55.3 1.2 %early_tiles.7.total_ref = f32[64,512]{1,0:T(8,128)S(1)} custom-call(bf16[8,512,512]{2,1,0:T(8,128)(2,1)S(1)} %place.1.placed_ref, bf16[64,512]{1,0:T(8,128)(2,1)S(1)} %collective-permute-done.23.refs_0_, bf16[64,512]{1,0:T(8,128)(2,1)S(1)} %collective-permute-done.24.refs_1_, bf16[64,512]{1,0:T(8,128)(2,1)S(1)} %collective-permute-done.25.refs_2_, ...), custom_call_target="tpu_custom_call" | custom-call | tf_op jit(solution)/shard_map/early_tiles/pallas_call | solution.py:86
  (55 shorter events, 9.7 us)
Async XLA Ops:
  0.8 6.2 %collective-permute-start = (bf16[64,512]{1,0:T(8,128)(2,1)S(1)}, bf16[64,512]{1,0:T(8,128)(2,1)S(1)}, u32[]{:S(2)}, u32[]{:S(2)}) collective-permute-start(bf16[64,512]{1,0:T(8,128)(2,1)S(1)} %bitcast.12), channel_id=1, source_target_pairs={{0,2},{1,3},{2,4},{3,5},{4,6},{5,7},{6,0},{7,1},{8,10},{9,11},{10,... | collective-permute-start | bytes 196616 | tf_op jit(solution)/shard_map/ppermute | solution.py:131
  2.1 6.6 %collective-permute-start.1 = (bf16[64,512]{1,0:T(8,128)(2,1)S(1)}, bf16[64,512]{1,0:T(8,128)(2,1)S(1)}, u32[]{:S(2)}, u32[]{:S(2)}) collective-permute-start(bf16[64,512]{1,0:T(8,128)(2,1)S(1)} %bitcast.13), channel_id=1, source_target_pairs={{0,4},{1,5},{2,6},{3,7},{4,0},{5,1},{6,2},{7,3},{8,12},{9,13},{10,... | collective-permute-start | bytes 196616 | tf_op jit(solution)/shard_map/ppermute | solution.py:131
  4.4 6.0 %collective-permute-start.2 = (bf16[64,512]{1,0:T(8,128)(2,1)S(1)}, bf16[64,512]{1,0:T(8,128)(2,1)S(1)}, u32[]{:S(2)}, u32[]{:S(2)}) collective-permute-start(bf16[64,512]{1,0:T(8,128)(2,1)S(1)} %bitcast.14), channel_id=1, source_target_pairs={{0,6},{1,7},{2,0},{3,1},{4,2},{5,3},{6,4},{7,5},{8,14},{9,15},{10,... | collective-permute-start | bytes 196616 | tf_op jit(solution)/shard_map/ppermute | solution.py:131
  5.5 8.9 %collective-permute-start.3 = (bf16[64,512]{1,0:T(8,128)(2,1)S(1)}, bf16[64,512]{1,0:T(8,128)(2,1)S(1)}, u32[]{:S(2)}, u32[]{:S(2)}) collective-permute-start(bf16[64,512]{1,0:T(8,128)(2,1)S(1)} %bitcast.15), channel_id=1, source_target_pairs={{0,1},{1,0},{2,3},{3,2},{4,5},{5,4},{6,7},{7,6},{8,9},{9,8},{10,11... | collective-permute-start | bytes 196616 | tf_op jit(solution)/shard_map/ppermute | solution.py:119
  7.0 7.4 %collective-permute-start.4 = (bf16[64,512]{1,0:T(8,128)(2,1)S(1)}, bf16[64,512]{1,0:T(8,128)(2,1)S(1)}, u32[]{:S(2)}, u32[]{:S(2)}) collective-permute-start(bf16[64,512]{1,0:T(8,128)(2,1)S(1)} %collective-permute-done.refs_1_), channel_id=1, source_target_pairs={{0,1},{1,0},{2,3},{3,2},{4,5},{5,4},{6,7},{7,6},{8,9},{9,8},{10,11... | collective-permute-start | bytes 196616 | tf_op jit(solution)/shard_map/ppermute | solution.py:119
  8.7 5.7 %collective-permute-start.5 = (bf16[64,512]{1,0:T(8,128)(2,1)S(1)}, bf16[64,512]{1,0:T(8,128)(2,1)S(1)}, u32[]{:S(2)}, u32[]{:S(2)}) collective-permute-start(bf16[64,512]{1,0:T(8,128)(2,1)S(1)} %collective-permute-done.1.refs_2_), channel_id=1, source_target_pairs={{0,1},{1,0},{2,3},{3,2},{4,5},{5,4},{6,7},{7,6},{8,9},{9,8},{10,11... | collective-permute-start | bytes 196616 | tf_op jit(solution)/shard_map/ppermute | solution.py:119
  10.4 4.1 %collective-permute-start.6 = (bf16[64,512]{1,0:T(8,128)(2,1)S(1)}, bf16[64,512]{1,0:T(8,128)(2,1)S(1)}, u32[]{:S(2)}, u32[]{:S(2)}) collective-permute-start(bf16[64,512]{1,0:T(8,128)(2,1)S(1)} %collective-permute-done.2.refs_3_), channel_id=1, source_target_pairs={{0,1},{1,0},{2,3},{3,2},{4,5},{5,4},{6,7},{7,6},{8,9},{9,8},{10,11... | collective-permute-start | bytes 196616 | tf_op jit(solution)/shard_map/ppermute | solution.py:119
  15.5 2.7 %collective-permute-start.7 = (bf16[64,512]{1,0:T(8,128)(2,1)S(1)}, bf16[64,512]{1,0:T(8,128)(2,1)S(1)}, u32[]{:S(2)}, u32[]{:S(2)}) collective-permute-start(bf16[64,512]{1,0:T(8,128)(2,1)S(1)} %late_tile_and_solve.4.trace_in), channel_id=1, source_target_pairs={{0,8},{1,9},{2,10},{3,11},{4,12},{5,13},{6,14},{7,15}} | collective-permute-start | bytes 196616 | tf_op jit(solution)/shard_map/ppermute | solution.py:136
  16.1 2.8 %collective-permute-start.8 = (bf16[64,512]{1,0:T(8,128)(2,1)S(1)}, bf16[64,512]{1,0:T(8,128)(2,1)S(1)}, u32[]{:S(2)}, u32[]{:S(2)}) collective-permute-start(bf16[64,512]{1,0:T(8,128)(2,1)S(1)} %late_tile_and_solve.4.trace_in), channel_id=1, source_target_pairs={{0,10},{1,11},{2,12},{3,13},{4,14},{5,15},{6,8},{7,9}} | collective-permute-start | bytes 196616 | tf_op jit(solution)/shard_map/ppermute | solution.py:136
  16.8 2.2 %collective-permute-start.9 = (bf16[64,512]{1,0:T(8,128)(2,1)S(1)}, bf16[64,512]{1,0:T(8,128)(2,1)S(1)}, u32[]{:S(2)}, u32[]{:S(2)}) collective-permute-start(bf16[64,512]{1,0:T(8,128)(2,1)S(1)} %late_tile_and_solve.4.trace_in), channel_id=1, source_target_pairs={{0,12},{1,13},{2,14},{3,15},{4,8},{5,9},{6,10},{7,11}} | collective-permute-start | bytes 196616 | tf_op jit(solution)/shard_map/ppermute | solution.py:136
  17.5 1.9 %collective-permute-start.10 = (bf16[64,512]{1,0:T(8,128)(2,1)S(1)}, bf16[64,512]{1,0:T(8,128)(2,1)S(1)}, u32[]{:S(2)}, u32[]{:S(2)}) collective-permute-start(bf16[64,512]{1,0:T(8,128)(2,1)S(1)} %late_tile_and_solve.4.trace_in), channel_id=1, source_target_pairs={{0,14},{1,15},{2,8},{3,9},{4,10},{5,11},{6,12},{7,13}} | collective-permute-start | bytes 196616 | tf_op jit(solution)/shard_map/ppermute | solution.py:136
  18.1 1.6 %collective-permute-start.11 = (bf16[64,512]{1,0:T(8,128)(2,1)S(1)}, bf16[64,512]{1,0:T(8,128)(2,1)S(1)}, u32[]{:S(2)}, u32[]{:S(2)}) collective-permute-start(bf16[64,512]{1,0:T(8,128)(2,1)S(1)} %collective-permute-done.7.refs_0_), channel_id=1, source_target_pairs={{0,1},{1,0},{2,3},{3,2},{4,5},{5,4},{6,7},{7,6},{8,9},{9,8},{10,11... | collective-permute-start | bytes 196616 | tf_op jit(solution)/shard_map/ppermute | solution.py:119
  20.7 2.7 %collective-permute-start.15 = (bf16[64,512]{1,0:T(8,128)(2,1)S(1)}, bf16[64,512]{1,0:T(8,128)(2,1)S(1)}, u32[]{:S(2)}, u32[]{:S(2)}) collective-permute-start(bf16[64,512]{1,0:T(8,128)(2,1)S(1)} %late_tile_and_solve.5.trace_in), channel_id=1, source_target_pairs={{8,16},{9,17},{10,18},{11,19},{12,20},{13,21},{14,22},{15,23}} | collective-permute-start | bytes 196616 | tf_op jit(solution)/shard_map/ppermute | solution.py:136
  21.3 2.3 %collective-permute-start.16 = (bf16[64,512]{1,0:T(8,128)(2,1)S(1)}, bf16[64,512]{1,0:T(8,128)(2,1)S(1)}, u32[]{:S(2)}, u32[]{:S(2)}) collective-permute-start(bf16[64,512]{1,0:T(8,128)(2,1)S(1)} %late_tile_and_solve.5.trace_in), channel_id=1, source_target_pairs={{8,18},{9,19},{10,20},{11,21},{12,22},{13,23},{14,16},{15,17}} | collective-permute-start | bytes 196616 | tf_op jit(solution)/shard_map/ppermute | solution.py:136
  22.0 1.9 %collective-permute-start.17 = (bf16[64,512]{1,0:T(8,128)(2,1)S(1)}, bf16[64,512]{1,0:T(8,128)(2,1)S(1)}, u32[]{:S(2)}, u32[]{:S(2)}) collective-permute-start(bf16[64,512]{1,0:T(8,128)(2,1)S(1)} %late_tile_and_solve.5.trace_in), channel_id=1, source_target_pairs={{8,20},{9,21},{10,22},{11,23},{12,16},{13,17},{14,18},{15,19}} | collective-permute-start | bytes 196616 | tf_op jit(solution)/shard_map/ppermute | solution.py:136
  22.7 1.4 %collective-permute-start.18 = (bf16[64,512]{1,0:T(8,128)(2,1)S(1)}, bf16[64,512]{1,0:T(8,128)(2,1)S(1)}, u32[]{:S(2)}, u32[]{:S(2)}) collective-permute-start(bf16[64,512]{1,0:T(8,128)(2,1)S(1)} %late_tile_and_solve.5.trace_in), channel_id=1, source_target_pairs={{8,22},{9,23},{10,16},{11,17},{12,18},{13,19},{14,20},{15,21}} | collective-permute-start | bytes 196616 | tf_op jit(solution)/shard_map/ppermute | solution.py:136
  25.4 22.6 %collective-permute-start.23 = (bf16[64,512]{1,0:T(8,128)(2,1)S(1)}, bf16[64,512]{1,0:T(8,128)(2,1)S(1)}, u32[]{:S(2)}, u32[]{:S(2)}) collective-permute-start(bf16[64,512]{1,0:T(8,128)(2,1)S(1)} %late_tile_and_solve.6.trace_in), channel_id=1, source_target_pairs={{16,24},{17,25},{18,26},{19,27},{20,28},{21,29},{22,30},{23,31}} | collective-permute-start | bytes 196616 | tf_op jit(solution)/shard_map/ppermute | solution.py:136
  26.6 25.5 %collective-permute-start.24 = (bf16[64,512]{1,0:T(8,128)(2,1)S(1)}, bf16[64,512]{1,0:T(8,128)(2,1)S(1)}, u32[]{:S(2)}, u32[]{:S(2)}) collective-permute-start(bf16[64,512]{1,0:T(8,128)(2,1)S(1)} %late_tile_and_solve.6.trace_in), channel_id=1, source_target_pairs={{16,26},{17,27},{18,28},{19,29},{20,30},{21,31},{22,24},{23,25}} | collective-permute-start | bytes 196616 | tf_op jit(solution)/shard_map/ppermute | solution.py:136
  27.9 25.4 %collective-permute-start.25 = (bf16[64,512]{1,0:T(8,128)(2,1)S(1)}, bf16[64,512]{1,0:T(8,128)(2,1)S(1)}, u32[]{:S(2)}, u32[]{:S(2)}) collective-permute-start(bf16[64,512]{1,0:T(8,128)(2,1)S(1)} %late_tile_and_solve.6.trace_in), channel_id=1, source_target_pairs={{16,28},{17,29},{18,30},{19,31},{20,24},{21,25},{22,26},{23,27}} | collective-permute-start | bytes 196616 | tf_op jit(solution)/shard_map/ppermute | solution.py:136
  29.2 25.1 %collective-permute-start.26 = (bf16[64,512]{1,0:T(8,128)(2,1)S(1)}, bf16[64,512]{1,0:T(8,128)(2,1)S(1)}, u32[]{:S(2)}, u32[]{:S(2)}) collective-permute-start(bf16[64,512]{1,0:T(8,128)(2,1)S(1)} %late_tile_and_solve.6.trace_in), channel_id=1, source_target_pairs={{16,30},{17,31},{18,24},{19,25},{20,26},{21,27},{22,28},{23,29}} | collective-permute-start | bytes 196616 | tf_op jit(solution)/shard_map/ppermute | solution.py:136
  48.0 6.5 %collective-permute-start.27 = (bf16[64,512]{1,0:T(8,128)(2,1)S(1)}, bf16[64,512]{1,0:T(8,128)(2,1)S(1)}, u32[]{:S(2)}, u32[]{:S(2)}) collective-permute-start(bf16[64,512]{1,0:T(8,128)(2,1)S(1)} %collective-permute-done.23.refs_0_), channel_id=1, source_target_pairs={{0,1},{1,0},{2,3},{3,2},{4,5},{5,4},{6,7},{7,6},{8,9},{9,8},{10,11... | collective-permute-start | bytes 196616 | tf_op jit(solution)/shard_map/ppermute | solution.py:119
  52.2 2.3 %collective-permute-start.28 = (bf16[64,512]{1,0:T(8,128)(2,1)S(1)}, bf16[64,512]{1,0:T(8,128)(2,1)S(1)}, u32[]{:S(2)}, u32[]{:S(2)}) collective-permute-start(bf16[64,512]{1,0:T(8,128)(2,1)S(1)} %collective-permute-done.24.refs_1_), channel_id=1, source_target_pairs={{0,1},{1,0},{2,3},{3,2},{4,5},{5,4},{6,7},{7,6},{8,9},{9,8},{10,11... | collective-permute-start | bytes 196616 | tf_op jit(solution)/shard_map/ppermute | solution.py:119
  53.3 1.9 %collective-permute-start.29 = (bf16[64,512]{1,0:T(8,128)(2,1)S(1)}, bf16[64,512]{1,0:T(8,128)(2,1)S(1)}, u32[]{:S(2)}, u32[]{:S(2)}) collective-permute-start(bf16[64,512]{1,0:T(8,128)(2,1)S(1)} %collective-permute-done.25.refs_2_), channel_id=1, source_target_pairs={{0,1},{1,0},{2,3},{3,2},{4,5},{5,4},{6,7},{7,6},{8,9},{9,8},{10,11... | collective-permute-start | bytes 196616 | tf_op jit(solution)/shard_map/ppermute | solution.py:119
  54.4 2.1 %collective-permute-start.30 = (bf16[64,512]{1,0:T(8,128)(2,1)S(1)}, bf16[64,512]{1,0:T(8,128)(2,1)S(1)}, u32[]{:S(2)}, u32[]{:S(2)}) collective-permute-start(bf16[64,512]{1,0:T(8,128)(2,1)S(1)} %collective-permute-done.26.refs_3_), channel_id=1, source_target_pairs={{0,1},{1,0},{2,3},{3,2},{4,5},{5,4},{6,7},{7,6},{8,9},{9,8},{10,11... | collective-permute-start | bytes 196616 | tf_op jit(solution)/shard_map/ppermute | solution.py:119
  (10 other events, 11.7 us)

commit v2 on v1

--- a/solution.py
+++ b/solution.py
@@ -17,6 +17,14 @@
 
 def params():
     return pltpu.CompilerParams(vmem_limit_bytes=VMEM_LIMIT)
+
+
+def step_of(order, chips):
+    return chips - 1 - order
+
+
+def order_of(step, chips):
+    return chips - 1 - step
 
 
 def place_kernel(chips, cols_ref, count_ref, greens_ref, placed_ref, sems):
@@ -28,8 +36,8 @@
     copies = []
     for slot in range(slots):
         column = cols_ref[slot]
-        hop = lax.rem(chip - column // CORES + chips, chips)
-        position = jnp.where(column % CORES == core, 0, chips) + hop
+        order = order_of(chip ^ (column // CORES), chips)
+        position = jnp.where(column % CORES == core, 0, chips) + order
         copy = pltpu.make_async_copy(greens_ref.at[slot], placed_ref.at[position], sems.at[slot])
         used = slot < count_ref[0]
         copies.append((used, copy))
@@ -60,6 +68,7 @@
         out_specs=IN_VMEM,
         scratch_shapes=[pltpu.SemaphoreType.DMA((slots,))],
         compiler_params=params(),
+        cost_estimate=pl.CostEstimate(flops=0, bytes_accessed=2 * greens.size * 2, transcendentals=0),
         name="place",
     )(cols, count, greens)
 
@@ -119,24 +128,37 @@
     return lax.ppermute(tile, "row", [(r, r ^ 1) for r in range(rows)])
 
 
+def sent(tile, source, target, step, slabs, rows, via=None):
+    pairs = [(source * rows + r, target * rows + (r ^ (step * CORES))) for r in range(rows)]
+    busy = {source, target}
+    if source != target and via is not None:
+        pairs += [(target * rows + r, via * rows + r) for r in range(rows)]
+        pairs += [(via * rows + r, source * rows + r) for r in range(rows)]
+        busy.add(via)
+    if source == target or via is not None:
+        pairs += [(s * rows + r, s * rows + (r ^ 1)) for s in range(slabs) if s not in busy for r in range(rows)]
+    return lax.ppermute(tile, ("slab", "row"), pairs)
+
+
 def direct(forcing, inflow, self_solve, greens, kept_cols, counts):
     slabs, rows = lax.axis_size("slab"), lax.axis_size("row")
     chips = rows // CORES
+    steps = [step_of(order, chips) for order in range(chips)]
     placed = place(chips, kept_cols[0, 0], counts[0], greens[0, 0])
     source = forcing[0].T
     solve = self_solve[0, 0]
-    trace = inflow.T
-    own = [trace]
-    for hop in range(1, chips):
-        own.append(lax.ppermute(trace, "row", [(r, (r + hop * CORES) % rows) for r in range(rows)]))
+    trace = jnp.zeros(source.shape, jnp.bfloat16)
+    entering = inflow.T
     for section in range(slabs):
-        if section > 0:
-            before, now = (section - 1) * rows, section * rows
+        if section == 0:
+            own = [sent(entering, 0, 0, step, slabs, rows) if step else entering for step in steps]
+            placed, source, solve, *own = lax.optimization_barrier((placed, source, solve, *own))
+        else:
+            others = [s % slabs for s in range(section + 1, section + slabs - 1)]
+            others += [None] * (chips - len(others))
             own = [
-                lax.ppermute(
-                    trace, ("slab", "row"), [(before + r, now + (r + hop * CORES) % rows) for r in range(rows)]
-                )
-                for hop in range(chips)
+                sent(trace, section - 1, section, step, slabs, rows, via)
+                for step, via in zip(steps, others)
             ]
         other = [swapped(tile, rows) for tile in own]
         total = early(section, placed, own + other[:-1])
@@ -168,7 +190,8 @@
 
 def shards(forcing, inflow, self_solve, greens, kept_cols, counts):
     rows, slots = lax.axis_size("row"), greens.shape[2]
-    if rows % CORES == 0 and rows <= 2 * slots:
+    chips = rows // CORES
+    if rows == chips * CORES and chips & (chips - 1) == 0 and rows <= 2 * slots:
         return direct(forcing, inflow, self_solve, greens, kept_cols, counts)
     return gathering(forcing, inflow, self_solve, greens, kept_cols, counts)
 

time: 58 us -> 48.9 us (0.84)
  waiting for transfers between devices: 24.4 us -> 9.97 us
  starting transfers between devices: 24.9 us -> 32.7 us
  local copies, waits for them, and re-layouts: 3.09 us -> 1.3 us
    ppermute x15, waiting for transfers between devices: 21.5 us -> 6.35 us  [sent(): return lax.ppermute(tile, ('slab', 'row'), pairs)]
    ppermute x15, starting transfers between devices: 15.1 us -> 26.4 us  [sent(): return lax.ppermute(tile, ('slab', 'row'), pairs)]
    ppermute x16, starting transfers between devices: 9.78 us -> 6.31 us  [swapped(): return lax.ppermute(tile, 'row', [(r, r ^ 1) for r in range(rows)])]
    unnamed x8 -> x9, local copies, waits for them, and re-layouts: 3.09 us -> 1.3 us
    ppermute x16, waiting for transfers between devices: 2.84 us -> 3.62 us  [swapped(): return lax.ppermute(tile, 'row', [(r, r ^ 1) for r in range(rows)])]
  transfers between devices with their start and end apart: 31 -> 31, of which waited for: 12 -> 16; matrix products, arithmetic and copies ran while one was open for 0% -> 0% of each run, Pallas kernels for 7% -> 7%
where the time goes in v2:
time: 48.9 us; the launch traced here: 48.7 us
  starting transfers between devices  32.7 us (67%)
  waiting for transfers between devices  9.97 us (20%)
  Pallas kernels  3.87 us (8%)
  local copies, waits for them, and re-layouts  1.3 us (3%)
  between operations  0.85 us (2%)
    ppermute x15, starting transfers between devices, sent(): return lax.ppermute(tile, ('slab', 'row'), pairs)  26.4 us
    ppermute x15, waiting for transfers between devices, sent(): return lax.ppermute(tile, ('slab', 'row'), pairs)  6.35 us
    ppermute x16, starting transfers between devices, swapped(): return lax.ppermute(tile, 'row', [(r, r ^ 1) for r in range(rows)])  6.31 us
    ppermute x16, waiting for transfers between devices, swapped(): return lax.ppermute(tile, 'row', [(r, r ^ 1) for r in range(rows)])  3.62 us
    pallas_call x1, Pallas kernels, place(): pl.pallas_call(functools.partial(place_kernel, chips), out_shape=pltpu.VM...  2.15 us
    unnamed x9, local copies, waits for them, and re-layouts  1.3 us
    pallas_call x4, Pallas kernels, early(): pl.pallas_call(functools.partial(early_kernel, section), out_shape=pltpu....  1.21 us
  transfers between devices with their start and end apart: 31, of which 16 were waited for; matrix products, arithmetic and copies ran while one was open for 0% of the time, Pallas kernels for 7%

profile of v2, /device:TPU:7, one launch (start us, length us, event | category | flops | bytes accessed | tf_op | source)
XLA Modules:
  0.0 48.7 jit_solution(5361208622905241378)
XLA Ops:
  0.0 0.7 %collective-permute-start = (bf16[64,512]{1,0:T(8,128)(2,1)}, bf16[64,512]{1,0:T(8,128)(2,1)S(1)}, u32[]{:S(2)}, u32[]{:S(2)}) collective-permute-start(bf16[64,512]{1,0:T(8,128)(2,1)} %bitcast.21), channel_id=1, source_target_pairs={{0,6},{1,7},{2,4},{3,5},{4,2},{5,3},{6,0},{7,1},{8,9},{9,8},{10,11... | collective-permute-start | bytes 196616 | tf_op jit(solution)/shard_map/ppermute | solution.py:140
  0.7 0.5 %collective-permute-start.2 = (bf16[64,512]{1,0:T(8,128)(2,1)}, bf16[64,512]{1,0:T(8,128)(2,1)S(1)}, u32[]{:S(2)}, u32[]{:S(2)}) collective-permute-start(bf16[64,512]{1,0:T(8,128)(2,1)} %bitcast.23), channel_id=1, source_target_pairs={{0,2},{1,3},{2,0},{3,1},{4,6},{5,7},{6,4},{7,5},{8,9},{9,8},{10,11... | collective-permute-start | bytes 196616 | tf_op jit(solution)/shard_map/ppermute | solution.py:140
  1.8 0.6 %copy-done.3 = s32[1,1,8]{2,1,0:T(1,128)S(1)} copy-done((s32[1,1,8]{2,1,0:T(1,128)S(1)}, s32[1,1,8]{2,1,0:T(1,128)}, u32[]{:S(2)}) %copy-start.3) | copy-done | bytes 56
  2.5 2.2 %place.1.placed_ref = bf16[8,512,512]{2,1,0:T(8,128)(2,1)S(1)} custom-call(s32[8]{0:T(128)S(1)} %bitcast.26, s32[1]{0:T(128)} %bitcast.11.count_ref, bf16[8,512,512]{2,1,0:T(8,128)(2,1)} %bitcast.27), custom_call_target="tpu_custom_call" | custom-call | bytes 8388608 | tf_op jit(solution)/shard_map/place/pallas_call | solution.py:64
  4.8 0.5 %collective-permute-start.4 = (bf16[64,512]{1,0:T(8,128)(2,1)S(1)}, bf16[64,512]{1,0:T(8,128)(2,1)S(1)}, u32[]{:S(2)}, u32[]{:S(2)}) collective-permute-start(bf16[64,512]{1,0:T(8,128)(2,1)S(1)} %collective-permute-done.1.refs_1_), channel_id=1, source_target_pairs={{0,1},{1,0},{2,3},{3,2},{4,5},{5,4},{6,7},{7,6},{8,9},{9,8},{10,11... | collective-permute-start | bytes 196616 | tf_op jit(solution)/shard_map/ppermute | solution.py:128
  7.2 6.4 %collective-permute-start.8 = (bf16[64,512]{1,0:T(8,128)(2,1)S(1)}, bf16[64,512]{1,0:T(8,128)(2,1)S(1)}, u32[]{:S(2)}, u32[]{:S(2)}) collective-permute-start(bf16[64,512]{1,0:T(8,128)(2,1)S(1)} %late_tile_and_solve.4.trace_in), channel_id=1, source_target_pairs={{0,12},{1,13},{2,14},{3,15},{4,8},{5,9},{6,10},{7,11},{8,24},{9,25... | collective-permute-start | bytes 196616 | tf_op jit(solution)/shard_map/ppermute | solution.py:140
  13.6 0.7 %collective-permute-start.9 = (bf16[64,512]{1,0:T(8,128)(2,1)S(1)}, bf16[64,512]{1,0:T(8,128)(2,1)S(1)}, u32[]{:S(2)}, u32[]{:S(2)}) collective-permute-start(bf16[64,512]{1,0:T(8,128)(2,1)S(1)} %late_tile_and_solve.4.trace_in), channel_id=1, source_target_pairs={{0,10},{1,11},{2,8},{3,9},{4,14},{5,15},{6,12},{7,13}} | collective-permute-start | bytes 196616 | tf_op jit(solution)/shard_map/ppermute | solution.py:140
  14.2 0.7 %collective-permute-start.10 = (bf16[64,512]{1,0:T(8,128)(2,1)S(1)}, bf16[64,512]{1,0:T(8,128)(2,1)S(1)}, u32[]{:S(2)}, u32[]{:S(2)}) collective-permute-start(bf16[64,512]{1,0:T(8,128)(2,1)S(1)} %late_tile_and_solve.4.trace_in), channel_id=1, source_target_pairs={{0,8},{1,9},{2,10},{3,11},{4,12},{5,13},{6,14},{7,15}} | collective-permute-start | bytes 196616 | tf_op jit(solution)/shard_map/ppermute | solution.py:140
  14.9 0.7 %collective-permute-start.11 = (bf16[64,512]{1,0:T(8,128)(2,1)S(1)}, bf16[64,512]{1,0:T(8,128)(2,1)S(1)}, u32[]{:S(2)}, u32[]{:S(2)}) collective-permute-start(bf16[64,512]{1,0:T(8,128)(2,1)S(1)} %collective-permute-done.7.refs_0_), channel_id=1, source_target_pairs={{0,1},{1,0},{2,3},{3,2},{4,5},{5,4},{6,7},{7,6},{8,9},{9,8},{10,11... | collective-permute-start | bytes 196616 | tf_op jit(solution)/shard_map/ppermute | solution.py:128
  17.5 7.6 %collective-permute-start.15 = (bf16[64,512]{1,0:T(8,128)(2,1)S(1)}, bf16[64,512]{1,0:T(8,128)(2,1)S(1)}, u32[]{:S(2)}, u32[]{:S(2)}) collective-permute-start(bf16[64,512]{1,0:T(8,128)(2,1)S(1)} %late_tile_and_solve.5.trace_in), channel_id=1, source_target_pairs={{8,22},{9,23},{10,20},{11,21},{12,18},{13,19},{14,16},{15,17},{16,... | collective-permute-start | bytes 196616 | tf_op jit(solution)/shard_map/ppermute | solution.py:140
  25.6 0.7 %collective-permute-start.17 = (bf16[64,512]{1,0:T(8,128)(2,1)S(1)}, bf16[64,512]{1,0:T(8,128)(2,1)S(1)}, u32[]{:S(2)}, u32[]{:S(2)}) collective-permute-start(bf16[64,512]{1,0:T(8,128)(2,1)S(1)} %late_tile_and_solve.5.trace_in), channel_id=1, source_target_pairs={{8,18},{9,19},{10,16},{11,17},{12,22},{13,23},{14,20},{15,21}} | collective-permute-start | bytes 196616 | tf_op jit(solution)/shard_map/ppermute | solution.py:140
  26.3 0.7 %collective-permute-start.18 = (bf16[64,512]{1,0:T(8,128)(2,1)S(1)}, bf16[64,512]{1,0:T(8,128)(2,1)S(1)}, u32[]{:S(2)}, u32[]{:S(2)}) collective-permute-start(bf16[64,512]{1,0:T(8,128)(2,1)S(1)} %late_tile_and_solve.5.trace_in), channel_id=1, source_target_pairs={{8,16},{9,17},{10,18},{11,19},{12,20},{13,21},{14,22},{15,23}} | collective-permute-start | bytes 196616 | tf_op jit(solution)/shard_map/ppermute | solution.py:140
  26.9 0.6 %collective-permute-start.19 = (bf16[64,512]{1,0:T(8,128)(2,1)S(1)}, bf16[64,512]{1,0:T(8,128)(2,1)S(1)}, u32[]{:S(2)}, u32[]{:S(2)}) collective-permute-start(bf16[64,512]{1,0:T(8,128)(2,1)S(1)} %collective-permute-done.15.refs_0_), channel_id=1, source_target_pairs={{0,1},{1,0},{2,3},{3,2},{4,5},{5,4},{6,7},{7,6},{8,9},{9,8},{10,11... | collective-permute-start | bytes 196616 | tf_op jit(solution)/shard_map/ppermute | solution.py:128
  27.5 0.5 %collective-permute-start.21 = (bf16[64,512]{1,0:T(8,128)(2,1)S(1)}, bf16[64,512]{1,0:T(8,128)(2,1)S(1)}, u32[]{:S(2)}, u32[]{:S(2)}) collective-permute-start(bf16[64,512]{1,0:T(8,128)(2,1)S(1)} %collective-permute-done.17.refs_2_), channel_id=1, source_target_pairs={{0,1},{1,0},{2,3},{3,2},{4,5},{5,4},{6,7},{7,6},{8,9},{9,8},{10,11... | collective-permute-start | bytes 196616 | tf_op jit(solution)/shard_map/ppermute | solution.py:128
  29.3 0.9 %collective-permute-start.23 = (bf16[64,512]{1,0:T(8,128)(2,1)S(1)}, bf16[64,512]{1,0:T(8,128)(2,1)S(1)}, u32[]{:S(2)}, u32[]{:S(2)}) collective-permute-start(bf16[64,512]{1,0:T(8,128)(2,1)S(1)} %late_tile_and_solve.6.trace_in), channel_id=1, source_target_pairs={{16,30},{17,31},{18,28},{19,29},{20,26},{21,27},{22,24},{23,25},{2... | collective-permute-start | bytes 196616 | tf_op jit(solution)/shard_map/ppermute | solution.py:140
  30.2 4.3 %collective-permute-start.24 = (bf16[64,512]{1,0:T(8,128)(2,1)S(1)}, bf16[64,512]{1,0:T(8,128)(2,1)S(1)}, u32[]{:S(2)}, u32[]{:S(2)}) collective-permute-start(bf16[64,512]{1,0:T(8,128)(2,1)S(1)} %late_tile_and_solve.6.trace_in), channel_id=1, source_target_pairs={{16,28},{17,29},{18,30},{19,31},{20,24},{21,25},{22,26},{23,27},{2... | collective-permute-start | bytes 196616 | tf_op jit(solution)/shard_map/ppermute | solution.py:140
  34.4 1.3 %collective-permute-start.25 = (bf16[64,512]{1,0:T(8,128)(2,1)S(1)}, bf16[64,512]{1,0:T(8,128)(2,1)S(1)}, u32[]{:S(2)}, u32[]{:S(2)}) collective-permute-start(bf16[64,512]{1,0:T(8,128)(2,1)S(1)} %late_tile_and_solve.6.trace_in), channel_id=1, source_target_pairs={{16,26},{17,27},{18,24},{19,25},{20,30},{21,31},{22,28},{23,29}} | collective-permute-start | bytes 196616 | tf_op jit(solution)/shard_map/ppermute | solution.py:140
  35.7 1.3 %collective-permute-start.26 = (bf16[64,512]{1,0:T(8,128)(2,1)S(1)}, bf16[64,512]{1,0:T(8,128)(2,1)S(1)}, u32[]{:S(2)}, u32[]{:S(2)}) collective-permute-start(bf16[64,512]{1,0:T(8,128)(2,1)S(1)} %late_tile_and_solve.6.trace_in), channel_id=1, source_target_pairs={{16,24},{17,25},{18,26},{19,27},{20,28},{21,29},{22,30},{23,31}} | collective-permute-start | bytes 196616 | tf_op jit(solution)/shard_map/ppermute | solution.py:140
  37.0 3.7 %collective-permute-done.23.refs_0_ = bf16[64,512]{1,0:T(8,128)(2,1)S(1)} collective-permute-done((bf16[64,512]{1,0:T(8,128)(2,1)S(1)}, bf16[64,512]{1,0:T(8,128)(2,1)S(1)}, u32[]{:S(2)}, u32[]{:S(2)}) %collective-permute-start.23) | collective-permute-done | bytes 65568 | tf_op jit(solution)/shard_map/ppermute | solution.py:140
  40.7 1.2 %collective-permute-start.27 = (bf16[64,512]{1,0:T(8,128)(2,1)S(1)}, bf16[64,512]{1,0:T(8,128)(2,1)S(1)}, u32[]{:S(2)}, u32[]{:S(2)}) collective-permute-start(bf16[64,512]{1,0:T(8,128)(2,1)S(1)} %collective-permute-done.23.refs_0_), channel_id=1, source_target_pairs={{0,1},{1,0},{2,3},{3,2},{4,5},{5,4},{6,7},{7,6},{8,9},{9,8},{10,11... | collective-permute-start | bytes 196616 | tf_op jit(solution)/shard_map/ppermute | solution.py:128
  41.9 2.5 %collective-permute-done.24.refs_1_ = bf16[64,512]{1,0:T(8,128)(2,1)S(1)} collective-permute-done((bf16[64,512]{1,0:T(8,128)(2,1)S(1)}, bf16[64,512]{1,0:T(8,128)(2,1)S(1)}, u32[]{:S(2)}, u32[]{:S(2)}) %collective-permute-start.24) | collective-permute-done | bytes 65568 | tf_op jit(solution)/shard_map/ppermute | solution.py:140
  44.4 0.8 %collective-permute-start.28 = (bf16[64,512]{1,0:T(8,128)(2,1)S(1)}, bf16[64,512]{1,0:T(8,128)(2,1)S(1)}, u32[]{:S(2)}, u32[]{:S(2)}) collective-permute-start(bf16[64,512]{1,0:T(8,128)(2,1)S(1)} %collective-permute-done.24.refs_1_), channel_id=1, source_target_pairs={{0,1},{1,0},{2,3},{3,2},{4,5},{5,4},{6,7},{7,6},{8,9},{9,8},{10,11... | collective-permute-start | bytes 196616 | tf_op jit(solution)/shard_map/ppermute | solution.py:128
  46.4 1.2 %early_tiles.7.total_ref = f32[64,512]{1,0:T(8,128)S(1)} custom-call(bf16[8,512,512]{2,1,0:T(8,128)(2,1)S(1)} %place.1.placed_ref, bf16[64,512]{1,0:T(8,128)(2,1)S(1)} %collective-permute-done.23.refs_0_, bf16[64,512]{1,0:T(8,128)(2,1)S(1)} %collective-permute-done.24.refs_1_, bf16[64,512]{1,0:T(8,128)(2,1)S(1)} %collective-permute-done.25.refs_2_, ...), custom_call_target="tpu_custom_call" | custom-call | tf_op jit(solution)/shard_map/early_tiles/pallas_call | solution.py:95
  48.1 0.6 %copy.15 = bf16[1,512,64]{1,2,0:T(8,128)(2,1)} copy(bf16[1,512,64]{1,2,0:T(8,128)(2,1)S(1)} %bitcast.12) | data formatting | bytes 131072
  (57 shorter events, 7.3 us)
Async XLA Ops:
  0.0 4.7 %collective-permute-start = (bf16[64,512]{1,0:T(8,128)(2,1)}, bf16[64,512]{1,0:T(8,128)(2,1)S(1)}, u32[]{:S(2)}, u32[]{:S(2)}) collective-permute-start(bf16[64,512]{1,0:T(8,128)(2,1)} %bitcast.21), channel_id=1, source_target_pairs={{0,6},{1,7},{2,4},{3,5},{4,2},{5,3},{6,0},{7,1},{8,9},{9,8},{10,11... | collective-permute-start | bytes 196616 | tf_op jit(solution)/shard_map/ppermute | solution.py:140
  0.7 4.0 %collective-permute-start.1 = (bf16[64,512]{1,0:T(8,128)(2,1)}, bf16[64,512]{1,0:T(8,128)(2,1)S(1)}, u32[]{:S(2)}, u32[]{:S(2)}) collective-permute-start(bf16[64,512]{1,0:T(8,128)(2,1)} %bitcast.22), channel_id=1, source_target_pairs={{0,4},{1,5},{2,6},{3,7},{4,0},{5,1},{6,2},{7,3},{8,9},{9,8},{10,11... | collective-permute-start | bytes 196616 | tf_op jit(solution)/shard_map/ppermute | solution.py:140
  0.7 4.0 %collective-permute-start.2 = (bf16[64,512]{1,0:T(8,128)(2,1)}, bf16[64,512]{1,0:T(8,128)(2,1)S(1)}, u32[]{:S(2)}, u32[]{:S(2)}) collective-permute-start(bf16[64,512]{1,0:T(8,128)(2,1)} %bitcast.23), channel_id=1, source_target_pairs={{0,2},{1,3},{2,0},{3,1},{4,6},{5,7},{6,4},{7,5},{8,9},{9,8},{10,11... | collective-permute-start | bytes 196616 | tf_op jit(solution)/shard_map/ppermute | solution.py:140
  4.8 1.4 %collective-permute-start.4 = (bf16[64,512]{1,0:T(8,128)(2,1)S(1)}, bf16[64,512]{1,0:T(8,128)(2,1)S(1)}, u32[]{:S(2)}, u32[]{:S(2)}) collective-permute-start(bf16[64,512]{1,0:T(8,128)(2,1)S(1)} %collective-permute-done.1.refs_1_), channel_id=1, source_target_pairs={{0,1},{1,0},{2,3},{3,2},{4,5},{5,4},{6,7},{7,6},{8,9},{9,8},{10,11... | collective-permute-start | bytes 196616 | tf_op jit(solution)/shard_map/ppermute | solution.py:128
  6.8 8.2 %collective-permute-start.7 = (bf16[64,512]{1,0:T(8,128)(2,1)S(1)}, bf16[64,512]{1,0:T(8,128)(2,1)S(1)}, u32[]{:S(2)}, u32[]{:S(2)}) collective-permute-start(bf16[64,512]{1,0:T(8,128)(2,1)S(1)} %late_tile_and_solve.4.trace_in), channel_id=1, source_target_pairs={{0,14},{1,15},{2,12},{3,13},{4,10},{5,11},{6,8},{7,9},{8,16},{9,17... | collective-permute-start | bytes 196616 | tf_op jit(solution)/shard_map/ppermute | solution.py:140
  7.2 8.5 %collective-permute-start.8 = (bf16[64,512]{1,0:T(8,128)(2,1)S(1)}, bf16[64,512]{1,0:T(8,128)(2,1)S(1)}, u32[]{:S(2)}, u32[]{:S(2)}) collective-permute-start(bf16[64,512]{1,0:T(8,128)(2,1)S(1)} %late_tile_and_solve.4.trace_in), channel_id=1, source_target_pairs={{0,12},{1,13},{2,14},{3,15},{4,8},{5,9},{6,10},{7,11},{8,24},{9,25... | collective-permute-start | bytes 196616 | tf_op jit(solution)/shard_map/ppermute | solution.py:140
  13.6 2.5 %collective-permute-start.9 = (bf16[64,512]{1,0:T(8,128)(2,1)S(1)}, bf16[64,512]{1,0:T(8,128)(2,1)S(1)}, u32[]{:S(2)}, u32[]{:S(2)}) collective-permute-start(bf16[64,512]{1,0:T(8,128)(2,1)S(1)} %late_tile_and_solve.4.trace_in), channel_id=1, source_target_pairs={{0,10},{1,11},{2,8},{3,9},{4,14},{5,15},{6,12},{7,13}} | collective-permute-start | bytes 196616 | tf_op jit(solution)/shard_map/ppermute | solution.py:140
  14.2 1.9 %collective-permute-start.10 = (bf16[64,512]{1,0:T(8,128)(2,1)S(1)}, bf16[64,512]{1,0:T(8,128)(2,1)S(1)}, u32[]{:S(2)}, u32[]{:S(2)}) collective-permute-start(bf16[64,512]{1,0:T(8,128)(2,1)S(1)} %late_tile_and_solve.4.trace_in), channel_id=1, source_target_pairs={{0,8},{1,9},{2,10},{3,11},{4,12},{5,13},{6,14},{7,15}} | collective-permute-start | bytes 196616 | tf_op jit(solution)/shard_map/ppermute | solution.py:140
  14.9 1.7 %collective-permute-start.11 = (bf16[64,512]{1,0:T(8,128)(2,1)S(1)}, bf16[64,512]{1,0:T(8,128)(2,1)S(1)}, u32[]{:S(2)}, u32[]{:S(2)}) collective-permute-start(bf16[64,512]{1,0:T(8,128)(2,1)S(1)} %collective-permute-done.7.refs_0_), channel_id=1, source_target_pairs={{0,1},{1,0},{2,3},{3,2},{4,5},{5,4},{6,7},{7,6},{8,9},{9,8},{10,11... | collective-permute-start | bytes 196616 | tf_op jit(solution)/shard_map/ppermute | solution.py:128
  15.6 1.4 %collective-permute-start.12 = (bf16[64,512]{1,0:T(8,128)(2,1)S(1)}, bf16[64,512]{1,0:T(8,128)(2,1)S(1)}, u32[]{:S(2)}, u32[]{:S(2)}) collective-permute-start(bf16[64,512]{1,0:T(8,128)(2,1)S(1)} %collective-permute-done.8.refs_1_), channel_id=1, source_target_pairs={{0,1},{1,0},{2,3},{3,2},{4,5},{5,4},{6,7},{7,6},{8,9},{9,8},{10,11... | collective-permute-start | bytes 196616 | tf_op jit(solution)/shard_map/ppermute | solution.py:128
  16.1 1.4 %collective-permute-start.14 = (bf16[64,512]{1,0:T(8,128)(2,1)S(1)}, bf16[64,512]{1,0:T(8,128)(2,1)S(1)}, u32[]{:S(2)}, u32[]{:S(2)}) collective-permute-start(bf16[64,512]{1,0:T(8,128)(2,1)S(1)} %collective-permute-done.10.refs_3_), channel_id=1, source_target_pairs={{0,1},{1,0},{2,3},{3,2},{4,5},{5,4},{6,7},{7,6},{8,9},{9,8},{10,11... | collective-permute-start | bytes 196616 | tf_op jit(solution)/shard_map/ppermute | solution.py:128
  17.5 9.4 %collective-permute-start.15 = (bf16[64,512]{1,0:T(8,128)(2,1)S(1)}, bf16[64,512]{1,0:T(8,128)(2,1)S(1)}, u32[]{:S(2)}, u32[]{:S(2)}) collective-permute-start(bf16[64,512]{1,0:T(8,128)(2,1)S(1)} %late_tile_and_solve.5.trace_in), channel_id=1, source_target_pairs={{8,22},{9,23},{10,20},{11,21},{12,18},{13,19},{14,16},{15,17},{16,... | collective-permute-start | bytes 196616 | tf_op jit(solution)/shard_map/ppermute | solution.py:140
  25.2 2.3 %collective-permute-start.16 = (bf16[64,512]{1,0:T(8,128)(2,1)S(1)}, bf16[64,512]{1,0:T(8,128)(2,1)S(1)}, u32[]{:S(2)}, u32[]{:S(2)}) collective-permute-start(bf16[64,512]{1,0:T(8,128)(2,1)S(1)} %late_tile_and_solve.5.trace_in), channel_id=1, source_target_pairs={{8,20},{9,21},{10,22},{11,23},{12,16},{13,17},{14,18},{15,19},{16,... | collective-permute-start | bytes 196616 | tf_op jit(solution)/shard_map/ppermute | solution.py:140
  25.6 1.9 %collective-permute-start.17 = (bf16[64,512]{1,0:T(8,128)(2,1)S(1)}, bf16[64,512]{1,0:T(8,128)(2,1)S(1)}, u32[]{:S(2)}, u32[]{:S(2)}) collective-permute-start(bf16[64,512]{1,0:T(8,128)(2,1)S(1)} %late_tile_and_solve.5.trace_in), channel_id=1, source_target_pairs={{8,18},{9,19},{10,16},{11,17},{12,22},{13,23},{14,20},{15,21}} | collective-permute-start | bytes 196616 | tf_op jit(solution)/shard_map/ppermute | solution.py:140
  26.3 1.8 %collective-permute-start.18 = (bf16[64,512]{1,0:T(8,128)(2,1)S(1)}, bf16[64,512]{1,0:T(8,128)(2,1)S(1)}, u32[]{:S(2)}, u32[]{:S(2)}) collective-permute-start(bf16[64,512]{1,0:T(8,128)(2,1)S(1)} %late_tile_and_solve.5.trace_in), channel_id=1, source_target_pairs={{8,16},{9,17},{10,18},{11,19},{12,20},{13,21},{14,22},{15,23}} | collective-permute-start | bytes 196616 | tf_op jit(solution)/shard_map/ppermute | solution.py:140
  26.9 1.5 %collective-permute-start.19 = (bf16[64,512]{1,0:T(8,128)(2,1)S(1)}, bf16[64,512]{1,0:T(8,128)(2,1)S(1)}, u32[]{:S(2)}, u32[]{:S(2)}) collective-permute-start(bf16[64,512]{1,0:T(8,128)(2,1)S(1)} %collective-permute-done.15.refs_0_), channel_id=1, source_target_pairs={{0,1},{1,0},{2,3},{3,2},{4,5},{5,4},{6,7},{7,6},{8,9},{9,8},{10,11... | collective-permute-start | bytes 196616 | tf_op jit(solution)/shard_map/ppermute | solution.py:128
  27.5 1.4 %collective-permute-start.21 = (bf16[64,512]{1,0:T(8,128)(2,1)S(1)}, bf16[64,512]{1,0:T(8,128)(2,1)S(1)}, u32[]{:S(2)}, u32[]{:S(2)}) collective-permute-start(bf16[64,512]{1,0:T(8,128)(2,1)S(1)} %collective-permute-done.17.refs_2_), channel_id=1, source_target_pairs={{0,1},{1,0},{2,3},{3,2},{4,5},{5,4},{6,7},{7,6},{8,9},{9,8},{10,11... | collective-permute-start | bytes 196616 | tf_op jit(solution)/shard_map/ppermute | solution.py:128
  29.3 11.4 %collective-permute-start.23 = (bf16[64,512]{1,0:T(8,128)(2,1)S(1)}, bf16[64,512]{1,0:T(8,128)(2,1)S(1)}, u32[]{:S(2)}, u32[]{:S(2)}) collective-permute-start(bf16[64,512]{1,0:T(8,128)(2,1)S(1)} %late_tile_and_solve.6.trace_in), channel_id=1, source_target_pairs={{16,30},{17,31},{18,28},{19,29},{20,26},{21,27},{22,24},{23,25},{2... | collective-permute-start | bytes 196616 | tf_op jit(solution)/shard_map/ppermute | solution.py:140
  30.2 14.2 %collective-permute-start.24 = (bf16[64,512]{1,0:T(8,128)(2,1)S(1)}, bf16[64,512]{1,0:T(8,128)(2,1)S(1)}, u32[]{:S(2)}, u32[]{:S(2)}) collective-permute-start(bf16[64,512]{1,0:T(8,128)(2,1)S(1)} %late_tile_and_solve.6.trace_in), channel_id=1, source_target_pairs={{16,28},{17,29},{18,30},{19,31},{20,24},{21,25},{22,26},{23,27},{2... | collective-permute-start | bytes 196616 | tf_op jit(solution)/shard_map/ppermute | solution.py:140
  34.4 10.7 %collective-permute-start.25 = (bf16[64,512]{1,0:T(8,128)(2,1)S(1)}, bf16[64,512]{1,0:T(8,128)(2,1)S(1)}, u32[]{:S(2)}, u32[]{:S(2)}) collective-permute-start(bf16[64,512]{1,0:T(8,128)(2,1)S(1)} %late_tile_and_solve.6.trace_in), channel_id=1, source_target_pairs={{16,26},{17,27},{18,24},{19,25},{20,30},{21,31},{22,28},{23,29}} | collective-permute-start | bytes 196616 | tf_op jit(solution)/shard_map/ppermute | solution.py:140
  35.7 9.6 %collective-permute-start.26 = (bf16[64,512]{1,0:T(8,128)(2,1)S(1)}, bf16[64,512]{1,0:T(8,128)(2,1)S(1)}, u32[]{:S(2)}, u32[]{:S(2)}) collective-permute-start(bf16[64,512]{1,0:T(8,128)(2,1)S(1)} %late_tile_and_solve.6.trace_in), channel_id=1, source_target_pairs={{16,24},{17,25},{18,26},{19,27},{20,28},{21,29},{22,30},{23,31}} | collective-permute-start | bytes 196616 | tf_op jit(solution)/shard_map/ppermute | solution.py:140
  40.7 5.0 %collective-permute-start.27 = (bf16[64,512]{1,0:T(8,128)(2,1)S(1)}, bf16[64,512]{1,0:T(8,128)(2,1)S(1)}, u32[]{:S(2)}, u32[]{:S(2)}) collective-permute-start(bf16[64,512]{1,0:T(8,128)(2,1)S(1)} %collective-permute-done.23.refs_0_), channel_id=1, source_target_pairs={{0,1},{1,0},{2,3},{3,2},{4,5},{5,4},{6,7},{7,6},{8,9},{9,8},{10,11... | collective-permute-start | bytes 196616 | tf_op jit(solution)/shard_map/ppermute | solution.py:128
  44.4 1.7 %collective-permute-start.28 = (bf16[64,512]{1,0:T(8,128)(2,1)S(1)}, bf16[64,512]{1,0:T(8,128)(2,1)S(1)}, u32[]{:S(2)}, u32[]{:S(2)}) collective-permute-start(bf16[64,512]{1,0:T(8,128)(2,1)S(1)} %collective-permute-done.24.refs_1_), channel_id=1, source_target_pairs={{0,1},{1,0},{2,3},{3,2},{4,5},{5,4},{6,7},{7,6},{8,9},{9,8},{10,11... | collective-permute-start | bytes 196616 | tf_op jit(solution)/shard_map/ppermute | solution.py:128
  45.3 2.3 %collective-permute-start.30 = (bf16[64,512]{1,0:T(8,128)(2,1)S(1)}, bf16[64,512]{1,0:T(8,128)(2,1)S(1)}, u32[]{:S(2)}, u32[]{:S(2)}) collective-permute-start(bf16[64,512]{1,0:T(8,128)(2,1)S(1)} %collective-permute-done.26.refs_3_), channel_id=1, source_target_pairs={{0,1},{1,0},{2,3},{3,2},{4,5},{5,4},{6,7},{7,6},{8,9},{9,8},{10,11... | collective-permute-start | bytes 196616 | tf_op jit(solution)/shard_map/ppermute | solution.py:128
  (11 other events, 16.6 us)

commit v3 on v2

--- a/solution.py
+++ b/solution.py
@@ -20,11 +20,13 @@
 
 
 def step_of(order, chips):
-    return chips - 1 - order
+    half = chips // 2
+    return half + order // 2 if order % 2 == 0 else half - 1 - order // 2
 
 
 def order_of(step, chips):
-    return chips - 1 - step
+    half = chips // 2
+    return jnp.where(step >= half, 2 * (step - half), 2 * (half - 1 - step) + 1)
 
 
 def place_kernel(chips, cols_ref, count_ref, greens_ref, placed_ref, sems):
@@ -132,12 +134,19 @@
     pairs = [(source * rows + r, target * rows + (r ^ (step * CORES))) for r in range(rows)]
     busy = {source, target}
     if source != target and via is not None:
-        pairs += [(target * rows + r, via * rows + r) for r in range(rows)]
+        pairs += [(target * rows + r, via * rows + (r if via != source else r ^ (step * CORES))) for r in range(rows)]
+    if via not in (None, source):
         pairs += [(via * rows + r, source * rows + r) for r in range(rows)]
+    if via is not None:
         busy.add(via)
-    if source == target or via is not None:
         pairs += [(s * rows + r, s * rows + (r ^ 1)) for s in range(slabs) if s not in busy for r in range(rows)]
     return lax.ppermute(tile, ("slab", "row"), pairs)
+
+
+def third_slabs(section, slabs, chips):
+    free = [s % slabs for s in range(section + 1, section + slabs - 1)]
+    free = [s for s in free if s != section - 2][: chips - 1]
+    return free + [None] * (chips - 1 - len(free)) + [section - 1]
 
 
 def direct(forcing, inflow, self_solve, greens, kept_cols, counts):
@@ -151,15 +160,11 @@
     entering = inflow.T
     for section in range(slabs):
         if section == 0:
-            own = [sent(entering, 0, 0, step, slabs, rows) if step else entering for step in steps]
+            own = [sent(entering, 0, 0, step, slabs, rows, 0) if step else entering for step in steps]
             placed, source, solve, *own = lax.optimization_barrier((placed, source, solve, *own))
         else:
-            others = [s % slabs for s in range(section + 1, section + slabs - 1)]
-            others += [None] * (chips - len(others))
-            own = [
-                sent(trace, section - 1, section, step, slabs, rows, via)
-                for step, via in zip(steps, others)
-            ]
+            vias = third_slabs(section, slabs, chips)
+            own = [sent(trace, section - 1, section, step, slabs, rows, via) for step, via in zip(steps, vias)]
         other = [swapped(tile, rows) for tile in own]
         total = early(section, placed, own + other[:-1])
         trace = late(section, placed, total, other[-1], source, solve, trace)
@@ -191,7 +196,7 @@
 def shards(forcing, inflow, self_solve, greens, kept_cols, counts):
     rows, slots = lax.axis_size("row"), greens.shape[2]
     chips = rows // CORES
-    if rows == chips * CORES and chips & (chips - 1) == 0 and rows <= 2 * slots:
+    if rows == chips * CORES and chips & (chips - 1) == 0 and 1 < chips and rows <= 2 * slots:
         return direct(forcing, inflow, self_solve, greens, kept_cols, counts)
     return gathering(forcing, inflow, self_solve, greens, kept_cols, counts)
 

time: 48.9 us -> 47.5 us (0.971)
  waiting for transfers between devices: 9.97 us -> 7.33 us
  starting transfers between devices: 32.7 us -> 34.1 us
    ppermute x15, waiting for transfers between devices: 6.35 us -> 4.22 us  [sent(): return lax.ppermute(tile, ('slab', 'row'), pairs)]
    ppermute x15, starting transfers between devices: 26.4 us -> 27.7 us  [sent(): return lax.ppermute(tile, ('slab', 'row'), pairs)]
    ppermute x16, waiting for transfers between devices: 3.62 us -> 3.11 us  [swapped(): return lax.ppermute(tile, 'row', [(r, r ^ 1) for r in range(rows)])]
  transfers between devices with their start and end apart: 31 -> 31, of which waited for: 16 -> 14; matrix products, arithmetic and copies ran while one was open for 0% -> 0% of each run, Pallas kernels for 7% -> 7%
where the time goes in v3:
time: 47.5 us; the launch traced here: 47.3 us
  starting transfers between devices  34.1 us (72%)
  waiting for transfers between devices  7.33 us (15%)
  Pallas kernels  3.73 us (8%)
  local copies, waits for them, and re-layouts  1.31 us (3%)
  between operations  0.82 us (2%)
    ppermute x15, starting transfers between devices, sent(): return lax.ppermute(tile, ('slab', 'row'), pairs)  27.7 us
    ppermute x16, starting transfers between devices, swapped(): return lax.ppermute(tile, 'row', [(r, r ^ 1) for r in range(rows)])  6.47 us
    ppermute x15, waiting for transfers between devices, sent(): return lax.ppermute(tile, ('slab', 'row'), pairs)  4.22 us
    ppermute x16, waiting for transfers between devices, swapped(): return lax.ppermute(tile, 'row', [(r, r ^ 1) for r in range(rows)])  3.11 us
    pallas_call x1, Pallas kernels, place(): pl.pallas_call(functools.partial(place_kernel, chips), out_shape=pltpu.VM...  2 us
    unnamed x9, local copies, waits for them, and re-layouts  1.3 us
    pallas_call x4, Pallas kernels, early(): pl.pallas_call(functools.partial(early_kernel, section), out_shape=pltpu....  1.23 us
  transfers between devices with their start and end apart: 31, of which 14 were waited for; matrix products, arithmetic and copies ran while one was open for 0% of the time, Pallas kernels for 7%

profile of v3, /device:TPU:7, one launch (start us, length us, event | category | flops | bytes accessed | tf_op | source)
XLA Modules:
  0.0 47.3 jit_solution(1483217007401299519)
XLA Ops:
  0.0 0.7 %collective-permute-start = (bf16[64,512]{1,0:T(8,128)(2,1)}, bf16[64,512]{1,0:T(8,128)(2,1)S(1)}, u32[]{:S(2)}, u32[]{:S(2)}) collective-permute-start(bf16[64,512]{1,0:T(8,128)(2,1)} %bitcast.21), channel_id=1, source_target_pairs={{0,4},{1,5},{2,6},{3,7},{4,0},{5,1},{6,2},{7,3},{8,9},{9,8},{10,11... | collective-permute-start | bytes 196616 | tf_op jit(solution)/shard_map/ppermute | solution.py:143
  0.7 0.5 %collective-permute-start.2 = (bf16[64,512]{1,0:T(8,128)(2,1)}, bf16[64,512]{1,0:T(8,128)(2,1)S(1)}, u32[]{:S(2)}, u32[]{:S(2)}) collective-permute-start(bf16[64,512]{1,0:T(8,128)(2,1)} %bitcast.23), channel_id=1, source_target_pairs={{0,6},{1,7},{2,4},{3,5},{4,2},{5,3},{6,0},{7,1},{8,9},{9,8},{10,11... | collective-permute-start | bytes 196616 | tf_op jit(solution)/shard_map/ppermute | solution.py:143
  1.8 0.6 %copy-done.3 = s32[1,1,8]{2,1,0:T(1,128)S(1)} copy-done((s32[1,1,8]{2,1,0:T(1,128)S(1)}, s32[1,1,8]{2,1,0:T(1,128)}, u32[]{:S(2)}) %copy-start.3) | copy-done | bytes 56
  2.5 2.0 %place.1.placed_ref = bf16[8,512,512]{2,1,0:T(8,128)(2,1)S(1)} custom-call(s32[8]{0:T(128)S(1)} %bitcast.26, s32[1]{0:T(128)} %bitcast.11.count_ref, bf16[8,512,512]{2,1,0:T(8,128)(2,1)} %bitcast.27), custom_call_target="tpu_custom_call" | custom-call | bytes 8388608 | tf_op jit(solution)/shard_map/place/pallas_call | solution.py:66
  4.6 0.9 %collective-permute-start.3 = (bf16[64,512]{1,0:T(8,128)(2,1)S(1)}, bf16[64,512]{1,0:T(8,128)(2,1)S(1)}, u32[]{:S(2)}, u32[]{:S(2)}) collective-permute-start(bf16[64,512]{1,0:T(8,128)(2,1)S(1)} %collective-permute-done.refs_0_), channel_id=1, source_target_pairs={{0,1},{1,0},{2,3},{3,2},{4,5},{5,4},{6,7},{7,6},{8,9},{9,8},{10,11... | collective-permute-start | bytes 196616 | tf_op jit(solution)/shard_map/ppermute | solution.py:130
  7.5 7.1 %collective-permute-start.8 = (bf16[64,512]{1,0:T(8,128)(2,1)S(1)}, bf16[64,512]{1,0:T(8,128)(2,1)S(1)}, u32[]{:S(2)}, u32[]{:S(2)}) collective-permute-start(bf16[64,512]{1,0:T(8,128)(2,1)S(1)} %late_tile_and_solve.4.trace_in), channel_id=1, source_target_pairs={{0,10},{1,11},{2,8},{3,9},{4,14},{5,15},{6,12},{7,13},{8,24},{9,25... | collective-permute-start | bytes 196616 | tf_op jit(solution)/shard_map/ppermute | solution.py:143
  14.6 0.7 %collective-permute-start.9 = (bf16[64,512]{1,0:T(8,128)(2,1)S(1)}, bf16[64,512]{1,0:T(8,128)(2,1)S(1)}, u32[]{:S(2)}, u32[]{:S(2)}) collective-permute-start(bf16[64,512]{1,0:T(8,128)(2,1)S(1)} %late_tile_and_solve.4.trace_in), channel_id=1, source_target_pairs={{0,14},{1,15},{2,12},{3,13},{4,10},{5,11},{6,8},{7,9}} | collective-permute-start | bytes 196616 | tf_op jit(solution)/shard_map/ppermute | solution.py:143
  15.3 0.7 %collective-permute-start.10 = (bf16[64,512]{1,0:T(8,128)(2,1)S(1)}, bf16[64,512]{1,0:T(8,128)(2,1)S(1)}, u32[]{:S(2)}, u32[]{:S(2)}) collective-permute-start(bf16[64,512]{1,0:T(8,128)(2,1)S(1)} %late_tile_and_solve.4.trace_in), channel_id=1, source_target_pairs={{0,8},{1,9},{2,10},{3,11},{4,12},{5,13},{6,14},{7,15},{8,0},{9,1},... | collective-permute-start | bytes 196616 | tf_op jit(solution)/shard_map/ppermute | solution.py:143
  16.1 1.1 %collective-permute-start.12 = (bf16[64,512]{1,0:T(8,128)(2,1)S(1)}, bf16[64,512]{1,0:T(8,128)(2,1)S(1)}, u32[]{:S(2)}, u32[]{:S(2)}) collective-permute-start(bf16[64,512]{1,0:T(8,128)(2,1)S(1)} %collective-permute-done.8.refs_1_), channel_id=1, source_target_pairs={{0,1},{1,0},{2,3},{3,2},{4,5},{5,4},{6,7},{7,6},{8,9},{9,8},{10,11... | collective-permute-start | bytes 196616 | tf_op jit(solution)/shard_map/ppermute | solution.py:130
  17.1 0.5 %collective-permute-start.14 = (bf16[64,512]{1,0:T(8,128)(2,1)S(1)}, bf16[64,512]{1,0:T(8,128)(2,1)S(1)}, u32[]{:S(2)}, u32[]{:S(2)}) collective-permute-start(bf16[64,512]{1,0:T(8,128)(2,1)S(1)} %collective-permute-done.10.refs_3_), channel_id=1, source_target_pairs={{0,1},{1,0},{2,3},{3,2},{4,5},{5,4},{6,7},{7,6},{8,9},{9,8},{10,11... | collective-permute-start | bytes 196616 | tf_op jit(solution)/shard_map/ppermute | solution.py:130
  18.6 6.1 %collective-permute-start.15 = (bf16[64,512]{1,0:T(8,128)(2,1)S(1)}, bf16[64,512]{1,0:T(8,128)(2,1)S(1)}, u32[]{:S(2)}, u32[]{:S(2)}) collective-permute-start(bf16[64,512]{1,0:T(8,128)(2,1)S(1)} %late_tile_and_solve.5.trace_in), channel_id=1, source_target_pairs={{8,20},{9,21},{10,22},{11,23},{12,16},{13,17},{14,18},{15,19},{16,... | collective-permute-start | bytes 196616 | tf_op jit(solution)/shard_map/ppermute | solution.py:143
  24.7 0.7 %collective-permute-start.16 = (bf16[64,512]{1,0:T(8,128)(2,1)S(1)}, bf16[64,512]{1,0:T(8,128)(2,1)S(1)}, u32[]{:S(2)}, u32[]{:S(2)}) collective-permute-start(bf16[64,512]{1,0:T(8,128)(2,1)S(1)} %late_tile_and_solve.5.trace_in), channel_id=1, source_target_pairs={{8,18},{9,19},{10,16},{11,17},{12,22},{13,23},{14,20},{15,21}} | collective-permute-start | bytes 196616 | tf_op jit(solution)/shard_map/ppermute | solution.py:143
  25.4 0.7 %collective-permute-start.17 = (bf16[64,512]{1,0:T(8,128)(2,1)S(1)}, bf16[64,512]{1,0:T(8,128)(2,1)S(1)}, u32[]{:S(2)}, u32[]{:S(2)}) collective-permute-start(bf16[64,512]{1,0:T(8,128)(2,1)S(1)} %late_tile_and_solve.5.trace_in), channel_id=1, source_target_pairs={{8,22},{9,23},{10,20},{11,21},{12,18},{13,19},{14,16},{15,17}} | collective-permute-start | bytes 196616 | tf_op jit(solution)/shard_map/ppermute | solution.py:143
  26.0 0.7 %collective-permute-start.18 = (bf16[64,512]{1,0:T(8,128)(2,1)S(1)}, bf16[64,512]{1,0:T(8,128)(2,1)S(1)}, u32[]{:S(2)}, u32[]{:S(2)}) collective-permute-start(bf16[64,512]{1,0:T(8,128)(2,1)S(1)} %late_tile_and_solve.5.trace_in), channel_id=1, source_target_pairs={{8,16},{9,17},{10,18},{11,19},{12,20},{13,21},{14,22},{15,23},{16,... | collective-permute-start | bytes 196616 | tf_op jit(solution)/shard_map/ppermute | solution.py:143
  26.7 0.5 %collective-permute-start.19 = (bf16[64,512]{1,0:T(8,128)(2,1)S(1)}, bf16[64,512]{1,0:T(8,128)(2,1)S(1)}, u32[]{:S(2)}, u32[]{:S(2)}) collective-permute-start(bf16[64,512]{1,0:T(8,128)(2,1)S(1)} %collective-permute-done.15.refs_0_), channel_id=1, source_target_pairs={{0,1},{1,0},{2,3},{3,2},{4,5},{5,4},{6,7},{7,6},{8,9},{9,8},{10,11... | collective-permute-start | bytes 196616 | tf_op jit(solution)/shard_map/ppermute | solution.py:130
  29.0 1.3 %collective-permute-start.24 = (bf16[64,512]{1,0:T(8,128)(2,1)S(1)}, bf16[64,512]{1,0:T(8,128)(2,1)S(1)}, u32[]{:S(2)}, u32[]{:S(2)}) collective-permute-start(bf16[64,512]{1,0:T(8,128)(2,1)S(1)} %late_tile_and_solve.6.trace_in), channel_id=1, source_target_pairs={{16,26},{17,27},{18,24},{19,25},{20,30},{21,31},{22,28},{23,29}} | collective-permute-start | bytes 196616 | tf_op jit(solution)/shard_map/ppermute | solution.py:143
  30.3 1.3 %collective-permute-start.25 = (bf16[64,512]{1,0:T(8,128)(2,1)S(1)}, bf16[64,512]{1,0:T(8,128)(2,1)S(1)}, u32[]{:S(2)}, u32[]{:S(2)}) collective-permute-start(bf16[64,512]{1,0:T(8,128)(2,1)S(1)} %late_tile_and_solve.6.trace_in), channel_id=1, source_target_pairs={{16,30},{17,31},{18,28},{19,29},{20,26},{21,27},{22,24},{23,25}} | collective-permute-start | bytes 196616 | tf_op jit(solution)/shard_map/ppermute | solution.py:143
  31.6 7.0 %collective-permute-start.26 = (bf16[64,512]{1,0:T(8,128)(2,1)S(1)}, bf16[64,512]{1,0:T(8,128)(2,1)S(1)}, u32[]{:S(2)}, u32[]{:S(2)}) collective-permute-start(bf16[64,512]{1,0:T(8,128)(2,1)S(1)} %late_tile_and_solve.6.trace_in), channel_id=1, source_target_pairs={{16,24},{17,25},{18,26},{19,27},{20,28},{21,29},{22,30},{23,31},{2... | collective-permute-start | bytes 196616 | tf_op jit(solution)/shard_map/ppermute | solution.py:143
  38.7 3.0 %collective-permute-done.23.refs_0_ = bf16[64,512]{1,0:T(8,128)(2,1)S(1)} collective-permute-done((bf16[64,512]{1,0:T(8,128)(2,1)S(1)}, bf16[64,512]{1,0:T(8,128)(2,1)S(1)}, u32[]{:S(2)}, u32[]{:S(2)}) %collective-permute-start.23) | collective-permute-done | bytes 65568 | tf_op jit(solution)/shard_map/ppermute | solution.py:143
  41.7 0.7 %collective-permute-start.27 = (bf16[64,512]{1,0:T(8,128)(2,1)S(1)}, bf16[64,512]{1,0:T(8,128)(2,1)S(1)}, u32[]{:S(2)}, u32[]{:S(2)}) collective-permute-start(bf16[64,512]{1,0:T(8,128)(2,1)S(1)} %collective-permute-done.23.refs_0_), channel_id=1, source_target_pairs={{0,1},{1,0},{2,3},{3,2},{4,5},{5,4},{6,7},{7,6},{8,9},{9,8},{10,11... | collective-permute-start | bytes 196616 | tf_op jit(solution)/shard_map/ppermute | solution.py:130
  42.9 0.8 %collective-permute-start.29 = (bf16[64,512]{1,0:T(8,128)(2,1)S(1)}, bf16[64,512]{1,0:T(8,128)(2,1)S(1)}, u32[]{:S(2)}, u32[]{:S(2)}) collective-permute-start(bf16[64,512]{1,0:T(8,128)(2,1)S(1)} %collective-permute-done.25.refs_2_), channel_id=1, source_target_pairs={{0,1},{1,0},{2,3},{3,2},{4,5},{5,4},{6,7},{7,6},{8,9},{9,8},{10,11... | collective-permute-start | bytes 196616 | tf_op jit(solution)/shard_map/ppermute | solution.py:130
  43.7 0.8 %collective-permute-done.26.refs_3_ = bf16[64,512]{1,0:T(8,128)(2,1)S(1)} collective-permute-done((bf16[64,512]{1,0:T(8,128)(2,1)S(1)}, bf16[64,512]{1,0:T(8,128)(2,1)S(1)}, u32[]{:S(2)}, u32[]{:S(2)}) %collective-permute-start.26) | collective-permute-done | bytes 65568 | tf_op jit(solution)/shard_map/ppermute | solution.py:143
  45.0 1.2 %early_tiles.7.total_ref = f32[64,512]{1,0:T(8,128)S(1)} custom-call(bf16[8,512,512]{2,1,0:T(8,128)(2,1)S(1)} %place.1.placed_ref, bf16[64,512]{1,0:T(8,128)(2,1)S(1)} %collective-permute-done.23.refs_0_, bf16[64,512]{1,0:T(8,128)(2,1)S(1)} %collective-permute-done.24.refs_1_, bf16[64,512]{1,0:T(8,128)(2,1)S(1)} %collective-permute-done.25.refs_2_, ...), custom_call_target="tpu_custom_call" | custom-call | tf_op jit(solution)/shard_map/early_tiles/pallas_call | solution.py:97
  46.7 0.6 %copy.15 = bf16[1,512,64]{1,2,0:T(8,128)(2,1)} copy(bf16[1,512,64]{1,2,0:T(8,128)(2,1)S(1)} %bitcast.12) | data formatting | bytes 131072
  (57 shorter events, 6.2 us)
Async XLA Ops:
  0.0 4.5 %collective-permute-start = (bf16[64,512]{1,0:T(8,128)(2,1)}, bf16[64,512]{1,0:T(8,128)(2,1)S(1)}, u32[]{:S(2)}, u32[]{:S(2)}) collective-permute-start(bf16[64,512]{1,0:T(8,128)(2,1)} %bitcast.21), channel_id=1, source_target_pairs={{0,4},{1,5},{2,6},{3,7},{4,0},{5,1},{6,2},{7,3},{8,9},{9,8},{10,11... | collective-permute-start | bytes 196616 | tf_op jit(solution)/shard_map/ppermute | solution.py:143
  0.7 3.9 %collective-permute-start.1 = (bf16[64,512]{1,0:T(8,128)(2,1)}, bf16[64,512]{1,0:T(8,128)(2,1)S(1)}, u32[]{:S(2)}, u32[]{:S(2)}) collective-permute-start(bf16[64,512]{1,0:T(8,128)(2,1)} %bitcast.22), channel_id=1, source_target_pairs={{0,2},{1,3},{2,0},{3,1},{4,6},{5,7},{6,4},{7,5},{8,9},{9,8},{10,11... | collective-permute-start | bytes 196616 | tf_op jit(solution)/shard_map/ppermute | solution.py:143
  0.7 3.9 %collective-permute-start.2 = (bf16[64,512]{1,0:T(8,128)(2,1)}, bf16[64,512]{1,0:T(8,128)(2,1)S(1)}, u32[]{:S(2)}, u32[]{:S(2)}) collective-permute-start(bf16[64,512]{1,0:T(8,128)(2,1)} %bitcast.23), channel_id=1, source_target_pairs={{0,6},{1,7},{2,4},{3,5},{4,2},{5,3},{6,0},{7,1},{8,9},{9,8},{10,11... | collective-permute-start | bytes 196616 | tf_op jit(solution)/shard_map/ppermute | solution.py:143
  4.6 1.8 %collective-permute-start.3 = (bf16[64,512]{1,0:T(8,128)(2,1)S(1)}, bf16[64,512]{1,0:T(8,128)(2,1)S(1)}, u32[]{:S(2)}, u32[]{:S(2)}) collective-permute-start(bf16[64,512]{1,0:T(8,128)(2,1)S(1)} %collective-permute-done.refs_0_), channel_id=1, source_target_pairs={{0,1},{1,0},{2,3},{3,2},{4,5},{5,4},{6,7},{7,6},{8,9},{9,8},{10,11... | collective-permute-start | bytes 196616 | tf_op jit(solution)/shard_map/ppermute | solution.py:130
  7.3 8.7 %collective-permute-start.7 = (bf16[64,512]{1,0:T(8,128)(2,1)S(1)}, bf16[64,512]{1,0:T(8,128)(2,1)S(1)}, u32[]{:S(2)}, u32[]{:S(2)}) collective-permute-start(bf16[64,512]{1,0:T(8,128)(2,1)S(1)} %late_tile_and_solve.4.trace_in), channel_id=1, source_target_pairs={{0,12},{1,13},{2,14},{3,15},{4,8},{5,9},{6,10},{7,11},{8,16},{9,17... | collective-permute-start | bytes 196616 | tf_op jit(solution)/shard_map/ppermute | solution.py:143
  7.5 8.6 %collective-permute-start.8 = (bf16[64,512]{1,0:T(8,128)(2,1)S(1)}, bf16[64,512]{1,0:T(8,128)(2,1)S(1)}, u32[]{:S(2)}, u32[]{:S(2)}) collective-permute-start(bf16[64,512]{1,0:T(8,128)(2,1)S(1)} %late_tile_and_solve.4.trace_in), channel_id=1, source_target_pairs={{0,10},{1,11},{2,8},{3,9},{4,14},{5,15},{6,12},{7,13},{8,24},{9,25... | collective-permute-start | bytes 196616 | tf_op jit(solution)/shard_map/ppermute | solution.py:143
  14.6 2.5 %collective-permute-start.9 = (bf16[64,512]{1,0:T(8,128)(2,1)S(1)}, bf16[64,512]{1,0:T(8,128)(2,1)S(1)}, u32[]{:S(2)}, u32[]{:S(2)}) collective-permute-start(bf16[64,512]{1,0:T(8,128)(2,1)S(1)} %late_tile_and_solve.4.trace_in), channel_id=1, source_target_pairs={{0,14},{1,15},{2,12},{3,13},{4,10},{5,11},{6,8},{7,9}} | collective-permute-start | bytes 196616 | tf_op jit(solution)/shard_map/ppermute | solution.py:143
  15.3 1.9 %collective-permute-start.10 = (bf16[64,512]{1,0:T(8,128)(2,1)S(1)}, bf16[64,512]{1,0:T(8,128)(2,1)S(1)}, u32[]{:S(2)}, u32[]{:S(2)}) collective-permute-start(bf16[64,512]{1,0:T(8,128)(2,1)S(1)} %late_tile_and_solve.4.trace_in), channel_id=1, source_target_pairs={{0,8},{1,9},{2,10},{3,11},{4,12},{5,13},{6,14},{7,15},{8,0},{9,1},... | collective-permute-start | bytes 196616 | tf_op jit(solution)/shard_map/ppermute | solution.py:143
  16.0 1.7 %collective-permute-start.11 = (bf16[64,512]{1,0:T(8,128)(2,1)S(1)}, bf16[64,512]{1,0:T(8,128)(2,1)S(1)}, u32[]{:S(2)}, u32[]{:S(2)}) collective-permute-start(bf16[64,512]{1,0:T(8,128)(2,1)S(1)} %collective-permute-done.7.refs_0_), channel_id=1, source_target_pairs={{0,1},{1,0},{2,3},{3,2},{4,5},{5,4},{6,7},{7,6},{8,9},{9,8},{10,11... | collective-permute-start | bytes 196616 | tf_op jit(solution)/shard_map/ppermute | solution.py:130
  16.1 2.0 %collective-permute-start.12 = (bf16[64,512]{1,0:T(8,128)(2,1)S(1)}, bf16[64,512]{1,0:T(8,128)(2,1)S(1)}, u32[]{:S(2)}, u32[]{:S(2)}) collective-permute-start(bf16[64,512]{1,0:T(8,128)(2,1)S(1)} %collective-permute-done.8.refs_1_), channel_id=1, source_target_pairs={{0,1},{1,0},{2,3},{3,2},{4,5},{5,4},{6,7},{7,6},{8,9},{9,8},{10,11... | collective-permute-start | bytes 196616 | tf_op jit(solution)/shard_map/ppermute | solution.py:130
  17.1 1.4 %collective-permute-start.14 = (bf16[64,512]{1,0:T(8,128)(2,1)S(1)}, bf16[64,512]{1,0:T(8,128)(2,1)S(1)}, u32[]{:S(2)}, u32[]{:S(2)}) collective-permute-start(bf16[64,512]{1,0:T(8,128)(2,1)S(1)} %collective-permute-done.10.refs_3_), channel_id=1, source_target_pairs={{0,1},{1,0},{2,3},{3,2},{4,5},{5,4},{6,7},{7,6},{8,9},{9,8},{10,11... | collective-permute-start | bytes 196616 | tf_op jit(solution)/shard_map/ppermute | solution.py:130
  18.6 8.2 %collective-permute-start.15 = (bf16[64,512]{1,0:T(8,128)(2,1)S(1)}, bf16[64,512]{1,0:T(8,128)(2,1)S(1)}, u32[]{:S(2)}, u32[]{:S(2)}) collective-permute-start(bf16[64,512]{1,0:T(8,128)(2,1)S(1)} %late_tile_and_solve.5.trace_in), channel_id=1, source_target_pairs={{8,20},{9,21},{10,22},{11,23},{12,16},{13,17},{14,18},{15,19},{16,... | collective-permute-start | bytes 196616 | tf_op jit(solution)/shard_map/ppermute | solution.py:143
  24.7 2.5 %collective-permute-start.16 = (bf16[64,512]{1,0:T(8,128)(2,1)S(1)}, bf16[64,512]{1,0:T(8,128)(2,1)S(1)}, u32[]{:S(2)}, u32[]{:S(2)}) collective-permute-start(bf16[64,512]{1,0:T(8,128)(2,1)S(1)} %late_tile_and_solve.5.trace_in), channel_id=1, source_target_pairs={{8,18},{9,19},{10,16},{11,17},{12,22},{13,23},{14,20},{15,21}} | collective-permute-start | bytes 196616 | tf_op jit(solution)/shard_map/ppermute | solution.py:143
  25.4 1.9 %collective-permute-start.17 = (bf16[64,512]{1,0:T(8,128)(2,1)S(1)}, bf16[64,512]{1,0:T(8,128)(2,1)S(1)}, u32[]{:S(2)}, u32[]{:S(2)}) collective-permute-start(bf16[64,512]{1,0:T(8,128)(2,1)S(1)} %late_tile_and_solve.5.trace_in), channel_id=1, source_target_pairs={{8,22},{9,23},{10,20},{11,21},{12,18},{13,19},{14,16},{15,17}} | collective-permute-start | bytes 196616 | tf_op jit(solution)/shard_map/ppermute | solution.py:143
  26.0 1.7 %collective-permute-start.18 = (bf16[64,512]{1,0:T(8,128)(2,1)S(1)}, bf16[64,512]{1,0:T(8,128)(2,1)S(1)}, u32[]{:S(2)}, u32[]{:S(2)}) collective-permute-start(bf16[64,512]{1,0:T(8,128)(2,1)S(1)} %late_tile_and_solve.5.trace_in), channel_id=1, source_target_pairs={{8,16},{9,17},{10,18},{11,19},{12,20},{13,21},{14,22},{15,23},{16,... | collective-permute-start | bytes 196616 | tf_op jit(solution)/shard_map/ppermute | solution.py:143
  26.7 1.4 %collective-permute-start.19 = (bf16[64,512]{1,0:T(8,128)(2,1)S(1)}, bf16[64,512]{1,0:T(8,128)(2,1)S(1)}, u32[]{:S(2)}, u32[]{:S(2)}) collective-permute-start(bf16[64,512]{1,0:T(8,128)(2,1)S(1)} %collective-permute-done.15.refs_0_), channel_id=1, source_target_pairs={{0,1},{1,0},{2,3},{3,2},{4,5},{5,4},{6,7},{7,6},{8,9},{9,8},{10,11... | collective-permute-start | bytes 196616 | tf_op jit(solution)/shard_map/ppermute | solution.py:130
  29.0 12.7 %collective-permute-start.23 = (bf16[64,512]{1,0:T(8,128)(2,1)S(1)}, bf16[64,512]{1,0:T(8,128)(2,1)S(1)}, u32[]{:S(2)}, u32[]{:S(2)}) collective-permute-start(bf16[64,512]{1,0:T(8,128)(2,1)S(1)} %late_tile_and_solve.6.trace_in), channel_id=1, source_target_pairs={{16,28},{17,29},{18,30},{19,31},{20,24},{21,25},{22,26},{23,27},{2... | collective-permute-start | bytes 196616 | tf_op jit(solution)/shard_map/ppermute | solution.py:143
  29.0 13.4 %collective-permute-start.24 = (bf16[64,512]{1,0:T(8,128)(2,1)S(1)}, bf16[64,512]{1,0:T(8,128)(2,1)S(1)}, u32[]{:S(2)}, u32[]{:S(2)}) collective-permute-start(bf16[64,512]{1,0:T(8,128)(2,1)S(1)} %late_tile_and_solve.6.trace_in), channel_id=1, source_target_pairs={{16,26},{17,27},{18,24},{19,25},{20,30},{21,31},{22,28},{23,29}} | collective-permute-start | bytes 196616 | tf_op jit(solution)/shard_map/ppermute | solution.py:143
  30.3 12.5 %collective-permute-start.25 = (bf16[64,512]{1,0:T(8,128)(2,1)S(1)}, bf16[64,512]{1,0:T(8,128)(2,1)S(1)}, u32[]{:S(2)}, u32[]{:S(2)}) collective-permute-start(bf16[64,512]{1,0:T(8,128)(2,1)S(1)} %late_tile_and_solve.6.trace_in), channel_id=1, source_target_pairs={{16,30},{17,31},{18,28},{19,29},{20,26},{21,27},{22,24},{23,25}} | collective-permute-start | bytes 196616 | tf_op jit(solution)/shard_map/ppermute | solution.py:143
  31.6 12.9 %collective-permute-start.26 = (bf16[64,512]{1,0:T(8,128)(2,1)S(1)}, bf16[64,512]{1,0:T(8,128)(2,1)S(1)}, u32[]{:S(2)}, u32[]{:S(2)}) collective-permute-start(bf16[64,512]{1,0:T(8,128)(2,1)S(1)} %late_tile_and_solve.6.trace_in), channel_id=1, source_target_pairs={{16,24},{17,25},{18,26},{19,27},{20,28},{21,29},{22,30},{23,31},{2... | collective-permute-start | bytes 196616 | tf_op jit(solution)/shard_map/ppermute | solution.py:143
  41.7 3.2 %collective-permute-start.27 = (bf16[64,512]{1,0:T(8,128)(2,1)S(1)}, bf16[64,512]{1,0:T(8,128)(2,1)S(1)}, u32[]{:S(2)}, u32[]{:S(2)}) collective-permute-start(bf16[64,512]{1,0:T(8,128)(2,1)S(1)} %collective-permute-done.23.refs_0_), channel_id=1, source_target_pairs={{0,1},{1,0},{2,3},{3,2},{4,5},{5,4},{6,7},{7,6},{8,9},{9,8},{10,11... | collective-permute-start | bytes 196616 | tf_op jit(solution)/shard_map/ppermute | solution.py:130
  42.4 2.6 %collective-permute-start.28 = (bf16[64,512]{1,0:T(8,128)(2,1)S(1)}, bf16[64,512]{1,0:T(8,128)(2,1)S(1)}, u32[]{:S(2)}, u32[]{:S(2)}) collective-permute-start(bf16[64,512]{1,0:T(8,128)(2,1)S(1)} %collective-permute-done.24.refs_1_), channel_id=1, source_target_pairs={{0,1},{1,0},{2,3},{3,2},{4,5},{5,4},{6,7},{7,6},{8,9},{9,8},{10,11... | collective-permute-start | bytes 196616 | tf_op jit(solution)/shard_map/ppermute | solution.py:130
  42.9 2.1 %collective-permute-start.29 = (bf16[64,512]{1,0:T(8,128)(2,1)S(1)}, bf16[64,512]{1,0:T(8,128)(2,1)S(1)}, u32[]{:S(2)}, u32[]{:S(2)}) collective-permute-start(bf16[64,512]{1,0:T(8,128)(2,1)S(1)} %collective-permute-done.25.refs_2_), channel_id=1, source_target_pairs={{0,1},{1,0},{2,3},{3,2},{4,5},{5,4},{6,7},{7,6},{8,9},{9,8},{10,11... | collective-permute-start | bytes 196616 | tf_op jit(solution)/shard_map/ppermute | solution.py:130
  44.5 1.7 %collective-permute-start.30 = (bf16[64,512]{1,0:T(8,128)(2,1)S(1)}, bf16[64,512]{1,0:T(8,128)(2,1)S(1)}, u32[]{:S(2)}, u32[]{:S(2)}) collective-permute-start(bf16[64,512]{1,0:T(8,128)(2,1)S(1)} %collective-permute-done.26.refs_3_), channel_id=1, source_target_pairs={{0,1},{1,0},{2,3},{3,2},{4,5},{5,4},{6,7},{7,6},{8,9},{9,8},{10,11... | collective-permute-start | bytes 196616 | tf_op jit(solution)/shard_map/ppermute | solution.py:130
  (11 other events, 18.5 us)

commit v4 on v3

v4 whole, which is shorter than its diff:
```python
import functools

import jax
import jax.numpy as jnp
from jax import lax
from jax.experimental import pallas as pl
from jax.experimental.pallas import tpu as pltpu
from jax.sharding import PartitionSpec as P

CORES = 2
VMEM_LIMIT = 48 * 2**20
LAST_LAST = (((1,), (1,)), ((), ()))
LAST_FIRST = (((1,), (0,)), ((), ()))
FIRST_LAST = (((0,), (1,)), ((), ()))
IN_VMEM = pl.BlockSpec(memory_space=pltpu.VMEM)
IN_SMEM = pl.BlockSpec(memory_space=pltpu.SMEM)
ANYWHERE = pl.BlockSpec(memory_space=pl.ANY)


def params():
    return pltpu.CompilerParams(vmem_limit_bytes=VMEM_LIMIT)


def step_of(order, chips):
    half = chips // 2
    return half + order // 2 if order % 2 == 0 else half - 1 - order // 2


def order_of(step, chips):
    half = chips // 2
    return jnp.where(step >= half, 2 * (step - half), 2 * (half - 1 - step) + 1)


def position_of(slot, chips, cols_ref):
    me = lax.axis_index("row")
    chip, core = me // CORES, me % CORES
    column = cols_ref[0, 0, slot]
    return jnp.where(column % CORES == core, 0, chips) + order_of(chip ^ (column // CORES), chips)


def place_kernel(chips, cols_ref, count_ref, greens_ref, solve_in, source_in, placed_ref, solve_ref, source_ref, sems):
    slots, positions = greens_ref.shape[2], placed_ref.shape[0]

    @pl.when(lax.axis_index("slab") == 0)
    def _():
        copies = [
            pltpu.make_async_copy(solve_in.at[0, 0], solve_ref, sems.at[slots]),
            pltpu.make_async_copy(source_in, source_ref, sems.at[slots + 1]),
        ]
        for copy in copies:
            copy.start()
        if positions > slots:
            placed_ref[...] = jnp.zeros_like(placed_ref)
        moves = []
        for slot in range(slots):
            position = position_of(slot, chips, cols_ref)
            move = pltpu.make_async_copy(greens_ref.at[0, 0, slot], placed_ref.at[position], sems.at[slot])
            used = slot < count_ref[0, 0]
            moves.append((used, move))
            pl.when(used)(move.start)
            if positions == slots:

                @pl.when(jnp.logical_not(used))
                def _():
                    placed_ref[position] = jnp.zeros(placed_ref.shape[1:], placed_ref.dtype)

        for used, move in moves:
            pl.when(used)(move.wait)
        for copy in copies:
            copy.wait()


def place(chips, cols, count, greens, solve, source):
    slots, rows, depth = greens.shape[2:]
    return pl.pallas_call(
        functools.partial(place_kernel, chips),
        out_shape=(
            pltpu.VMEM((chips * CORES, rows, depth), greens.dtype),
            pltpu.VMEM(solve.shape[2:], solve.dtype),
            pltpu.VMEM(source.shape, source.dtype),
        ),
        in_specs=[IN_SMEM] * 2 + [ANYWHERE] * 3,
        out_specs=(IN_VMEM,) * 3,
        scratch_shapes=[pltpu.SemaphoreType.DMA((slots + 2,))],
        compiler_params=params(),
        cost_estimate=pl.CostEstimate(flops=0, bytes_accessed=2 * greens.size * 2, transcendentals=0),
        name="place",
    )(cols, count, greens, solve, source)


def fold_kernel(section, chips, cols_ref, count_ref, greens_ref, solve_in, source_in, folded_ref, base_ref, held_ref, solve_ref, source_ref, sems):
    slots, positions = greens_ref.shape[2], folded_ref.shape[0]

    @pl.when(lax.axis_index("slab") == section)
    def _():
        copies = [
            pltpu.make_async_copy(greens_ref.at[0, 0, slot], held_ref.at[slot], sems.at[slot]) for slot in range(slots)
        ]
        early_copies = [
            pltpu.make_async_copy(solve_in.at[0, 0], solve_ref, sems.at[slots]),
            pltpu.make_async_copy(source_in, source_ref, sems.at[slots + 1]),
        ]
        for copy in early_copies + copies:
            copy.start()
        if positions > slots:
            folded_ref[...] = jnp.zeros_like(folded_ref)
        for copy in early_copies:
            copy.wait()
        base_ref[...] = lax.dot_general(source_ref[...], solve_ref[...], LAST_LAST, preferred_element_type=jnp.float32)
        for slot, copy in enumerate(copies):
            position = position_of(slot, chips, cols_ref)
            copy.wait()
            solved = lax.dot_general(held_ref[slot], solve_ref[...], FIRST_LAST, preferred_element_type=jnp.float32)
            used = slot < count_ref[0, 0]
            folded_ref[position] = jnp.where(used, solved, jnp.zeros_like(solved)).astype(folded_ref.dtype)


def fold(section, chips, cols, count, greens, solve, source):
    slots, rows, depth = greens.shape[2:]
    return pl.pallas_call(
        functools.partial(fold_kernel, section, chips),
        out_shape=(
            pltpu.VMEM((chips * CORES, depth, rows), greens.dtype),
            pltpu.VMEM(source.shape, jnp.float32),
        ),
        in_specs=[IN_SMEM] * 2 + [ANYWHERE] * 3,
        out_specs=(IN_VMEM,) * 2,
        scratch_shapes=[
            pltpu.VMEM((slots, rows, depth), greens.dtype),
            pltpu.VMEM(solve.shape[2:], solve.dtype),
            pltpu.VMEM(source.shape, source.dtype),
            pltpu.SemaphoreType.DMA((slots + 2,)),
        ],
        compiler_params=params(),
        cost_estimate=pl.CostEstimate(
            flops=2 * greens.size * rows, bytes_accessed=2 * greens.size * 2, transcendentals=0
        ),
        name="fold",
    )(cols, count, greens, solve, source)


def products(tiles, positions, placed_ref, folded, total):
    for tile, position in zip(tiles, positions):
        dims = LAST_FIRST if folded else LAST_LAST
        total += lax.dot_general(tile[...], placed_ref[position], dims, preferred_element_type=jnp.float32)
    return total


def early_kernel(section, positions, placed_ref, before_ref, *refs):
    tiles, total_ref = refs[:-1], refs[-1]

    @pl.when(lax.axis_index("slab") == section)
    def _():
        before = before_ref[...].astype(jnp.float32)
        total_ref[...] = products(tiles, positions, placed_ref, section > 0, before)


def early(section, positions, placed, before, tiles):
    return pl.pallas_call(
        functools.partial(early_kernel, section, positions),
        out_shape=pltpu.VMEM(before.shape, jnp.float32),
        in_specs=[IN_VMEM] * (2 + len(tiles)),
        out_specs=IN_VMEM,
        compiler_params=params(),
        name="early_tiles",
    )(placed, before, *tiles)


def late_kernel(section, position, placed_ref, total_ref, tile_ref, *refs):
    solve_ref, trace_ref = refs[0], refs[-1]

    @pl.when(lax.axis_index("slab") == section)
    def _():
        total = products([tile_ref], [position], placed_ref, section > 0, total_ref[...])
        if section == 0:
            coupled = total.astype(jnp.bfloat16)
            total = lax.dot_general(coupled, solve_ref[...], LAST_LAST, preferred_element_type=jnp.float32)
        trace_ref[...] = total.astype(trace_ref.dtype)


def late(section, position, placed, total, tile, solve, trace):
    operands = (placed, total, tile, solve, trace) if section == 0 else (placed, total, tile, trace)
    return pl.pallas_call(
        functools.partial(late_kernel, section, position),
        out_shape=pltpu.VMEM(trace.shape, trace.dtype),
        in_specs=[IN_VMEM] * len(operands),
        out_specs=IN_VMEM,
        input_output_aliases={len(operands) - 1: 0},
        compiler_params=params(),
        name="late_tile",
    )(*operands)


def swapped(tile, rows):
    return lax.ppermute(tile, "row", [(r, r ^ 1) for r in range(rows)])


def sent(tile, source, target, step, slabs, rows, via=None):
    pairs = [(source * rows + r, target * rows + (r ^ (step * CORES))) for r in range(rows)]
    busy = {source, target}
    if source != target and via is not None:
        pairs += [(target * rows + r, via * rows + (r if via != source else r ^ (step * CORES))) for r in range(rows)]
    if via not in (None, source):
        pairs += [(via * rows + r, source * rows + r) for r in range(rows)]
    if via is not None:
        busy.add(via)
        pairs += [(s * rows + r, s * rows + (r ^ 1)) for s in range(slabs) if s not in busy for r in range(rows)]
    return lax.ppermute(tile, ("slab", "row"), pairs)


def third_slabs(section, slabs, chips):
    free = [s % slabs for s in range(section + 1, section + slabs - 1)]
    free = [s for s in free if s != section - 2][-1:]
    return (free + [None] * chips)[:chips]


def direct(forcing, inflow, self_solve, greens, kept_cols, counts):
    slabs, rows = lax.axis_size("slab"), lax.axis_size("row")
    chips = rows // CORES
    steps = [step_of(order, chips) for order in range(chips)]
    entering, source = inflow.T, forcing[0].T
    greens, self_solve, source = (
        pltpu.with_memory_space_constraint(array, pltpu.HBM) for array in (greens, self_solve, source)
    )
    placed, solve, base = place(chips, kept_cols, counts, greens, self_solve, source)
    trace = jnp.zeros(entering.shape, jnp.bfloat16)
    for section in range(slabs):
        if section == 0:
            own = [sent(entering, 0, 0, step, slabs, rows, 0) for step in steps if step]
            entering, placed, base, solve, own[0] = lax.optimization_barrier((entering, placed, base, solve, own[0]))
            orders = [steps.index(0)] + [order for order, step in enumerate(steps) if step]
            own = [entering] + own
        else:
            vias = third_slabs(section, slabs, chips)
            own = [sent(trace, section - 1, section, step, slabs, rows, via) for step, via in zip(steps, vias)]
            orders = list(range(chips))
            placed, base = fold(section, chips, kept_cols, counts, greens, self_solve, source)
            placed, base, own[0] = lax.optimization_barrier((placed, base, own[0]))
        other = [swapped(tile, rows) for tile in own]
        arriving = []
        for order, *both in zip(orders, own, other):
            arriving += [(tile, side * chips + order) for side, tile in enumerate(both)]
        total = base
        for first in [0, *range(3, len(arriving) - 1, 2)]:
            tiles, positions = zip(*arriving[first : first + 3 if first == 0 else first + 2])
            total = early(section, positions, placed, total, tiles)
        trace = late(section, arriving[-1][1], placed, total, other[-1], solve, trace)
    return trace.T[None]


def shifted(array, axis, by):
    size = lax.axis_size(axis)
    return lax.ppermute(array, axis, [(i, i + by) for i in range(size) if 0 <= i + by < size])


def gathering(forcing, inflow, self_solve, greens, kept_cols, counts):
    source, green_row, solve = forcing[0], greens[0, 0], self_solve[0, 0]
    valid = jnp.arange(green_row.shape[0], dtype=jnp.int32) < counts[0, 0]
    incoming = inflow
    for section in range(lax.axis_size("slab")):
        if section > 0:
            arrived = shifted(trace, "slab", 1)
            incoming = jnp.where(lax.axis_index("slab") == 0, inflow, arrived)
        gathered = lax.all_gather(incoming, "row", axis=0)
        chosen = gathered[kept_cols[0, 0]]
        chosen = jnp.where(valid[:, None, None], chosen, jnp.zeros((), chosen.dtype))
        total = jnp.einsum("kij,kjw->iw", green_row, chosen, preferred_element_type=jnp.float32)
        coupled = (total + source.astype(jnp.float32)).astype(jnp.bfloat16)
        trace = jnp.dot(solve, coupled, preferred_element_type=jnp.float32).astype(jnp.bfloat16)
    return trace[None]


def shards(forcing, inflow, self_solve, greens, kept_cols, counts):
    rows, slots = lax.axis_size("row"), greens.shape[2]
    chips = rows // CORES
    if rows == chips * CORES and chips & (chips - 1) == 0 and 1 < chips and rows <= 2 * slots:
        return direct(forcing, inflow, self_solve, greens, kept_cols, counts)
    return gathering(forcing, inflow, self_solve, greens, kept_cols, counts)


def solution(mesh):
    placed = (
        P("slab", "row", None),
        P("row", None),
        P("slab", "row", None, None),
        P("slab", "row", None, None, None),
        P("slab", "row", None),
        P("slab", "row"),
    )
    return jax.shard_map(
        shards, mesh=mesh, in_specs=placed, out_specs=P("slab", "row", None), check_vma=False
    )
```

time: 47.5 us -> 44.9 us (0.945)
  starting transfers between devices: 34.1 us -> 28.2 us
  Pallas kernels: 3.73 us -> 9.14 us
  waiting for transfers between devices: 7.33 us -> 5.36 us
    pallas_call x9 -> x20, Pallas kernels: 3.73 us -> 9.14 us  [the longest x3 7.28 us: fold(): pl.pallas_call(functools.partial(fold_kernel, section, chips), out_shape=...]
    ppermute x15, starting transfers between devices: 27.7 us -> 22.4 us  [sent(): return lax.ppermute(tile, ('slab', 'row'), pairs)]
    ppermute x15, waiting for transfers between devices: 4.22 us -> 2.26 us  [sent(): return lax.ppermute(tile, ('slab', 'row'), pairs)]
    ppermute x16, starting transfers between devices: 6.47 us -> 5.77 us  [swapped(): return lax.ppermute(tile, 'row', [(r, r ^ 1) for r in range(rows)])]
    unnamed x9 -> x7, local copies, waits for them, and re-layouts: 1.3 us -> 1.29 us
  transfers between devices with their start and end apart: 31 -> 31, of which waited for: 14 -> 14; matrix products, arithmetic and copies ran while one was open for 0% -> 0% of each run, Pallas kernels for 7% -> 20%
where the time goes in v4:
time: 44.9 us
  starting transfers between devices  28.2 us (63%)
  Pallas kernels  9.14 us (20%)
  waiting for transfers between devices  5.36 us (12%)
  local copies, waits for them, and re-layouts  1.3 us (3%)
  between operations  0.89 us (2%)
    ppermute x15, starting transfers between devices, sent(): return lax.ppermute(tile, ('slab', 'row'), pairs)  22.4 us
    pallas_call x3, Pallas kernels, fold(): pl.pallas_call(functools.partial(fold_kernel, section, chips), out_shape=...  7.28 us
    ppermute x16, starting transfers between devices, swapped(): return lax.ppermute(tile, 'row', [(r, r ^ 1) for r in range(rows)])  5.77 us
    ppermute x16, waiting for transfers between devices, swapped(): return lax.ppermute(tile, 'row', [(r, r ^ 1) for r in range(rows)])  3.09 us
    ppermute x15, waiting for transfers between devices, sent(): return lax.ppermute(tile, ('slab', 'row'), pairs)  2.26 us
    unnamed x7, local copies, waits for them, and re-layouts  1.29 us
    pallas_call x12, Pallas kernels, early(): pl.pallas_call(functools.partial(early_kernel, section, positions), out_s...  1 us
  transfers between devices with their start and end apart: 31, of which 14 were waited for; matrix products, arithmetic and copies ran while one was open for 0% of the time, Pallas kernels for 20%

profile of v4, /device:TPU:7, one launch (start us, length us, event | category | flops | bytes accessed | tf_op | source)
XLA Modules:
  0.0 44.9 jit_solution(9804914528182466423)
XLA Ops:
  0.0 0.7 %collective-permute-start = (bf16[64,512]{1,0:T(8,128)(2,1)}, bf16[64,512]{1,0:T(8,128)(2,1)S(1)}, u32[]{:S(2)}, u32[]{:S(2)}) collective-permute-start(bf16[64,512]{1,0:T(8,128)(2,1)} %bitcast.8), channel_id=1, source_target_pairs={{0,4},{1,5},{2,6},{3,7},{4,0},{5,1},{6,2},{7,3},{8,9},{9,8},{10,11... | collective-permute-start | bytes 196616 | tf_op jit(solution)/shard_map/ppermute | solution.py:208
  1.9 0.6 %copy-done.1 = s32[1,1,8]{2,1,0:T(1,128)S(1)} copy-done((s32[1,1,8]{2,1,0:T(1,128)S(1)}, s32[1,1,8]{2,1,0:T(1,128)}, u32[]{:S(2)}) %copy-start.1) | copy-done | bytes 56
  2.5 0.6 %place.1 = (bf16[8,512,512]{2,1,0:T(8,128)(2,1)S(1)}, bf16[512,512]{1,0:T(8,128)(2,1)S(1)}, bf16[64,512]{1,0:T(8,128)(2,1)S(1)}) custom-call(s32[1,1,8]{2,1,0:T(1,128)S(1)} %copy-done.1, s32[1,1]{1,0:T(1,128)S(6)} %copy.16.count_ref, bf16[1,1,8,512,512]{4,3,2,1,0:T(8,128)(2,1)} %greens_ref.7, bf16[1,1,512,512]{3,2,1,0:T(8,128)(2,1)} %solve_in.7, ...), custom_call_target="tpu_custom_call" | custom-call | bytes 8388608 | tf_op jit(solution)/shard_map/place/pallas_call | solution.py:75
  5.2 8.2 %collective-permute-start.7 = (bf16[64,512]{1,0:T(8,128)(2,1)S(1)}, bf16[64,512]{1,0:T(8,128)(2,1)S(1)}, u32[]{:S(2)}, u32[]{:S(2)}) collective-permute-start(bf16[64,512]{1,0:T(8,128)(2,1)S(1)} %late_tile.4.refs_0_), channel_id=1, source_target_pairs={{0,12},{1,13},{2,14},{3,15},{4,8},{5,9},{6,10},{7,11},{8,24},{9,25... | collective-permute-start | bytes 196616 | tf_op jit(solution)/shard_map/ppermute | solution.py:208
  13.4 0.7 %collective-permute-start.9 = (bf16[64,512]{1,0:T(8,128)(2,1)S(1)}, bf16[64,512]{1,0:T(8,128)(2,1)S(1)}, u32[]{:S(2)}, u32[]{:S(2)}) collective-permute-start(bf16[64,512]{1,0:T(8,128)(2,1)S(1)} %late_tile.4.refs_0_), channel_id=1, source_target_pairs={{0,10},{1,11},{2,8},{3,9},{4,14},{5,15},{6,12},{7,13}} | collective-permute-start | bytes 196616 | tf_op jit(solution)/shard_map/ppermute | solution.py:208
  14.1 0.7 %collective-permute-start.11 = (bf16[64,512]{1,0:T(8,128)(2,1)S(1)}, bf16[64,512]{1,0:T(8,128)(2,1)S(1)}, u32[]{:S(2)}, u32[]{:S(2)}) collective-permute-start(bf16[64,512]{1,0:T(8,128)(2,1)S(1)} %late_tile.4.refs_0_), channel_id=1, source_target_pairs={{0,14},{1,15},{2,12},{3,13},{4,10},{5,11},{6,8},{7,9}} | collective-permute-start | bytes 196616 | tf_op jit(solution)/shard_map/ppermute | solution.py:208
  14.7 0.7 %collective-permute-start.13 = (bf16[64,512]{1,0:T(8,128)(2,1)S(1)}, bf16[64,512]{1,0:T(8,128)(2,1)S(1)}, u32[]{:S(2)}, u32[]{:S(2)}) collective-permute-start(bf16[64,512]{1,0:T(8,128)(2,1)S(1)} %late_tile.4.refs_0_), channel_id=1, source_target_pairs={{0,8},{1,9},{2,10},{3,11},{4,12},{5,13},{6,14},{7,15}} | collective-permute-start | bytes 196616 | tf_op jit(solution)/shard_map/ppermute | solution.py:208
  15.4 0.7 %fold.5 = (bf16[8,512,512]{2,1,0:T(8,128)(2,1)S(1)}, f32[64,512]{1,0:T(8,128)S(1)}) custom-call(s32[1,1,8]{2,1,0:T(1,128)S(1)} %copy-done.1, s32[1,1]{1,0:T(1,128)S(6)} %copy.16.count_ref, bf16[1,1,8,512,512]{4,3,2,1,0:T(8,128)(2,1)} %greens_ref.7, bf16[1,1,512,512]{3,2,1,0:T(8,128)(2,1)} %solve_in.7, bf16[64,512]{1,0:T(8,128)(2,1)} %bitcast.14), custom_call_target="tpu_custom_call" | custom-call | flops 2147483648 | bytes 8388608 | tf_op jit(solution)/shard_map/fold/pallas_call | solution.py:120
  18.2 5.2 %collective-permute-start.15 = (bf16[64,512]{1,0:T(8,128)(2,1)S(1)}, bf16[64,512]{1,0:T(8,128)(2,1)S(1)}, u32[]{:S(2)}, u32[]{:S(2)}) collective-permute-start(bf16[64,512]{1,0:T(8,128)(2,1)S(1)} %late_tile.5.refs_0_), channel_id=1, source_target_pairs={{8,20},{9,21},{10,22},{11,23},{12,16},{13,17},{14,18},{15,19},{16,... | collective-permute-start | bytes 196616 | tf_op jit(solution)/shard_map/ppermute | solution.py:208
  23.4 0.7 %collective-permute-start.17 = (bf16[64,512]{1,0:T(8,128)(2,1)S(1)}, bf16[64,512]{1,0:T(8,128)(2,1)S(1)}, u32[]{:S(2)}, u32[]{:S(2)}) collective-permute-start(bf16[64,512]{1,0:T(8,128)(2,1)S(1)} %late_tile.5.refs_0_), channel_id=1, source_target_pairs={{8,18},{9,19},{10,16},{11,17},{12,22},{13,23},{14,20},{15,21}} | collective-permute-start | bytes 196616 | tf_op jit(solution)/shard_map/ppermute | solution.py:208
  24.0 0.7 %collective-permute-start.19 = (bf16[64,512]{1,0:T(8,128)(2,1)S(1)}, bf16[64,512]{1,0:T(8,128)(2,1)S(1)}, u32[]{:S(2)}, u32[]{:S(2)}) collective-permute-start(bf16[64,512]{1,0:T(8,128)(2,1)S(1)} %late_tile.5.refs_0_), channel_id=1, source_target_pairs={{8,22},{9,23},{10,20},{11,21},{12,18},{13,19},{14,16},{15,17}} | collective-permute-start | bytes 196616 | tf_op jit(solution)/shard_map/ppermute | solution.py:208
  24.7 0.7 %collective-permute-start.21 = (bf16[64,512]{1,0:T(8,128)(2,1)S(1)}, bf16[64,512]{1,0:T(8,128)(2,1)S(1)}, u32[]{:S(2)}, u32[]{:S(2)}) collective-permute-start(bf16[64,512]{1,0:T(8,128)(2,1)S(1)} %late_tile.5.refs_0_), channel_id=1, source_target_pairs={{8,16},{9,17},{10,18},{11,19},{12,20},{13,21},{14,22},{15,23}} | collective-permute-start | bytes 196616 | tf_op jit(solution)/shard_map/ppermute | solution.py:208
  25.4 0.7 %fold.4 = (bf16[8,512,512]{2,1,0:T(8,128)(2,1)S(1)}, f32[64,512]{1,0:T(8,128)S(1)}) custom-call(s32[1,1,8]{2,1,0:T(1,128)S(1)} %copy-done.2, s32[1,1]{1,0:T(1,128)S(6)} %copy.16.count_ref, bf16[1,1,8,512,512]{4,3,2,1,0:T(8,128)(2,1)} %greens_ref.7, bf16[1,1,512,512]{3,2,1,0:T(8,128)(2,1)} %solve_in.7, bf16[64,512]{1,0:T(8,128)(2,1)} %bitcast.15), custom_call_target="tpu_custom_call" | custom-call | flops 2147483648 | bytes 8388608 | tf_op jit(solution)/shard_map/fold/pallas_call | solution.py:120
  26.1 0.5 %collective-permute-start.16 = (bf16[64,512]{1,0:T(8,128)(2,1)S(1)}, bf16[64,512]{1,0:T(8,128)(2,1)S(1)}, u32[]{:S(2)}, u32[]{:S(2)}) collective-permute-start(bf16[64,512]{1,0:T(8,128)(2,1)S(1)} %collective-permute-done.15.refs_0_), channel_id=1, source_target_pairs={{0,1},{1,0},{2,3},{3,2},{4,5},{5,4},{6,7},{7,6},{8,9},{9,8},{10,11... | collective-permute-start | bytes 196616 | tf_op jit(solution)/shard_map/ppermute | solution.py:195
  28.4 1.3 %collective-permute-start.25 = (bf16[64,512]{1,0:T(8,128)(2,1)S(1)}, bf16[64,512]{1,0:T(8,128)(2,1)S(1)}, u32[]{:S(2)}, u32[]{:S(2)}) collective-permute-start(bf16[64,512]{1,0:T(8,128)(2,1)S(1)} %late_tile.6.refs_0_), channel_id=1, source_target_pairs={{16,26},{17,27},{18,24},{19,25},{20,30},{21,31},{22,28},{23,29}} | collective-permute-start | bytes 196616 | tf_op jit(solution)/shard_map/ppermute | solution.py:208
  29.6 1.3 %collective-permute-start.27 = (bf16[64,512]{1,0:T(8,128)(2,1)S(1)}, bf16[64,512]{1,0:T(8,128)(2,1)S(1)}, u32[]{:S(2)}, u32[]{:S(2)}) collective-permute-start(bf16[64,512]{1,0:T(8,128)(2,1)S(1)} %late_tile.6.refs_0_), channel_id=1, source_target_pairs={{16,30},{17,31},{18,28},{19,29},{20,26},{21,27},{22,24},{23,25}} | collective-permute-start | bytes 196616 | tf_op jit(solution)/shard_map/ppermute | solution.py:208
  30.9 1.3 %collective-permute-start.29 = (bf16[64,512]{1,0:T(8,128)(2,1)S(1)}, bf16[64,512]{1,0:T(8,128)(2,1)S(1)}, u32[]{:S(2)}, u32[]{:S(2)}) collective-permute-start(bf16[64,512]{1,0:T(8,128)(2,1)S(1)} %late_tile.6.refs_0_), channel_id=1, source_target_pairs={{16,24},{17,25},{18,26},{19,27},{20,28},{21,29},{22,30},{23,31}} | collective-permute-start | bytes 196616 | tf_op jit(solution)/shard_map/ppermute | solution.py:208
  32.2 6.0 %fold.3 = (bf16[8,512,512]{2,1,0:T(8,128)(2,1)S(1)}, f32[64,512]{1,0:T(8,128)S(1)}) custom-call(s32[1,1,8]{2,1,0:T(1,128)S(1)} %copy-done.2, s32[1,1]{1,0:T(1,128)S(6)} %copy.16.count_ref, bf16[1,1,8,512,512]{4,3,2,1,0:T(8,128)(2,1)} %greens_ref.7, bf16[1,1,512,512]{3,2,1,0:T(8,128)(2,1)} %solve_in.7, bf16[64,512]{1,0:T(8,128)(2,1)} %bitcast.16), custom_call_target="tpu_custom_call" | custom-call | flops 2147483648 | bytes 8388608 | tf_op jit(solution)/shard_map/fold/pallas_call | solution.py:120
  38.2 0.6 %collective-permute-done.23.refs_0_ = bf16[64,512]{1,0:T(8,128)(2,1)S(1)} collective-permute-done((bf16[64,512]{1,0:T(8,128)(2,1)S(1)}, bf16[64,512]{1,0:T(8,128)(2,1)S(1)}, u32[]{:S(2)}, u32[]{:S(2)}) %collective-permute-start.23) | collective-permute-done | bytes 65568 | tf_op jit(solution)/shard_map/ppermute | solution.py:208
  38.8 1.1 %collective-permute-start.24 = (bf16[64,512]{1,0:T(8,128)(2,1)S(1)}, bf16[64,512]{1,0:T(8,128)(2,1)S(1)}, u32[]{:S(2)}, u32[]{:S(2)}) collective-permute-start(bf16[64,512]{1,0:T(8,128)(2,1)S(1)} %collective-permute-done.23.refs_0_), channel_id=1, source_target_pairs={{0,1},{1,0},{2,3},{3,2},{4,5},{5,4},{6,7},{7,6},{8,9},{9,8},{10,11... | collective-permute-start | bytes 196616 | tf_op jit(solution)/shard_map/ppermute | solution.py:195
  40.0 1.6 %collective-permute-done.27.refs_1_ = bf16[64,512]{1,0:T(8,128)(2,1)S(1)} collective-permute-done((bf16[64,512]{1,0:T(8,128)(2,1)S(1)}, bf16[64,512]{1,0:T(8,128)(2,1)S(1)}, u32[]{:S(2)}, u32[]{:S(2)}) %collective-permute-start.27) | collective-permute-done | bytes 65568 | tf_op jit(solution)/shard_map/ppermute | solution.py:208
  41.6 0.7 %collective-permute-start.28 = (bf16[64,512]{1,0:T(8,128)(2,1)S(1)}, bf16[64,512]{1,0:T(8,128)(2,1)S(1)}, u32[]{:S(2)}, u32[]{:S(2)}) collective-permute-start(bf16[64,512]{1,0:T(8,128)(2,1)S(1)} %collective-permute-done.27.refs_1_), channel_id=1, source_target_pairs={{0,1},{1,0},{2,3},{3,2},{4,5},{5,4},{6,7},{7,6},{8,9},{9,8},{10,11... | collective-permute-start | bytes 196616 | tf_op jit(solution)/shard_map/ppermute | solution.py:195
  42.3 0.7 %collective-permute-start.30 = (bf16[64,512]{1,0:T(8,128)(2,1)S(1)}, bf16[64,512]{1,0:T(8,128)(2,1)S(1)}, u32[]{:S(2)}, u32[]{:S(2)}) collective-permute-start(bf16[64,512]{1,0:T(8,128)(2,1)S(1)} %collective-permute-done.29.refs_1_), channel_id=1, source_target_pairs={{0,1},{1,0},{2,3},{3,2},{4,5},{5,4},{6,7},{7,6},{8,9},{9,8},{10,11... | collective-permute-start | bytes 196616 | tf_op jit(solution)/shard_map/ppermute | solution.py:195
  44.2 0.6 %copy.15 = bf16[1,512,64]{1,2,0:T(8,128)(2,1)} copy(bf16[1,512,64]{1,2,0:T(8,128)(2,1)S(1)} %bitcast.7) | data formatting | bytes 131072
  (66 shorter events, 7.7 us)
Async XLA Ops:
  0.0 3.2 %collective-permute-start = (bf16[64,512]{1,0:T(8,128)(2,1)}, bf16[64,512]{1,0:T(8,128)(2,1)S(1)}, u32[]{:S(2)}, u32[]{:S(2)}) collective-permute-start(bf16[64,512]{1,0:T(8,128)(2,1)} %bitcast.8), channel_id=1, source_target_pairs={{0,4},{1,5},{2,6},{3,7},{4,0},{5,1},{6,2},{7,3},{8,9},{9,8},{10,11... | collective-permute-start | bytes 196616 | tf_op jit(solution)/shard_map/ppermute | solution.py:208
  0.7 3.1 %collective-permute-start.3 = (bf16[64,512]{1,0:T(8,128)(2,1)}, bf16[64,512]{1,0:T(8,128)(2,1)S(1)}, u32[]{:S(2)}, u32[]{:S(2)}) collective-permute-start(bf16[64,512]{1,0:T(8,128)(2,1)} %bitcast.9), channel_id=1, source_target_pairs={{0,2},{1,3},{2,0},{3,1},{4,6},{5,7},{6,4},{7,5},{8,9},{9,8},{10,11... | collective-permute-start | bytes 196616 | tf_op jit(solution)/shard_map/ppermute | solution.py:208
  0.7 3.1 %collective-permute-start.5 = (bf16[64,512]{1,0:T(8,128)(2,1)}, bf16[64,512]{1,0:T(8,128)(2,1)S(1)}, u32[]{:S(2)}, u32[]{:S(2)}) collective-permute-start(bf16[64,512]{1,0:T(8,128)(2,1)} %bitcast.10), channel_id=1, source_target_pairs={{0,6},{1,7},{2,4},{3,5},{4,2},{5,3},{6,0},{7,1},{8,9},{9,8},{10,11... | collective-permute-start | bytes 196616 | tf_op jit(solution)/shard_map/ppermute | solution.py:208
  3.2 1.3 %collective-permute-start.1 = (bf16[64,512]{1,0:T(8,128)(2,1)S(1)}, bf16[64,512]{1,0:T(8,128)(2,1)S(1)}, u32[]{:S(2)}, u32[]{:S(2)}) collective-permute-start(bf16[64,512]{1,0:T(8,128)(2,1)S(1)} %bitcast.11), channel_id=1, source_target_pairs={{0,1},{1,0},{2,3},{3,2},{4,5},{5,4},{6,7},{7,6},{8,9},{9,8},{10,11... | collective-permute-start | bytes 196616 | tf_op jit(solution)/shard_map/ppermute | solution.py:195
  3.3 1.4 %collective-permute-start.2 = (bf16[64,512]{1,0:T(8,128)(2,1)S(1)}, bf16[64,512]{1,0:T(8,128)(2,1)S(1)}, u32[]{:S(2)}, u32[]{:S(2)}) collective-permute-start(bf16[64,512]{1,0:T(8,128)(2,1)S(1)} %collective-permute-done.refs_2_), channel_id=1, source_target_pairs={{0,1},{1,0},{2,3},{3,2},{4,5},{5,4},{6,7},{7,6},{8,9},{9,8},{10,11... | collective-permute-start | bytes 196616 | tf_op jit(solution)/shard_map/ppermute | solution.py:195
  3.8 1.3 %collective-permute-start.6 = (bf16[64,512]{1,0:T(8,128)(2,1)S(1)}, bf16[64,512]{1,0:T(8,128)(2,1)S(1)}, u32[]{:S(2)}, u32[]{:S(2)}) collective-permute-start(bf16[64,512]{1,0:T(8,128)(2,1)S(1)} %collective-permute-done.5.refs_1_), channel_id=1, source_target_pairs={{0,1},{1,0},{2,3},{3,2},{4,5},{5,4},{6,7},{7,6},{8,9},{9,8},{10,11... | collective-permute-start | bytes 196616 | tf_op jit(solution)/shard_map/ppermute | solution.py:195
  5.2 10.9 %collective-permute-start.7 = (bf16[64,512]{1,0:T(8,128)(2,1)S(1)}, bf16[64,512]{1,0:T(8,128)(2,1)S(1)}, u32[]{:S(2)}, u32[]{:S(2)}) collective-permute-start(bf16[64,512]{1,0:T(8,128)(2,1)S(1)} %late_tile.4.refs_0_), channel_id=1, source_target_pairs={{0,12},{1,13},{2,14},{3,15},{4,8},{5,9},{6,10},{7,11},{8,24},{9,25... | collective-permute-start | bytes 196616 | tf_op jit(solution)/shard_map/ppermute | solution.py:208
  13.4 3.0 %collective-permute-start.9 = (bf16[64,512]{1,0:T(8,128)(2,1)S(1)}, bf16[64,512]{1,0:T(8,128)(2,1)S(1)}, u32[]{:S(2)}, u32[]{:S(2)}) collective-permute-start(bf16[64,512]{1,0:T(8,128)(2,1)S(1)} %late_tile.4.refs_0_), channel_id=1, source_target_pairs={{0,10},{1,11},{2,8},{3,9},{4,14},{5,15},{6,12},{7,13}} | collective-permute-start | bytes 196616 | tf_op jit(solution)/shard_map/ppermute | solution.py:208
  14.1 2.6 %collective-permute-start.11 = (bf16[64,512]{1,0:T(8,128)(2,1)S(1)}, bf16[64,512]{1,0:T(8,128)(2,1)S(1)}, u32[]{:S(2)}, u32[]{:S(2)}) collective-permute-start(bf16[64,512]{1,0:T(8,128)(2,1)S(1)} %late_tile.4.refs_0_), channel_id=1, source_target_pairs={{0,14},{1,15},{2,12},{3,13},{4,10},{5,11},{6,8},{7,9}} | collective-permute-start | bytes 196616 | tf_op jit(solution)/shard_map/ppermute | solution.py:208
  14.7 2.2 %collective-permute-start.13 = (bf16[64,512]{1,0:T(8,128)(2,1)S(1)}, bf16[64,512]{1,0:T(8,128)(2,1)S(1)}, u32[]{:S(2)}, u32[]{:S(2)}) collective-permute-start(bf16[64,512]{1,0:T(8,128)(2,1)S(1)} %late_tile.4.refs_0_), channel_id=1, source_target_pairs={{0,8},{1,9},{2,10},{3,11},{4,12},{5,13},{6,14},{7,15}} | collective-permute-start | bytes 196616 | tf_op jit(solution)/shard_map/ppermute | solution.py:208
  18.2 7.8 %collective-permute-start.15 = (bf16[64,512]{1,0:T(8,128)(2,1)S(1)}, bf16[64,512]{1,0:T(8,128)(2,1)S(1)}, u32[]{:S(2)}, u32[]{:S(2)}) collective-permute-start(bf16[64,512]{1,0:T(8,128)(2,1)S(1)} %late_tile.5.refs_0_), channel_id=1, source_target_pairs={{8,20},{9,21},{10,22},{11,23},{12,16},{13,17},{14,18},{15,19},{16,... | collective-permute-start | bytes 196616 | tf_op jit(solution)/shard_map/ppermute | solution.py:208
  23.4 3.2 %collective-permute-start.17 = (bf16[64,512]{1,0:T(8,128)(2,1)S(1)}, bf16[64,512]{1,0:T(8,128)(2,1)S(1)}, u32[]{:S(2)}, u32[]{:S(2)}) collective-permute-start(bf16[64,512]{1,0:T(8,128)(2,1)S(1)} %late_tile.5.refs_0_), channel_id=1, source_target_pairs={{8,18},{9,19},{10,16},{11,17},{12,22},{13,23},{14,20},{15,21}} | collective-permute-start | bytes 196616 | tf_op jit(solution)/shard_map/ppermute | solution.py:208
  24.0 2.6 %collective-permute-start.19 = (bf16[64,512]{1,0:T(8,128)(2,1)S(1)}, bf16[64,512]{1,0:T(8,128)(2,1)S(1)}, u32[]{:S(2)}, u32[]{:S(2)}) collective-permute-start(bf16[64,512]{1,0:T(8,128)(2,1)S(1)} %late_tile.5.refs_0_), channel_id=1, source_target_pairs={{8,22},{9,23},{10,20},{11,21},{12,18},{13,19},{14,16},{15,17}} | collective-permute-start | bytes 196616 | tf_op jit(solution)/shard_map/ppermute | solution.py:208
  24.7 2.4 %collective-permute-start.21 = (bf16[64,512]{1,0:T(8,128)(2,1)S(1)}, bf16[64,512]{1,0:T(8,128)(2,1)S(1)}, u32[]{:S(2)}, u32[]{:S(2)}) collective-permute-start(bf16[64,512]{1,0:T(8,128)(2,1)S(1)} %late_tile.5.refs_0_), channel_id=1, source_target_pairs={{8,16},{9,17},{10,18},{11,19},{12,20},{13,21},{14,22},{15,23}} | collective-permute-start | bytes 196616 | tf_op jit(solution)/shard_map/ppermute | solution.py:208
  26.1 1.4 %collective-permute-start.16 = (bf16[64,512]{1,0:T(8,128)(2,1)S(1)}, bf16[64,512]{1,0:T(8,128)(2,1)S(1)}, u32[]{:S(2)}, u32[]{:S(2)}) collective-permute-start(bf16[64,512]{1,0:T(8,128)(2,1)S(1)} %collective-permute-done.15.refs_0_), channel_id=1, source_target_pairs={{0,1},{1,0},{2,3},{3,2},{4,5},{5,4},{6,7},{7,6},{8,9},{9,8},{10,11... | collective-permute-start | bytes 196616 | tf_op jit(solution)/shard_map/ppermute | solution.py:195
  26.7 1.3 %collective-permute-start.20 = (bf16[64,512]{1,0:T(8,128)(2,1)S(1)}, bf16[64,512]{1,0:T(8,128)(2,1)S(1)}, u32[]{:S(2)}, u32[]{:S(2)}) collective-permute-start(bf16[64,512]{1,0:T(8,128)(2,1)S(1)} %collective-permute-done.19.refs_1_), channel_id=1, source_target_pairs={{0,1},{1,0},{2,3},{3,2},{4,5},{5,4},{6,7},{7,6},{8,9},{9,8},{10,11... | collective-permute-start | bytes 196616 | tf_op jit(solution)/shard_map/ppermute | solution.py:195
  28.4 10.5 %collective-permute-start.23 = (bf16[64,512]{1,0:T(8,128)(2,1)S(1)}, bf16[64,512]{1,0:T(8,128)(2,1)S(1)}, u32[]{:S(2)}, u32[]{:S(2)}) collective-permute-start(bf16[64,512]{1,0:T(8,128)(2,1)S(1)} %late_tile.6.refs_0_), channel_id=1, source_target_pairs={{16,28},{17,29},{18,30},{19,31},{20,24},{21,25},{22,26},{23,27},{2... | collective-permute-start | bytes 196616 | tf_op jit(solution)/shard_map/ppermute | solution.py:208
  28.4 11.5 %collective-permute-start.25 = (bf16[64,512]{1,0:T(8,128)(2,1)S(1)}, bf16[64,512]{1,0:T(8,128)(2,1)S(1)}, u32[]{:S(2)}, u32[]{:S(2)}) collective-permute-start(bf16[64,512]{1,0:T(8,128)(2,1)S(1)} %late_tile.6.refs_0_), channel_id=1, source_target_pairs={{16,26},{17,27},{18,24},{19,25},{20,30},{21,31},{22,28},{23,29}} | collective-permute-start | bytes 196616 | tf_op jit(solution)/shard_map/ppermute | solution.py:208
  29.6 11.9 %collective-permute-start.27 = (bf16[64,512]{1,0:T(8,128)(2,1)S(1)}, bf16[64,512]{1,0:T(8,128)(2,1)S(1)}, u32[]{:S(2)}, u32[]{:S(2)}) collective-permute-start(bf16[64,512]{1,0:T(8,128)(2,1)S(1)} %late_tile.6.refs_0_), channel_id=1, source_target_pairs={{16,30},{17,31},{18,28},{19,29},{20,26},{21,27},{22,24},{23,25}} | collective-permute-start | bytes 196616 | tf_op jit(solution)/shard_map/ppermute | solution.py:208
  30.9 11.3 %collective-permute-start.29 = (bf16[64,512]{1,0:T(8,128)(2,1)S(1)}, bf16[64,512]{1,0:T(8,128)(2,1)S(1)}, u32[]{:S(2)}, u32[]{:S(2)}) collective-permute-start(bf16[64,512]{1,0:T(8,128)(2,1)S(1)} %late_tile.6.refs_0_), channel_id=1, source_target_pairs={{16,24},{17,25},{18,26},{19,27},{20,28},{21,29},{22,30},{23,31}} | collective-permute-start | bytes 196616 | tf_op jit(solution)/shard_map/ppermute | solution.py:208
  38.8 4.1 %collective-permute-start.24 = (bf16[64,512]{1,0:T(8,128)(2,1)S(1)}, bf16[64,512]{1,0:T(8,128)(2,1)S(1)}, u32[]{:S(2)}, u32[]{:S(2)}) collective-permute-start(bf16[64,512]{1,0:T(8,128)(2,1)S(1)} %collective-permute-done.23.refs_0_), channel_id=1, source_target_pairs={{0,1},{1,0},{2,3},{3,2},{4,5},{5,4},{6,7},{7,6},{8,9},{9,8},{10,11... | collective-permute-start | bytes 196616 | tf_op jit(solution)/shard_map/ppermute | solution.py:195
  39.9 3.5 %collective-permute-start.26 = (bf16[64,512]{1,0:T(8,128)(2,1)S(1)}, bf16[64,512]{1,0:T(8,128)(2,1)S(1)}, u32[]{:S(2)}, u32[]{:S(2)}) collective-permute-start(bf16[64,512]{1,0:T(8,128)(2,1)S(1)} %collective-permute-done.25.refs_2_), channel_id=1, source_target_pairs={{0,1},{1,0},{2,3},{3,2},{4,5},{5,4},{6,7},{7,6},{8,9},{9,8},{10,11... | collective-permute-start | bytes 196616 | tf_op jit(solution)/shard_map/ppermute | solution.py:195
  41.6 2.1 %collective-permute-start.28 = (bf16[64,512]{1,0:T(8,128)(2,1)S(1)}, bf16[64,512]{1,0:T(8,128)(2,1)S(1)}, u32[]{:S(2)}, u32[]{:S(2)}) collective-permute-start(bf16[64,512]{1,0:T(8,128)(2,1)S(1)} %collective-permute-done.27.refs_1_), channel_id=1, source_target_pairs={{0,1},{1,0},{2,3},{3,2},{4,5},{5,4},{6,7},{7,6},{8,9},{9,8},{10,11... | collective-permute-start | bytes 196616 | tf_op jit(solution)/shard_map/ppermute | solution.py:195
  42.3 1.7 %collective-permute-start.30 = (bf16[64,512]{1,0:T(8,128)(2,1)S(1)}, bf16[64,512]{1,0:T(8,128)(2,1)S(1)}, u32[]{:S(2)}, u32[]{:S(2)}) collective-permute-start(bf16[64,512]{1,0:T(8,128)(2,1)S(1)} %collective-permute-done.29.refs_1_), channel_id=1, source_target_pairs={{0,1},{1,0},{2,3},{3,2},{4,5},{5,4},{6,7},{7,6},{8,9},{9,8},{10,11... | collective-permute-start | bytes 196616 | tf_op jit(solution)/shard_map/ppermute | solution.py:195
  (10 other events, 20.4 us)

commit v5 on v4

--- a/solution.py
+++ b/solution.py
@@ -107,12 +107,17 @@
         for copy in early_copies:
             copy.wait()
         base_ref[...] = lax.dot_general(source_ref[...], solve_ref[...], LAST_LAST, preferred_element_type=jnp.float32)
-        for slot, copy in enumerate(copies):
-            position = position_of(slot, chips, cols_ref)
+        for copy in copies:
             copy.wait()
+
+        def fold_slot(slot, carry):
             solved = lax.dot_general(held_ref[slot], solve_ref[...], FIRST_LAST, preferred_element_type=jnp.float32)
             used = slot < count_ref[0, 0]
-            folded_ref[position] = jnp.where(used, solved, jnp.zeros_like(solved)).astype(folded_ref.dtype)
+            solved = jnp.where(used, solved, jnp.zeros_like(solved)).astype(folded_ref.dtype)
+            folded_ref[position_of(slot, chips, cols_ref)] = solved
+            return carry
+
+        lax.fori_loop(0, slots, fold_slot, 0)
 
 
 def fold(section, chips, cols, count, greens, solve, source):
@@ -195,47 +200,56 @@
     return lax.ppermute(tile, "row", [(r, r ^ 1) for r in range(rows)])
 
 
-def sent(tile, source, target, step, slabs, rows, via=None):
-    pairs = [(source * rows + r, target * rows + (r ^ (step * CORES))) for r in range(rows)]
-    busy = {source, target}
-    if source != target and via is not None:
-        pairs += [(target * rows + r, via * rows + (r if via != source else r ^ (step * CORES))) for r in range(rows)]
-    if via not in (None, source):
-        pairs += [(via * rows + r, source * rows + r) for r in range(rows)]
+def sent(tile, source, target, step, slabs, rows, via):
+    partner = [r ^ (step * CORES) for r in range(rows)]
+    pairs = [(source * rows + r, target * rows + partner[r]) for r in range(rows)]
     if via is not None:
-        busy.add(via)
-        pairs += [(s * rows + r, s * rows + (r ^ 1)) for s in range(slabs) if s not in busy for r in range(rows)]
+        path = [target, *via, source] if source != target else [source]
+        for here, there in zip(path, path[1:]):
+            pairs += [(here * rows + r, there * rows + (r if via else partner[r])) for r in range(rows)]
+        pairs += [(s * rows + r, s * rows + (r ^ 1)) for s in range(slabs) if s not in path for r in range(rows)]
     return lax.ppermute(tile, ("slab", "row"), pairs)
 
 
-def third_slabs(section, slabs, chips):
-    free = [s % slabs for s in range(section + 1, section + slabs - 1)]
-    free = [s for s in free if s != section - 2][-1:]
-    return (free + [None] * chips)[:chips]
+def ways(section, slabs, chips):
+    others = [s % slabs for s in range(section + 1, section + slabs - 1)]
+    if len(others) < 2 or chips < 4:
+        return [None] * chips
+    free, late = others[0], others[-1]
+    if section == 1:
+        return [(free,), None, None, None] + [None] * (chips - 4)
+    if section < slabs - 1:
+        return [(free,), None, None, None] + [None] * (chips - 4)
+    return [(free,), None, (late, free), ()][:1] + [None] * (chips - 4) + [(free,), None, (late, free), ()][1:]
 
 
 def direct(forcing, inflow, self_solve, greens, kept_cols, counts):
     slabs, rows = lax.axis_size("slab"), lax.axis_size("row")
-    chips = rows // CORES
+    chips, last = rows // CORES, slabs - 1
     steps = [step_of(order, chips) for order in range(chips)]
     entering, source = inflow.T, forcing[0].T
     greens, self_solve, source = (
         pltpu.with_memory_space_constraint(array, pltpu.HBM) for array in (greens, self_solve, source)
     )
-    placed, solve, base = place(chips, kept_cols, counts, greens, self_solve, source)
+    given = (chips, kept_cols, counts, greens, self_solve, source)
+    placed, solve, base = place(*given)
+    ready = fold(last, *given) if last > 0 else ()
     trace = jnp.zeros(entering.shape, jnp.bfloat16)
     for section in range(slabs):
         if section == 0:
-            own = [sent(entering, 0, 0, step, slabs, rows, 0) for step in steps if step]
-            entering, placed, base, solve, own[0] = lax.optimization_barrier((entering, placed, base, solve, own[0]))
+            own = [sent(entering, 0, 0, step, slabs, rows, ()) for step in steps if step]
+            placed, base, solve, *ready, own[0] = lax.optimization_barrier((placed, base, solve, *ready, own[0]))
             orders = [steps.index(0)] + [order for order, step in enumerate(steps) if step]
             own = [entering] + own
         else:
-            vias = third_slabs(section, slabs, chips)
+            vias = ways(section, slabs, chips)
             own = [sent(trace, section - 1, section, step, slabs, rows, via) for step, via in zip(steps, vias)]
             orders = list(range(chips))
-            placed, base = fold(section, chips, kept_cols, counts, greens, self_solve, source)
-            placed, base, own[0] = lax.optimization_barrier((placed, base, own[0]))
+            if section < last:
+                placed, base = fold(section, *given)
+                placed, base, own[0] = lax.optimization_barrier((placed, base, own[0]))
+            else:
+                placed, base = ready
         other = [swapped(tile, rows) for tile in own]
         arriving = []
         for order, *both in zip(orders, own, other):

time: 44.9 us -> 44.6 us (level)
  starting transfers between devices: 28.2 us -> 24.8 us
  waiting for transfers between devices: 5.36 us -> 7.35 us
  Pallas kernels: 9.14 us -> 9.94 us
    ppermute x15, starting transfers between devices: 22.4 us -> 19.3 us  [sent(): return lax.ppermute(tile, ('slab', 'row'), pairs)]
    ppermute x15, waiting for transfers between devices: 2.26 us -> 4.38 us  [sent(): return lax.ppermute(tile, ('slab', 'row'), pairs)]
    pallas_call x3, Pallas kernels: 7.28 us -> 8.07 us  [fold(): pl.pallas_call(functools.partial(fold_kernel, section, chips), out_shape=...]
  transfers between devices with their start and end apart: 31 -> 31, of which waited for: 14 -> 13; matrix products, arithmetic and copies ran while one was open for 0% -> 0% of each run, Pallas kernels for 20% -> 22%
where the time goes in v5:
time: 44.6 us; the launch traced here: 44.3 us
  starting transfers between devices  24.8 us (56%)
  Pallas kernels  9.94 us (22%)
  waiting for transfers between devices  7.35 us (16%)
  local copies, waits for them, and re-layouts  1.3 us (3%)
  between operations  0.88 us (2%)
    ppermute x15, starting transfers between devices, sent(): return lax.ppermute(tile, ('slab', 'row'), pairs)  19.3 us
    pallas_call x3, Pallas kernels, fold(): pl.pallas_call(functools.partial(fold_kernel, section, chips), out_shape=...  8.07 us
    ppermute x16, starting transfers between devices, swapped(): return lax.ppermute(tile, 'row', [(r, r ^ 1) for r in range(rows)])  5.56 us
    ppermute x15, waiting for transfers between devices, sent(): return lax.ppermute(tile, ('slab', 'row'), pairs)  4.38 us
    ppermute x16, waiting for transfers between devices, swapped(): return lax.ppermute(tile, 'row', [(r, r ^ 1) for r in range(rows)])  2.96 us
    unnamed x7, local copies, waits for them, and re-layouts  1.29 us
    pallas_call x12, Pallas kernels, early(): pl.pallas_call(functools.partial(early_kernel, section, positions), out_s...  1 us
  transfers between devices with their start and end apart: 31, of which 13 were waited for; matrix products, arithmetic and copies ran while one was open for 0% of the time, Pallas kernels for 22%

profile of v5, /device:TPU:7, one launch (start us, length us, event | category | flops | bytes accessed | tf_op | source)
XLA Modules:
  0.0 44.3 jit_solution(8804085618809930216)
XLA Ops:
  0.0 0.7 %collective-permute-start = (bf16[64,512]{1,0:T(8,128)(2,1)}, bf16[64,512]{1,0:T(8,128)(2,1)S(1)}, u32[]{:S(2)}, u32[]{:S(2)}) collective-permute-start(bf16[64,512]{1,0:T(8,128)(2,1)} %bitcast.8), channel_id=1, source_target_pairs={{0,4},{1,5},{2,6},{3,7},{4,0},{5,1},{6,2},{7,3},{8,9},{9,8},{10,11... | collective-permute-start | bytes 196616 | tf_op jit(solution)/shard_map/ppermute | solution.py:211
  0.7 0.5 %collective-permute-start.3 = (bf16[64,512]{1,0:T(8,128)(2,1)}, bf16[64,512]{1,0:T(8,128)(2,1)S(1)}, u32[]{:S(2)}, u32[]{:S(2)}) collective-permute-start(bf16[64,512]{1,0:T(8,128)(2,1)} %bitcast.10), channel_id=1, source_target_pairs={{0,2},{1,3},{2,0},{3,1},{4,6},{5,7},{6,4},{7,5},{8,9},{9,8},{10,11... | collective-permute-start | bytes 196616 | tf_op jit(solution)/shard_map/ppermute | solution.py:211
  1.9 0.6 %copy-done.1 = s32[1,1,8]{2,1,0:T(1,128)S(1)} copy-done((s32[1,1,8]{2,1,0:T(1,128)S(1)}, s32[1,1,8]{2,1,0:T(1,128)}, u32[]{:S(2)}) %copy-start.1) | copy-done | bytes 56
  2.5 6.8 %fold.3 = (bf16[8,512,512]{2,1,0:T(8,128)(2,1)S(1)}, f32[64,512]{1,0:T(8,128)S(1)}) custom-call(s32[1,1,8]{2,1,0:T(1,128)S(1)} %copy-done.1, s32[1,1]{1,0:T(1,128)S(6)} %copy.16.count_ref, bf16[1,1,8,512,512]{4,3,2,1,0:T(8,128)(2,1)} %greens_ref.7, bf16[1,1,512,512]{3,2,1,0:T(8,128)(2,1)} %solve_in.7, bf16[64,512]{1,0:T(8,128)(2,1)} %bitcast.13), custom_call_target="tpu_custom_call" | custom-call | flops 2147483648 | bytes 8388608 | tf_op jit(solution)/shard_map/fold/pallas_call | solution.py:125
  9.3 0.7 %place.1 = (bf16[8,512,512]{2,1,0:T(8,128)(2,1)S(1)}, bf16[512,512]{1,0:T(8,128)(2,1)S(1)}, bf16[64,512]{1,0:T(8,128)(2,1)S(1)}) custom-call(s32[1,1,8]{2,1,0:T(1,128)S(1)} %copy-done.1, s32[1,1]{1,0:T(1,128)S(6)} %copy.16.count_ref, bf16[1,1,8,512,512]{4,3,2,1,0:T(8,128)(2,1)} %greens_ref.7, bf16[1,1,512,512]{3,2,1,0:T(8,128)(2,1)} %solve_in.7, ...), custom_call_target="tpu_custom_call" | custom-call | bytes 8388608 | tf_op jit(solution)/shard_map/place/pallas_call | solution.py:75
  10.0 0.6 %collective-permute-start.2 = (bf16[64,512]{1,0:T(8,128)(2,1)S(1)}, bf16[64,512]{1,0:T(8,128)(2,1)S(1)}, u32[]{:S(2)}, u32[]{:S(2)}) collective-permute-start(bf16[64,512]{1,0:T(8,128)(2,1)S(1)} %collective-permute-done.refs_2_), channel_id=1, source_target_pairs={{0,1},{1,0},{2,3},{3,2},{4,5},{5,4},{6,7},{7,6},{8,9},{9,8},{10,11... | collective-permute-start | bytes 196616 | tf_op jit(solution)/shard_map/ppermute | solution.py:200
  12.4 0.7 %collective-permute-start.9 = (bf16[64,512]{1,0:T(8,128)(2,1)S(1)}, bf16[64,512]{1,0:T(8,128)(2,1)S(1)}, u32[]{:S(2)}, u32[]{:S(2)}) collective-permute-start(bf16[64,512]{1,0:T(8,128)(2,1)S(1)} %late_tile.4.refs_0_), channel_id=1, source_target_pairs={{0,10},{1,11},{2,8},{3,9},{4,14},{5,15},{6,12},{7,13}} | collective-permute-start | bytes 196616 | tf_op jit(solution)/shard_map/ppermute | solution.py:211
  13.0 0.7 %collective-permute-start.11 = (bf16[64,512]{1,0:T(8,128)(2,1)S(1)}, bf16[64,512]{1,0:T(8,128)(2,1)S(1)}, u32[]{:S(2)}, u32[]{:S(2)}) collective-permute-start(bf16[64,512]{1,0:T(8,128)(2,1)S(1)} %late_tile.4.refs_0_), channel_id=1, source_target_pairs={{0,14},{1,15},{2,12},{3,13},{4,10},{5,11},{6,8},{7,9}} | collective-permute-start | bytes 196616 | tf_op jit(solution)/shard_map/ppermute | solution.py:211
  13.7 0.7 %collective-permute-start.13 = (bf16[64,512]{1,0:T(8,128)(2,1)S(1)}, bf16[64,512]{1,0:T(8,128)(2,1)S(1)}, u32[]{:S(2)}, u32[]{:S(2)}) collective-permute-start(bf16[64,512]{1,0:T(8,128)(2,1)S(1)} %late_tile.4.refs_0_), channel_id=1, source_target_pairs={{0,8},{1,9},{2,10},{3,11},{4,12},{5,13},{6,14},{7,15}} | collective-permute-start | bytes 196616 | tf_op jit(solution)/shard_map/ppermute | solution.py:211
  14.4 0.7 %fold.5 = (bf16[8,512,512]{2,1,0:T(8,128)(2,1)S(1)}, f32[64,512]{1,0:T(8,128)S(1)}) custom-call(s32[1,1,8]{2,1,0:T(1,128)S(1)} %copy-done.2, s32[1,1]{1,0:T(1,128)S(6)} %copy.16.count_ref, bf16[1,1,8,512,512]{4,3,2,1,0:T(8,128)(2,1)} %greens_ref.7, bf16[1,1,512,512]{3,2,1,0:T(8,128)(2,1)} %solve_in.7, bf16[64,512]{1,0:T(8,128)(2,1)} %bitcast.15), custom_call_target="tpu_custom_call" | custom-call | flops 2147483648 | bytes 8388608 | tf_op jit(solution)/shard_map/fold/pallas_call | solution.py:125
  17.1 6.3 %collective-permute-start.15 = (bf16[64,512]{1,0:T(8,128)(2,1)S(1)}, bf16[64,512]{1,0:T(8,128)(2,1)S(1)}, u32[]{:S(2)}, u32[]{:S(2)}) collective-permute-start(bf16[64,512]{1,0:T(8,128)(2,1)S(1)} %late_tile.5.refs_0_), channel_id=1, source_target_pairs={{8,20},{9,21},{10,22},{11,23},{12,16},{13,17},{14,18},{15,19},{16,... | collective-permute-start | bytes 196616 | tf_op jit(solution)/shard_map/ppermute | solution.py:211
  23.4 0.7 %collective-permute-start.17 = (bf16[64,512]{1,0:T(8,128)(2,1)S(1)}, bf16[64,512]{1,0:T(8,128)(2,1)S(1)}, u32[]{:S(2)}, u32[]{:S(2)}) collective-permute-start(bf16[64,512]{1,0:T(8,128)(2,1)S(1)} %late_tile.5.refs_0_), channel_id=1, source_target_pairs={{8,18},{9,19},{10,16},{11,17},{12,22},{13,23},{14,20},{15,21}} | collective-permute-start | bytes 196616 | tf_op jit(solution)/shard_map/ppermute | solution.py:211
  24.0 0.7 %collective-permute-start.19 = (bf16[64,512]{1,0:T(8,128)(2,1)S(1)}, bf16[64,512]{1,0:T(8,128)(2,1)S(1)}, u32[]{:S(2)}, u32[]{:S(2)}) collective-permute-start(bf16[64,512]{1,0:T(8,128)(2,1)S(1)} %late_tile.5.refs_0_), channel_id=1, source_target_pairs={{8,22},{9,23},{10,20},{11,21},{12,18},{13,19},{14,16},{15,17}} | collective-permute-start | bytes 196616 | tf_op jit(solution)/shard_map/ppermute | solution.py:211
  24.7 0.7 %collective-permute-start.21 = (bf16[64,512]{1,0:T(8,128)(2,1)S(1)}, bf16[64,512]{1,0:T(8,128)(2,1)S(1)}, u32[]{:S(2)}, u32[]{:S(2)}) collective-permute-start(bf16[64,512]{1,0:T(8,128)(2,1)S(1)} %late_tile.5.refs_0_), channel_id=1, source_target_pairs={{8,16},{9,17},{10,18},{11,19},{12,20},{13,21},{14,22},{15,23}} | collective-permute-start | bytes 196616 | tf_op jit(solution)/shard_map/ppermute | solution.py:211
  25.4 0.7 %fold.4 = (bf16[8,512,512]{2,1,0:T(8,128)(2,1)S(1)}, f32[64,512]{1,0:T(8,128)S(1)}) custom-call(s32[1,1,8]{2,1,0:T(1,128)S(1)} %copy-done.2, s32[1,1]{1,0:T(1,128)S(6)} %copy.16.count_ref, bf16[1,1,8,512,512]{4,3,2,1,0:T(8,128)(2,1)} %greens_ref.7, bf16[1,1,512,512]{3,2,1,0:T(8,128)(2,1)} %solve_in.7, bf16[64,512]{1,0:T(8,128)(2,1)} %bitcast.16), custom_call_target="tpu_custom_call" | custom-call | flops 2147483648 | bytes 8388608 | tf_op jit(solution)/shard_map/fold/pallas_call | solution.py:125
  26.0 0.5 %collective-permute-start.16 = (bf16[64,512]{1,0:T(8,128)(2,1)S(1)}, bf16[64,512]{1,0:T(8,128)(2,1)S(1)}, u32[]{:S(2)}, u32[]{:S(2)}) collective-permute-start(bf16[64,512]{1,0:T(8,128)(2,1)S(1)} %collective-permute-done.15.refs_0_), channel_id=1, source_target_pairs={{0,1},{1,0},{2,3},{3,2},{4,5},{5,4},{6,7},{7,6},{8,9},{9,8},{10,11... | collective-permute-start | bytes 196616 | tf_op jit(solution)/shard_map/ppermute | solution.py:200
  28.4 1.3 %collective-permute-start.25 = (bf16[64,512]{1,0:T(8,128)(2,1)S(1)}, bf16[64,512]{1,0:T(8,128)(2,1)S(1)}, u32[]{:S(2)}, u32[]{:S(2)}) collective-permute-start(bf16[64,512]{1,0:T(8,128)(2,1)S(1)} %late_tile.6.refs_0_), channel_id=1, source_target_pairs={{16,26},{17,27},{18,24},{19,25},{20,30},{21,31},{22,28},{23,29}} | collective-permute-start | bytes 196616 | tf_op jit(solution)/shard_map/ppermute | solution.py:211
  29.6 3.4 %collective-permute-start.27 = (bf16[64,512]{1,0:T(8,128)(2,1)S(1)}, bf16[64,512]{1,0:T(8,128)(2,1)S(1)}, u32[]{:S(2)}, u32[]{:S(2)}) collective-permute-start(bf16[64,512]{1,0:T(8,128)(2,1)S(1)} %late_tile.6.refs_0_), channel_id=1, source_target_pairs={{16,30},{17,31},{18,28},{19,29},{20,26},{21,27},{22,24},{23,25},{2... | collective-permute-start | bytes 196616 | tf_op jit(solution)/shard_map/ppermute | solution.py:211
  33.1 2.7 %collective-permute-start.29 = (bf16[64,512]{1,0:T(8,128)(2,1)S(1)}, bf16[64,512]{1,0:T(8,128)(2,1)S(1)}, u32[]{:S(2)}, u32[]{:S(2)}) collective-permute-start(bf16[64,512]{1,0:T(8,128)(2,1)S(1)} %late_tile.6.refs_0_), channel_id=1, source_target_pairs={{16,24},{17,25},{18,26},{19,27},{20,28},{21,29},{22,30},{23,31},{2... | collective-permute-start | bytes 196616 | tf_op jit(solution)/shard_map/ppermute | solution.py:211
  35.8 2.9 %collective-permute-done.23.refs_0_ = bf16[64,512]{1,0:T(8,128)(2,1)S(1)} collective-permute-done((bf16[64,512]{1,0:T(8,128)(2,1)S(1)}, bf16[64,512]{1,0:T(8,128)(2,1)S(1)}, u32[]{:S(2)}, u32[]{:S(2)}) %collective-permute-start.23) | collective-permute-done | bytes 65568 | tf_op jit(solution)/shard_map/ppermute | solution.py:211
  38.6 1.3 %collective-permute-start.24 = (bf16[64,512]{1,0:T(8,128)(2,1)S(1)}, bf16[64,512]{1,0:T(8,128)(2,1)S(1)}, u32[]{:S(2)}, u32[]{:S(2)}) collective-permute-start(bf16[64,512]{1,0:T(8,128)(2,1)S(1)} %collective-permute-done.23.refs_0_), channel_id=1, source_target_pairs={{0,1},{1,0},{2,3},{3,2},{4,5},{5,4},{6,7},{7,6},{8,9},{9,8},{10,11... | collective-permute-start | bytes 196616 | tf_op jit(solution)/shard_map/ppermute | solution.py:200
  40.0 1.5 %collective-permute-done.27.refs_1_ = bf16[64,512]{1,0:T(8,128)(2,1)S(1)} collective-permute-done((bf16[64,512]{1,0:T(8,128)(2,1)S(1)}, bf16[64,512]{1,0:T(8,128)(2,1)S(1)}, u32[]{:S(2)}, u32[]{:S(2)}) %collective-permute-start.27) | collective-permute-done | bytes 65568 | tf_op jit(solution)/shard_map/ppermute | solution.py:211
  41.5 0.7 %collective-permute-start.28 = (bf16[64,512]{1,0:T(8,128)(2,1)S(1)}, bf16[64,512]{1,0:T(8,128)(2,1)S(1)}, u32[]{:S(2)}, u32[]{:S(2)}) collective-permute-start(bf16[64,512]{1,0:T(8,128)(2,1)S(1)} %collective-permute-done.27.refs_1_), channel_id=1, source_target_pairs={{0,1},{1,0},{2,3},{3,2},{4,5},{5,4},{6,7},{7,6},{8,9},{9,8},{10,11... | collective-permute-start | bytes 196616 | tf_op jit(solution)/shard_map/ppermute | solution.py:200
  43.6 0.6 %copy.15 = bf16[1,512,64]{1,2,0:T(8,128)(2,1)} copy(bf16[1,512,64]{1,2,0:T(8,128)(2,1)S(1)} %bitcast.7) | data formatting | bytes 131072
  (66 shorter events, 7.1 us)
Async XLA Ops:
  0.0 10.0 %collective-permute-start = (bf16[64,512]{1,0:T(8,128)(2,1)}, bf16[64,512]{1,0:T(8,128)(2,1)S(1)}, u32[]{:S(2)}, u32[]{:S(2)}) collective-permute-start(bf16[64,512]{1,0:T(8,128)(2,1)} %bitcast.8), channel_id=1, source_target_pairs={{0,4},{1,5},{2,6},{3,7},{4,0},{5,1},{6,2},{7,3},{8,9},{9,8},{10,11... | collective-permute-start | bytes 196616 | tf_op jit(solution)/shard_map/ppermute | solution.py:211
  0.7 10.4 %collective-permute-start.1 = (bf16[64,512]{1,0:T(8,128)(2,1)}, bf16[64,512]{1,0:T(8,128)(2,1)S(1)}, u32[]{:S(2)}, u32[]{:S(2)}) collective-permute-start(bf16[64,512]{1,0:T(8,128)(2,1)} %bitcast.9), channel_id=1, source_target_pairs={{0,1},{1,0},{2,3},{3,2},{4,5},{5,4},{6,7},{7,6},{8,9},{9,8},{10,11... | collective-permute-start | bytes 196616 | tf_op jit(solution)/shard_map/ppermute | solution.py:200
  0.7 9.9 %collective-permute-start.3 = (bf16[64,512]{1,0:T(8,128)(2,1)}, bf16[64,512]{1,0:T(8,128)(2,1)S(1)}, u32[]{:S(2)}, u32[]{:S(2)}) collective-permute-start(bf16[64,512]{1,0:T(8,128)(2,1)} %bitcast.10), channel_id=1, source_target_pairs={{0,2},{1,3},{2,0},{3,1},{4,6},{5,7},{6,4},{7,5},{8,9},{9,8},{10,11... | collective-permute-start | bytes 196616 | tf_op jit(solution)/shard_map/ppermute | solution.py:211
  1.2 9.4 %collective-permute-start.5 = (bf16[64,512]{1,0:T(8,128)(2,1)}, bf16[64,512]{1,0:T(8,128)(2,1)S(1)}, u32[]{:S(2)}, u32[]{:S(2)}) collective-permute-start(bf16[64,512]{1,0:T(8,128)(2,1)} %bitcast.11), channel_id=1, source_target_pairs={{0,6},{1,7},{2,4},{3,5},{4,2},{5,3},{6,0},{7,1},{8,9},{9,8},{10,11... | collective-permute-start | bytes 196616 | tf_op jit(solution)/shard_map/ppermute | solution.py:211
  10.0 1.5 %collective-permute-start.2 = (bf16[64,512]{1,0:T(8,128)(2,1)S(1)}, bf16[64,512]{1,0:T(8,128)(2,1)S(1)}, u32[]{:S(2)}, u32[]{:S(2)}) collective-permute-start(bf16[64,512]{1,0:T(8,128)(2,1)S(1)} %collective-permute-done.refs_2_), channel_id=1, source_target_pairs={{0,1},{1,0},{2,3},{3,2},{4,5},{5,4},{6,7},{7,6},{8,9},{9,8},{10,11... | collective-permute-start | bytes 196616 | tf_op jit(solution)/shard_map/ppermute | solution.py:200
  10.6 1.3 %collective-permute-start.6 = (bf16[64,512]{1,0:T(8,128)(2,1)S(1)}, bf16[64,512]{1,0:T(8,128)(2,1)S(1)}, u32[]{:S(2)}, u32[]{:S(2)}) collective-permute-start(bf16[64,512]{1,0:T(8,128)(2,1)S(1)} %collective-permute-done.5.refs_1_), channel_id=1, source_target_pairs={{0,1},{1,0},{2,3},{3,2},{4,5},{5,4},{6,7},{7,6},{8,9},{9,8},{10,11... | collective-permute-start | bytes 196616 | tf_op jit(solution)/shard_map/ppermute | solution.py:200
  12.0 3.1 %collective-permute-start.7 = (bf16[64,512]{1,0:T(8,128)(2,1)S(1)}, bf16[64,512]{1,0:T(8,128)(2,1)S(1)}, u32[]{:S(2)}, u32[]{:S(2)}) collective-permute-start(bf16[64,512]{1,0:T(8,128)(2,1)S(1)} %late_tile.4.refs_0_), channel_id=1, source_target_pairs={{0,12},{1,13},{2,14},{3,15},{4,8},{5,9},{6,10},{7,11},{8,16},{9,17... | collective-permute-start | bytes 196616 | tf_op jit(solution)/shard_map/ppermute | solution.py:211
  12.4 2.9 %collective-permute-start.9 = (bf16[64,512]{1,0:T(8,128)(2,1)S(1)}, bf16[64,512]{1,0:T(8,128)(2,1)S(1)}, u32[]{:S(2)}, u32[]{:S(2)}) collective-permute-start(bf16[64,512]{1,0:T(8,128)(2,1)S(1)} %late_tile.4.refs_0_), channel_id=1, source_target_pairs={{0,10},{1,11},{2,8},{3,9},{4,14},{5,15},{6,12},{7,13}} | collective-permute-start | bytes 196616 | tf_op jit(solution)/shard_map/ppermute | solution.py:211
  13.0 2.6 %collective-permute-start.11 = (bf16[64,512]{1,0:T(8,128)(2,1)S(1)}, bf16[64,512]{1,0:T(8,128)(2,1)S(1)}, u32[]{:S(2)}, u32[]{:S(2)}) collective-permute-start(bf16[64,512]{1,0:T(8,128)(2,1)S(1)} %late_tile.4.refs_0_), channel_id=1, source_target_pairs={{0,14},{1,15},{2,12},{3,13},{4,10},{5,11},{6,8},{7,9}} | collective-permute-start | bytes 196616 | tf_op jit(solution)/shard_map/ppermute | solution.py:211
  13.7 2.1 %collective-permute-start.13 = (bf16[64,512]{1,0:T(8,128)(2,1)S(1)}, bf16[64,512]{1,0:T(8,128)(2,1)S(1)}, u32[]{:S(2)}, u32[]{:S(2)}) collective-permute-start(bf16[64,512]{1,0:T(8,128)(2,1)S(1)} %late_tile.4.refs_0_), channel_id=1, source_target_pairs={{0,8},{1,9},{2,10},{3,11},{4,12},{5,13},{6,14},{7,15}} | collective-permute-start | bytes 196616 | tf_op jit(solution)/shard_map/ppermute | solution.py:211
  15.1 1.3 %collective-permute-start.8 = (bf16[64,512]{1,0:T(8,128)(2,1)S(1)}, bf16[64,512]{1,0:T(8,128)(2,1)S(1)}, u32[]{:S(2)}, u32[]{:S(2)}) collective-permute-start(bf16[64,512]{1,0:T(8,128)(2,1)S(1)} %collective-permute-done.7.refs_0_), channel_id=1, source_target_pairs={{0,1},{1,0},{2,3},{3,2},{4,5},{5,4},{6,7},{7,6},{8,9},{9,8},{10,11... | collective-permute-start | bytes 196616 | tf_op jit(solution)/shard_map/ppermute | solution.py:200
  17.1 9.0 %collective-permute-start.15 = (bf16[64,512]{1,0:T(8,128)(2,1)S(1)}, bf16[64,512]{1,0:T(8,128)(2,1)S(1)}, u32[]{:S(2)}, u32[]{:S(2)}) collective-permute-start(bf16[64,512]{1,0:T(8,128)(2,1)S(1)} %late_tile.5.refs_0_), channel_id=1, source_target_pairs={{8,20},{9,21},{10,22},{11,23},{12,16},{13,17},{14,18},{15,19},{16,... | collective-permute-start | bytes 196616 | tf_op jit(solution)/shard_map/ppermute | solution.py:211
  23.4 3.2 %collective-permute-start.17 = (bf16[64,512]{1,0:T(8,128)(2,1)S(1)}, bf16[64,512]{1,0:T(8,128)(2,1)S(1)}, u32[]{:S(2)}, u32[]{:S(2)}) collective-permute-start(bf16[64,512]{1,0:T(8,128)(2,1)S(1)} %late_tile.5.refs_0_), channel_id=1, source_target_pairs={{8,18},{9,19},{10,16},{11,17},{12,22},{13,23},{14,20},{15,21}} | collective-permute-start | bytes 196616 | tf_op jit(solution)/shard_map/ppermute | solution.py:211
  24.0 2.6 %collective-permute-start.19 = (bf16[64,512]{1,0:T(8,128)(2,1)S(1)}, bf16[64,512]{1,0:T(8,128)(2,1)S(1)}, u32[]{:S(2)}, u32[]{:S(2)}) collective-permute-start(bf16[64,512]{1,0:T(8,128)(2,1)S(1)} %late_tile.5.refs_0_), channel_id=1, source_target_pairs={{8,22},{9,23},{10,20},{11,21},{12,18},{13,19},{14,16},{15,17}} | collective-permute-start | bytes 196616 | tf_op jit(solution)/shard_map/ppermute | solution.py:211
  24.7 2.4 %collective-permute-start.21 = (bf16[64,512]{1,0:T(8,128)(2,1)S(1)}, bf16[64,512]{1,0:T(8,128)(2,1)S(1)}, u32[]{:S(2)}, u32[]{:S(2)}) collective-permute-start(bf16[64,512]{1,0:T(8,128)(2,1)S(1)} %late_tile.5.refs_0_), channel_id=1, source_target_pairs={{8,16},{9,17},{10,18},{11,19},{12,20},{13,21},{14,22},{15,23}} | collective-permute-start | bytes 196616 | tf_op jit(solution)/shard_map/ppermute | solution.py:211
  26.0 1.4 %collective-permute-start.16 = (bf16[64,512]{1,0:T(8,128)(2,1)S(1)}, bf16[64,512]{1,0:T(8,128)(2,1)S(1)}, u32[]{:S(2)}, u32[]{:S(2)}) collective-permute-start(bf16[64,512]{1,0:T(8,128)(2,1)S(1)} %collective-permute-done.15.refs_0_), channel_id=1, source_target_pairs={{0,1},{1,0},{2,3},{3,2},{4,5},{5,4},{6,7},{7,6},{8,9},{9,8},{10,11... | collective-permute-start | bytes 196616 | tf_op jit(solution)/shard_map/ppermute | solution.py:200
  26.7 1.3 %collective-permute-start.20 = (bf16[64,512]{1,0:T(8,128)(2,1)S(1)}, bf16[64,512]{1,0:T(8,128)(2,1)S(1)}, u32[]{:S(2)}, u32[]{:S(2)}) collective-permute-start(bf16[64,512]{1,0:T(8,128)(2,1)S(1)} %collective-permute-done.19.refs_1_), channel_id=1, source_target_pairs={{0,1},{1,0},{2,3},{3,2},{4,5},{5,4},{6,7},{7,6},{8,9},{9,8},{10,11... | collective-permute-start | bytes 196616 | tf_op jit(solution)/shard_map/ppermute | solution.py:200
  28.4 10.3 %collective-permute-start.23 = (bf16[64,512]{1,0:T(8,128)(2,1)S(1)}, bf16[64,512]{1,0:T(8,128)(2,1)S(1)}, u32[]{:S(2)}, u32[]{:S(2)}) collective-permute-start(bf16[64,512]{1,0:T(8,128)(2,1)S(1)} %late_tile.6.refs_0_), channel_id=1, source_target_pairs={{16,28},{17,29},{18,30},{19,31},{20,24},{21,25},{22,26},{23,27},{2... | collective-permute-start | bytes 196616 | tf_op jit(solution)/shard_map/ppermute | solution.py:211
  28.4 11.6 %collective-permute-start.25 = (bf16[64,512]{1,0:T(8,128)(2,1)S(1)}, bf16[64,512]{1,0:T(8,128)(2,1)S(1)}, u32[]{:S(2)}, u32[]{:S(2)}) collective-permute-start(bf16[64,512]{1,0:T(8,128)(2,1)S(1)} %late_tile.6.refs_0_), channel_id=1, source_target_pairs={{16,26},{17,27},{18,24},{19,25},{20,30},{21,31},{22,28},{23,29}} | collective-permute-start | bytes 196616 | tf_op jit(solution)/shard_map/ppermute | solution.py:211
  29.6 11.8 %collective-permute-start.27 = (bf16[64,512]{1,0:T(8,128)(2,1)S(1)}, bf16[64,512]{1,0:T(8,128)(2,1)S(1)}, u32[]{:S(2)}, u32[]{:S(2)}) collective-permute-start(bf16[64,512]{1,0:T(8,128)(2,1)S(1)} %late_tile.6.refs_0_), channel_id=1, source_target_pairs={{16,30},{17,31},{18,28},{19,29},{20,26},{21,27},{22,24},{23,25},{2... | collective-permute-start | bytes 196616 | tf_op jit(solution)/shard_map/ppermute | solution.py:211
  33.1 9.1 %collective-permute-start.29 = (bf16[64,512]{1,0:T(8,128)(2,1)S(1)}, bf16[64,512]{1,0:T(8,128)(2,1)S(1)}, u32[]{:S(2)}, u32[]{:S(2)}) collective-permute-start(bf16[64,512]{1,0:T(8,128)(2,1)S(1)} %late_tile.6.refs_0_), channel_id=1, source_target_pairs={{16,24},{17,25},{18,26},{19,27},{20,28},{21,29},{22,30},{23,31},{2... | collective-permute-start | bytes 196616 | tf_op jit(solution)/shard_map/ppermute | solution.py:211
  38.6 3.7 %collective-permute-start.24 = (bf16[64,512]{1,0:T(8,128)(2,1)S(1)}, bf16[64,512]{1,0:T(8,128)(2,1)S(1)}, u32[]{:S(2)}, u32[]{:S(2)}) collective-permute-start(bf16[64,512]{1,0:T(8,128)(2,1)S(1)} %collective-permute-done.23.refs_0_), channel_id=1, source_target_pairs={{0,1},{1,0},{2,3},{3,2},{4,5},{5,4},{6,7},{7,6},{8,9},{9,8},{10,11... | collective-permute-start | bytes 196616 | tf_op jit(solution)/shard_map/ppermute | solution.py:200
  40.0 2.8 %collective-permute-start.26 = (bf16[64,512]{1,0:T(8,128)(2,1)S(1)}, bf16[64,512]{1,0:T(8,128)(2,1)S(1)}, u32[]{:S(2)}, u32[]{:S(2)}) collective-permute-start(bf16[64,512]{1,0:T(8,128)(2,1)S(1)} %collective-permute-done.25.refs_2_), channel_id=1, source_target_pairs={{0,1},{1,0},{2,3},{3,2},{4,5},{5,4},{6,7},{7,6},{8,9},{9,8},{10,11... | collective-permute-start | bytes 196616 | tf_op jit(solution)/shard_map/ppermute | solution.py:200
  41.5 1.6 %collective-permute-start.28 = (bf16[64,512]{1,0:T(8,128)(2,1)S(1)}, bf16[64,512]{1,0:T(8,128)(2,1)S(1)}, u32[]{:S(2)}, u32[]{:S(2)}) collective-permute-start(bf16[64,512]{1,0:T(8,128)(2,1)S(1)} %collective-permute-done.27.refs_1_), channel_id=1, source_target_pairs={{0,1},{1,0},{2,3},{3,2},{4,5},{5,4},{6,7},{7,6},{8,9},{9,8},{10,11... | collective-permute-start | bytes 196616 | tf_op jit(solution)/shard_map/ppermute | solution.py:200
  (10 other events, 14.2 us)

commit v6 on v5

--- a/solution.py
+++ b/solution.py
@@ -38,8 +38,16 @@
     return jnp.where(column % CORES == core, 0, chips) + order_of(chip ^ (column // CORES), chips)
 
 
-def place_kernel(chips, cols_ref, count_ref, greens_ref, solve_in, source_in, placed_ref, solve_ref, source_ref, sems):
+def spot_of(spots_ref, slot, positions):
+    spot = spots_ref[slot]
+    return spot < positions, jnp.where(spot < positions, spot, spot - positions)
+
+
+def place_kernel(chips, cols_ref, count_ref, greens_ref, solve_in, source_in, spots_ref, placed_ref, solve_ref, source_ref, sems):
     slots, positions = greens_ref.shape[2], placed_ref.shape[0]
+    for slot in range(slots):
+        position = position_of(slot, chips, cols_ref)
+        spots_ref[slot] = jnp.where(slot < count_ref[0, 0], position, position + positions)
 
     @pl.when(lax.axis_index("slab") == 0)
     def _():
@@ -53,9 +61,8 @@
             placed_ref[...] = jnp.zeros_like(placed_ref)
         moves = []
         for slot in range(slots):
-            position = position_of(slot, chips, cols_ref)
+            used, position = spot_of(spots_ref, slot, positions)
             move = pltpu.make_async_copy(greens_ref.at[0, 0, slot], placed_ref.at[position], sems.at[slot])
-            used = slot < count_ref[0, 0]
             moves.append((used, move))
             pl.when(used)(move.start)
             if positions == slots:
@@ -75,12 +82,13 @@
     return pl.pallas_call(
         functools.partial(place_kernel, chips),
         out_shape=(
+            pltpu.SMEM((slots,), jnp.int32),
             pltpu.VMEM((chips * CORES, rows, depth), greens.dtype),
             pltpu.VMEM(solve.shape[2:], solve.dtype),
             pltpu.VMEM(source.shape, source.dtype),
         ),
         in_specs=[IN_SMEM] * 2 + [ANYWHERE] * 3,
-        out_specs=(IN_VMEM,) * 3,
+        out_specs=(IN_SMEM,) + (IN_VMEM,) * 3,
         scratch_shapes=[pltpu.SemaphoreType.DMA((slots + 2,))],
         compiler_params=params(),
         cost_estimate=pl.CostEstimate(flops=0, bytes_accessed=2 * greens.size * 2, transcendentals=0),
@@ -88,47 +96,44 @@
     )(cols, count, greens, solve, source)
 
 
-def fold_kernel(section, chips, cols_ref, count_ref, greens_ref, solve_in, source_in, folded_ref, base_ref, held_ref, solve_ref, source_ref, sems):
+def fold_kernel(section, spots_ref, greens_ref, solve_in, source_in, folded_ref, base_ref, held_ref, solve_ref, source_ref, sems):
     slots, positions = greens_ref.shape[2], folded_ref.shape[0]
 
     @pl.when(lax.axis_index("slab") == section)
     def _():
         copies = [
-            pltpu.make_async_copy(greens_ref.at[0, 0, slot], held_ref.at[slot], sems.at[slot]) for slot in range(slots)
-        ]
-        early_copies = [
             pltpu.make_async_copy(solve_in.at[0, 0], solve_ref, sems.at[slots]),
             pltpu.make_async_copy(source_in, source_ref, sems.at[slots + 1]),
         ]
-        for copy in early_copies + copies:
+        copies += [
+            pltpu.make_async_copy(greens_ref.at[0, 0, slot], held_ref.at[slot], sems.at[slot]) for slot in range(slots)
+        ]
+        for copy in copies:
             copy.start()
         if positions > slots:
             folded_ref[...] = jnp.zeros_like(folded_ref)
-        for copy in early_copies:
+        for copy in copies:
             copy.wait()
         base_ref[...] = lax.dot_general(source_ref[...], solve_ref[...], LAST_LAST, preferred_element_type=jnp.float32)
-        for copy in copies:
-            copy.wait()
 
         def fold_slot(slot, carry):
             solved = lax.dot_general(held_ref[slot], solve_ref[...], FIRST_LAST, preferred_element_type=jnp.float32)
-            used = slot < count_ref[0, 0]
-            solved = jnp.where(used, solved, jnp.zeros_like(solved)).astype(folded_ref.dtype)
-            folded_ref[position_of(slot, chips, cols_ref)] = solved
+            used, position = spot_of(spots_ref, slot, positions)
+            folded_ref[position] = jnp.where(used, solved, jnp.zeros_like(solved)).astype(folded_ref.dtype)
             return carry
 
         lax.fori_loop(0, slots, fold_slot, 0)
 
 
-def fold(section, chips, cols, count, greens, solve, source):
+def fold(section, positions, spots, greens, solve, source):
     slots, rows, depth = greens.shape[2:]
     return pl.pallas_call(
-        functools.partial(fold_kernel, section, chips),
+        functools.partial(fold_kernel, section),
         out_shape=(
-            pltpu.VMEM((chips * CORES, depth, rows), greens.dtype),
+            pltpu.VMEM((positions, depth, rows), greens.dtype),
             pltpu.VMEM(source.shape, jnp.float32),
         ),
-        in_specs=[IN_SMEM] * 2 + [ANYWHERE] * 3,
+        in_specs=[IN_SMEM] + [ANYWHERE] * 3,
         out_specs=(IN_VMEM,) * 2,
         scratch_shapes=[
             pltpu.VMEM((slots, rows, depth), greens.dtype),
@@ -141,7 +146,7 @@
             flops=2 * greens.size * rows, bytes_accessed=2 * greens.size * 2, transcendentals=0
         ),
         name="fold",
-    )(cols, count, greens, solve, source)
+    )(spots, greens, solve, source)
 
 
 def products(tiles, positions, placed_ref, folded, total):
@@ -216,11 +221,9 @@
     if len(others) < 2 or chips < 4:
         return [None] * chips
     free, late = others[0], others[-1]
-    if section == 1:
-        return [(free,), None, None, None] + [None] * (chips - 4)
     if section < slabs - 1:
-        return [(free,), None, None, None] + [None] * (chips - 4)
-    return [(free,), None, (late, free), ()][:1] + [None] * (chips - 4) + [(free,), None, (late, free), ()][1:]
+        return [(free,)] + [None] * (chips - 1)
+    return [(free,)] + [None] * (chips - 3) + [(late, free), ()]
 
 
 def direct(forcing, inflow, self_solve, greens, kept_cols, counts):
@@ -231,8 +234,8 @@
     greens, self_solve, source = (
         pltpu.with_memory_space_constraint(array, pltpu.HBM) for array in (greens, self_solve, source)
     )
-    given = (chips, kept_cols, counts, greens, self_solve, source)
-    placed, solve, base = place(*given)
+    spots, placed, solve, base = place(chips, kept_cols, counts, greens, self_solve, source)
+    given = (rows, spots, greens, self_solve, source)
     ready = fold(last, *given) if last > 0 else ()
     trace = jnp.zeros(entering.shape, jnp.bfloat16)
     for section in range(slabs):
@@ -250,14 +253,26 @@
                 placed, base, own[0] = lax.optimization_barrier((placed, base, own[0]))
             else:
                 placed, base = ready
-        other = [swapped(tile, rows) for tile in own]
-        arriving = []
-        for order, *both in zip(orders, own, other):
-            arriving += [(tile, side * chips + order) for side, tile in enumerate(both)]
-        total = base
-        for first in [0, *range(3, len(arriving) - 1, 2)]:
-            tiles, positions = zip(*arriving[first : first + 3 if first == 0 else first + 2])
+        if section == 0:
+            other = [swapped(tile, rows) for tile in own[:-1]]
+            held = [(own[0], orders[0]), (other[0], chips + orders[0])] + [(own[i], orders[i]) for i in range(1, chips - 1)]
+            tiles, positions = zip(*held)
+            total = early(section, positions, placed, base, tiles)
+            own[-1], total = lax.optimization_barrier((own[-1], total))
+            other.append(swapped(own[-1], rows))
+            held = [(other[i], chips + orders[i]) for i in range(1, chips - 1)] + [(own[-1], orders[-1])]
+            tiles, positions = zip(*held)
             total = early(section, positions, placed, total, tiles)
+            arriving = [(None, chips + orders[-1])]
+        else:
+            other = [swapped(tile, rows) for tile in own]
+            arriving = []
+            for order, *both in zip(orders, own, other):
+                arriving += [(tile, side * chips + order) for side, tile in enumerate(both)]
+            total = base
+            for first in [0, *range(3, len(arriving) - 1, 2)]:
+                tiles, positions = zip(*arriving[first : first + 3 if first == 0 else first + 2])
+                total = early(section, positions, placed, total, tiles)
         trace = late(section, arriving[-1][1], placed, total, other[-1], solve, trace)
     return trace.T[None]
 

time: 44.6 us -> 44.7 us (level)
  starting transfers between devices: 24.8 us -> 26.5 us
  Pallas kernels: 9.94 us -> 8.69 us
    pallas_call x4, Pallas kernels: 8.72 us -> 7.48 us  [the longest x3 6.76 us: fold(): pl.pallas_call(functools.partial(fold_kernel, section), out_shape=(pltpu....]
    ppermute x15, starting transfers between devices: 19.3 us -> 20.3 us  [sent(): return lax.ppermute(tile, ('slab', 'row'), pairs)]
    ppermute x16, starting transfers between devices: 5.56 us -> 6.27 us  [swapped(): return lax.ppermute(tile, 'row', [(r, r ^ 1) for r in range(rows)])]
    unnamed x7 -> x5, local copies, waits for them, and re-layouts: 1.29 us -> 1.29 us
    pallas_call x12 -> x11, Pallas kernels: 1 us -> 1 us  [early(): pl.pallas_call(functools.partial(early_kernel, section, positions), out_s...]
  transfers between devices with their start and end apart: 31 -> 31, of which waited for: 13 -> 13; matrix products, arithmetic and copies ran while one was open for 0% -> 0% of each run, Pallas kernels for 22% -> 19%
where the time goes in v6:
time: 44.7 us; the launch traced here: 44.5 us
  starting transfers between devices  26.5 us (59%)
  Pallas kernels  8.69 us (19%)
  waiting for transfers between devices  7.1 us (16%)
  local copies, waits for them, and re-layouts  1.29 us (3%)
  between operations  0.87 us (2%)
    ppermute x15, starting transfers between devices, sent(): return lax.ppermute(tile, ('slab', 'row'), pairs)  20.3 us
    pallas_call x3, Pallas kernels, fold(): pl.pallas_call(functools.partial(fold_kernel, section), out_shape=(pltpu....  6.76 us
    ppermute x16, starting transfers between devices, swapped(): return lax.ppermute(tile, 'row', [(r, r ^ 1) for r in range(rows)])  6.27 us
    ppermute x15, waiting for transfers between devices, sent(): return lax.ppermute(tile, ('slab', 'row'), pairs)  4.13 us
    ppermute x16, waiting for transfers between devices, swapped(): return lax.ppermute(tile, 'row', [(r, r ^ 1) for r in range(rows)])  2.97 us
    unnamed x5, local copies, waits for them, and re-layouts  1.29 us
    pallas_call x11, Pallas kernels, early(): pl.pallas_call(functools.partial(early_kernel, section, positions), out_s...  1 us
  transfers between devices with their start and end apart: 31, of which 13 were waited for; matrix products, arithmetic and copies ran while one was open for 0% of the time, Pallas kernels for 19%

profile of v6, /device:TPU:7, one launch (start us, length us, event | category | flops | bytes accessed | tf_op | source)
XLA Modules:
  0.0 44.5 jit_solution(4480027044977816580)
XLA Ops:
  0.0 0.7 %collective-permute-start = (bf16[64,512]{1,0:T(8,128)(2,1)}, bf16[64,512]{1,0:T(8,128)(2,1)S(1)}, u32[]{:S(2)}, u32[]{:S(2)}) collective-permute-start(bf16[64,512]{1,0:T(8,128)(2,1)} %bitcast.8), channel_id=1, source_target_pairs={{0,4},{1,5},{2,6},{3,7},{4,0},{5,1},{6,2},{7,3},{8,9},{9,8},{10,11... | collective-permute-start | bytes 196616 | tf_op jit(solution)/shard_map/ppermute | solution.py:216
  0.7 0.5 %collective-permute-start.2 = (bf16[64,512]{1,0:T(8,128)(2,1)}, bf16[64,512]{1,0:T(8,128)(2,1)S(1)}, u32[]{:S(2)}, u32[]{:S(2)}) collective-permute-start(bf16[64,512]{1,0:T(8,128)(2,1)} %bitcast.10), channel_id=1, source_target_pairs={{0,1},{1,0},{2,3},{3,2},{4,5},{5,4},{6,7},{7,6},{8,9},{9,8},{10,11... | collective-permute-start | bytes 196616 | tf_op jit(solution)/shard_map/ppermute | solution.py:205
  1.9 0.6 %copy-done.1 = s32[1,1,8]{2,1,0:T(1,128)S(1)} copy-done((s32[1,1,8]{2,1,0:T(1,128)S(1)}, s32[1,1,8]{2,1,0:T(1,128)}, u32[]{:S(2)}) %copy-start.1) | copy-done | bytes 56
  2.5 0.7 %place.1 = (s32[8]{0:T(128)S(4)}, bf16[8,512,512]{2,1,0:T(8,128)(2,1)S(1)}, bf16[512,512]{1,0:T(8,128)(2,1)S(1)}, bf16[64,512]{1,0:T(8,128)(2,1)S(1)}) custom-call(s32[1,1,8]{2,1,0:T(1,128)S(1)} %copy-done.1, s32[1,1]{1,0:T(1,128)S(6)} %copy.16.count_ref, bf16[1,1,8,512,512]{4,3,2,1,0:T(8,128)(2,1)} %greens_ref.7, bf16[1,1,512,512]{3,2,1,0:T(8,128)(2,1)} %solve_in.7, ...), custom_call_target="tpu_custom_call" | custom-call | bytes 8388608 | tf_op jit(solution)/shard_map/place/pallas_call | solution.py:82
  3.2 6.5 %fold.3 = (bf16[8,512,512]{2,1,0:T(8,128)(2,1)S(1)}, f32[64,512]{1,0:T(8,128)S(1)}) custom-call(s32[8]{0:T(128)S(4)} %get-tuple-element.32.spots_ref, bf16[1,1,8,512,512]{4,3,2,1,0:T(8,128)(2,1)} %greens_ref.7, bf16[1,1,512,512]{3,2,1,0:T(8,128)(2,1)} %solve_in.7, bf16[64,512]{1,0:T(8,128)(2,1)} %bitcast.14), custom_call_target="tpu_custom_call" | custom-call | flops 2147483648 | bytes 8388608 | tf_op jit(solution)/shard_map/fold/pallas_call | solution.py:130
  9.8 0.6 %collective-permute-start.4 = (bf16[64,512]{1,0:T(8,128)(2,1)S(1)}, bf16[64,512]{1,0:T(8,128)(2,1)S(1)}, u32[]{:S(2)}, u32[]{:S(2)}) collective-permute-start(bf16[64,512]{1,0:T(8,128)(2,1)S(1)} %collective-permute-done.refs_2_), channel_id=1, source_target_pairs={{0,1},{1,0},{2,3},{3,2},{4,5},{5,4},{6,7},{7,6},{8,9},{9,8},{10,11... | collective-permute-start | bytes 196616 | tf_op jit(solution)/shard_map/ppermute | solution.py:205
  10.5 0.5 %collective-permute-start.6 = (bf16[64,512]{1,0:T(8,128)(2,1)S(1)}, bf16[64,512]{1,0:T(8,128)(2,1)S(1)}, u32[]{:S(2)}, u32[]{:S(2)}) collective-permute-start(bf16[64,512]{1,0:T(8,128)(2,1)S(1)} %collective-permute-done.1.refs_2_), channel_id=1, source_target_pairs={{0,1},{1,0},{2,3},{3,2},{4,5},{5,4},{6,7},{7,6},{8,9},{9,8},{10,11... | collective-permute-start | bytes 196616 | tf_op jit(solution)/shard_map/ppermute | solution.py:205
  12.3 0.7 %collective-permute-start.9 = (bf16[64,512]{1,0:T(8,128)(2,1)S(1)}, bf16[64,512]{1,0:T(8,128)(2,1)S(1)}, u32[]{:S(2)}, u32[]{:S(2)}) collective-permute-start(bf16[64,512]{1,0:T(8,128)(2,1)S(1)} %late_tile.4.refs_0_), channel_id=1, source_target_pairs={{0,10},{1,11},{2,8},{3,9},{4,14},{5,15},{6,12},{7,13}} | collective-permute-start | bytes 196616 | tf_op jit(solution)/shard_map/ppermute | solution.py:216
  13.0 0.7 %collective-permute-start.11 = (bf16[64,512]{1,0:T(8,128)(2,1)S(1)}, bf16[64,512]{1,0:T(8,128)(2,1)S(1)}, u32[]{:S(2)}, u32[]{:S(2)}) collective-permute-start(bf16[64,512]{1,0:T(8,128)(2,1)S(1)} %late_tile.4.refs_0_), channel_id=1, source_target_pairs={{0,14},{1,15},{2,12},{3,13},{4,10},{5,11},{6,8},{7,9}} | collective-permute-start | bytes 196616 | tf_op jit(solution)/shard_map/ppermute | solution.py:216
  13.7 0.7 %collective-permute-start.13 = (bf16[64,512]{1,0:T(8,128)(2,1)S(1)}, bf16[64,512]{1,0:T(8,128)(2,1)S(1)}, u32[]{:S(2)}, u32[]{:S(2)}) collective-permute-start(bf16[64,512]{1,0:T(8,128)(2,1)S(1)} %late_tile.4.refs_0_), channel_id=1, source_target_pairs={{0,8},{1,9},{2,10},{3,11},{4,12},{5,13},{6,14},{7,15}} | collective-permute-start | bytes 196616 | tf_op jit(solution)/shard_map/ppermute | solution.py:216
  16.5 7.2 %collective-permute-start.15 = (bf16[64,512]{1,0:T(8,128)(2,1)S(1)}, bf16[64,512]{1,0:T(8,128)(2,1)S(1)}, u32[]{:S(2)}, u32[]{:S(2)}) collective-permute-start(bf16[64,512]{1,0:T(8,128)(2,1)S(1)} %late_tile.5.refs_0_), channel_id=1, source_target_pairs={{8,20},{9,21},{10,22},{11,23},{12,16},{13,17},{14,18},{15,19},{16,... | collective-permute-start | bytes 196616 | tf_op jit(solution)/shard_map/ppermute | solution.py:216
  23.6 0.7 %collective-permute-start.17 = (bf16[64,512]{1,0:T(8,128)(2,1)S(1)}, bf16[64,512]{1,0:T(8,128)(2,1)S(1)}, u32[]{:S(2)}, u32[]{:S(2)}) collective-permute-start(bf16[64,512]{1,0:T(8,128)(2,1)S(1)} %late_tile.5.refs_0_), channel_id=1, source_target_pairs={{8,18},{9,19},{10,16},{11,17},{12,22},{13,23},{14,20},{15,21}} | collective-permute-start | bytes 196616 | tf_op jit(solution)/shard_map/ppermute | solution.py:216
  24.3 0.7 %collective-permute-start.19 = (bf16[64,512]{1,0:T(8,128)(2,1)S(1)}, bf16[64,512]{1,0:T(8,128)(2,1)S(1)}, u32[]{:S(2)}, u32[]{:S(2)}) collective-permute-start(bf16[64,512]{1,0:T(8,128)(2,1)S(1)} %late_tile.5.refs_0_), channel_id=1, source_target_pairs={{8,22},{9,23},{10,20},{11,21},{12,18},{13,19},{14,16},{15,17}} | collective-permute-start | bytes 196616 | tf_op jit(solution)/shard_map/ppermute | solution.py:216
  24.9 0.7 %collective-permute-start.21 = (bf16[64,512]{1,0:T(8,128)(2,1)S(1)}, bf16[64,512]{1,0:T(8,128)(2,1)S(1)}, u32[]{:S(2)}, u32[]{:S(2)}) collective-permute-start(bf16[64,512]{1,0:T(8,128)(2,1)S(1)} %late_tile.5.refs_0_), channel_id=1, source_target_pairs={{8,16},{9,17},{10,18},{11,19},{12,20},{13,21},{14,22},{15,23}} | collective-permute-start | bytes 196616 | tf_op jit(solution)/shard_map/ppermute | solution.py:216
  25.7 0.7 %collective-permute-start.16 = (bf16[64,512]{1,0:T(8,128)(2,1)S(1)}, bf16[64,512]{1,0:T(8,128)(2,1)S(1)}, u32[]{:S(2)}, u32[]{:S(2)}) collective-permute-start(bf16[64,512]{1,0:T(8,128)(2,1)S(1)} %collective-permute-done.15.refs_0_), channel_id=1, source_target_pairs={{0,1},{1,0},{2,3},{3,2},{4,5},{5,4},{6,7},{7,6},{8,9},{9,8},{10,11... | collective-permute-start | bytes 196616 | tf_op jit(solution)/shard_map/ppermute | solution.py:205
  26.5 0.4 collective-permute-start.20
  28.2 1.3 %collective-permute-start.25 = (bf16[64,512]{1,0:T(8,128)(2,1)S(1)}, bf16[64,512]{1,0:T(8,128)(2,1)S(1)}, u32[]{:S(2)}, u32[]{:S(2)}) collective-permute-start(bf16[64,512]{1,0:T(8,128)(2,1)S(1)} %late_tile.6.refs_0_), channel_id=1, source_target_pairs={{16,26},{17,27},{18,24},{19,25},{20,30},{21,31},{22,28},{23,29}} | collective-permute-start | bytes 196616 | tf_op jit(solution)/shard_map/ppermute | solution.py:216
  29.5 4.1 %collective-permute-start.27 = (bf16[64,512]{1,0:T(8,128)(2,1)S(1)}, bf16[64,512]{1,0:T(8,128)(2,1)S(1)}, u32[]{:S(2)}, u32[]{:S(2)}) collective-permute-start(bf16[64,512]{1,0:T(8,128)(2,1)S(1)} %late_tile.6.refs_0_), channel_id=1, source_target_pairs={{16,30},{17,31},{18,28},{19,29},{20,26},{21,27},{22,24},{23,25},{2... | collective-permute-start | bytes 196616 | tf_op jit(solution)/shard_map/ppermute | solution.py:216
  33.6 2.7 %collective-permute-start.29 = (bf16[64,512]{1,0:T(8,128)(2,1)S(1)}, bf16[64,512]{1,0:T(8,128)(2,1)S(1)}, u32[]{:S(2)}, u32[]{:S(2)}) collective-permute-start(bf16[64,512]{1,0:T(8,128)(2,1)S(1)} %late_tile.6.refs_0_), channel_id=1, source_target_pairs={{16,24},{17,25},{18,26},{19,27},{20,28},{21,29},{22,30},{23,31},{2... | collective-permute-start | bytes 196616 | tf_op jit(solution)/shard_map/ppermute | solution.py:216
  36.3 2.7 %collective-permute-done.23.refs_0_ = bf16[64,512]{1,0:T(8,128)(2,1)S(1)} collective-permute-done((bf16[64,512]{1,0:T(8,128)(2,1)S(1)}, bf16[64,512]{1,0:T(8,128)(2,1)S(1)}, u32[]{:S(2)}, u32[]{:S(2)}) %collective-permute-start.23) | collective-permute-done | bytes 65568 | tf_op jit(solution)/shard_map/ppermute | solution.py:216
  39.0 1.3 %collective-permute-start.24 = (bf16[64,512]{1,0:T(8,128)(2,1)S(1)}, bf16[64,512]{1,0:T(8,128)(2,1)S(1)}, u32[]{:S(2)}, u32[]{:S(2)}) collective-permute-start(bf16[64,512]{1,0:T(8,128)(2,1)S(1)} %collective-permute-done.23.refs_0_), channel_id=1, source_target_pairs={{0,1},{1,0},{2,3},{3,2},{4,5},{5,4},{6,7},{7,6},{8,9},{9,8},{10,11... | collective-permute-start | bytes 196616 | tf_op jit(solution)/shard_map/ppermute | solution.py:205
  40.2 1.4 %collective-permute-done.27.refs_1_ = bf16[64,512]{1,0:T(8,128)(2,1)S(1)} collective-permute-done((bf16[64,512]{1,0:T(8,128)(2,1)S(1)}, bf16[64,512]{1,0:T(8,128)(2,1)S(1)}, u32[]{:S(2)}, u32[]{:S(2)}) %collective-permute-start.27) | collective-permute-done | bytes 65568 | tf_op jit(solution)/shard_map/ppermute | solution.py:216
  41.6 0.7 %collective-permute-start.28 = (bf16[64,512]{1,0:T(8,128)(2,1)S(1)}, bf16[64,512]{1,0:T(8,128)(2,1)S(1)}, u32[]{:S(2)}, u32[]{:S(2)}) collective-permute-start(bf16[64,512]{1,0:T(8,128)(2,1)S(1)} %collective-permute-done.27.refs_1_), channel_id=1, source_target_pairs={{0,1},{1,0},{2,3},{3,2},{4,5},{5,4},{6,7},{7,6},{8,9},{9,8},{10,11... | collective-permute-start | bytes 196616 | tf_op jit(solution)/shard_map/ppermute | solution.py:205
  43.9 0.6 %copy.15 = bf16[1,512,64]{1,2,0:T(8,128)(2,1)} copy(bf16[1,512,64]{1,2,0:T(8,128)(2,1)S(1)} %bitcast.7) | data formatting | bytes 131072
  (63 shorter events, 6.5 us)
Async XLA Ops:
  0.0 9.8 %collective-permute-start = (bf16[64,512]{1,0:T(8,128)(2,1)}, bf16[64,512]{1,0:T(8,128)(2,1)S(1)}, u32[]{:S(2)}, u32[]{:S(2)}) collective-permute-start(bf16[64,512]{1,0:T(8,128)(2,1)} %bitcast.8), channel_id=1, source_target_pairs={{0,4},{1,5},{2,6},{3,7},{4,0},{5,1},{6,2},{7,3},{8,9},{9,8},{10,11... | collective-permute-start | bytes 196616 | tf_op jit(solution)/shard_map/ppermute | solution.py:216
  0.7 9.7 %collective-permute-start.3 = (bf16[64,512]{1,0:T(8,128)(2,1)}, bf16[64,512]{1,0:T(8,128)(2,1)S(1)}, u32[]{:S(2)}, u32[]{:S(2)}) collective-permute-start(bf16[64,512]{1,0:T(8,128)(2,1)} %bitcast.9), channel_id=1, source_target_pairs={{0,2},{1,3},{2,0},{3,1},{4,6},{5,7},{6,4},{7,5},{8,9},{9,8},{10,11... | collective-permute-start | bytes 196616 | tf_op jit(solution)/shard_map/ppermute | solution.py:216
  0.7 9.8 %collective-permute-start.2 = (bf16[64,512]{1,0:T(8,128)(2,1)}, bf16[64,512]{1,0:T(8,128)(2,1)S(1)}, u32[]{:S(2)}, u32[]{:S(2)}) collective-permute-start(bf16[64,512]{1,0:T(8,128)(2,1)} %bitcast.10), channel_id=1, source_target_pairs={{0,1},{1,0},{2,3},{3,2},{4,5},{5,4},{6,7},{7,6},{8,9},{9,8},{10,11... | collective-permute-start | bytes 196616 | tf_op jit(solution)/shard_map/ppermute | solution.py:205
  1.2 9.3 %collective-permute-start.1 = (bf16[64,512]{1,0:T(8,128)(2,1)}, bf16[64,512]{1,0:T(8,128)(2,1)S(1)}, u32[]{:S(2)}, u32[]{:S(2)}) collective-permute-start(bf16[64,512]{1,0:T(8,128)(2,1)} %bitcast.11), channel_id=1, source_target_pairs={{0,6},{1,7},{2,4},{3,5},{4,2},{5,3},{6,0},{7,1},{8,9},{9,8},{10,11... | collective-permute-start | bytes 196616 | tf_op jit(solution)/shard_map/ppermute | solution.py:216
  9.8 1.5 %collective-permute-start.4 = (bf16[64,512]{1,0:T(8,128)(2,1)S(1)}, bf16[64,512]{1,0:T(8,128)(2,1)S(1)}, u32[]{:S(2)}, u32[]{:S(2)}) collective-permute-start(bf16[64,512]{1,0:T(8,128)(2,1)S(1)} %collective-permute-done.refs_2_), channel_id=1, source_target_pairs={{0,1},{1,0},{2,3},{3,2},{4,5},{5,4},{6,7},{7,6},{8,9},{9,8},{10,11... | collective-permute-start | bytes 196616 | tf_op jit(solution)/shard_map/ppermute | solution.py:205
  10.5 1.4 %collective-permute-start.6 = (bf16[64,512]{1,0:T(8,128)(2,1)S(1)}, bf16[64,512]{1,0:T(8,128)(2,1)S(1)}, u32[]{:S(2)}, u32[]{:S(2)}) collective-permute-start(bf16[64,512]{1,0:T(8,128)(2,1)S(1)} %collective-permute-done.1.refs_2_), channel_id=1, source_target_pairs={{0,1},{1,0},{2,3},{3,2},{4,5},{5,4},{6,7},{7,6},{8,9},{9,8},{10,11... | collective-permute-start | bytes 196616 | tf_op jit(solution)/shard_map/ppermute | solution.py:205
  11.9 2.5 %collective-permute-start.7 = (bf16[64,512]{1,0:T(8,128)(2,1)S(1)}, bf16[64,512]{1,0:T(8,128)(2,1)S(1)}, u32[]{:S(2)}, u32[]{:S(2)}) collective-permute-start(bf16[64,512]{1,0:T(8,128)(2,1)S(1)} %late_tile.4.refs_0_), channel_id=1, source_target_pairs={{0,12},{1,13},{2,14},{3,15},{4,8},{5,9},{6,10},{7,11},{8,16},{9,17... | collective-permute-start | bytes 196616 | tf_op jit(solution)/shard_map/ppermute | solution.py:216
  12.3 2.3 %collective-permute-start.9 = (bf16[64,512]{1,0:T(8,128)(2,1)S(1)}, bf16[64,512]{1,0:T(8,128)(2,1)S(1)}, u32[]{:S(2)}, u32[]{:S(2)}) collective-permute-start(bf16[64,512]{1,0:T(8,128)(2,1)S(1)} %late_tile.4.refs_0_), channel_id=1, source_target_pairs={{0,10},{1,11},{2,8},{3,9},{4,14},{5,15},{6,12},{7,13}} | collective-permute-start | bytes 196616 | tf_op jit(solution)/shard_map/ppermute | solution.py:216
  13.0 2.1 %collective-permute-start.11 = (bf16[64,512]{1,0:T(8,128)(2,1)S(1)}, bf16[64,512]{1,0:T(8,128)(2,1)S(1)}, u32[]{:S(2)}, u32[]{:S(2)}) collective-permute-start(bf16[64,512]{1,0:T(8,128)(2,1)S(1)} %late_tile.4.refs_0_), channel_id=1, source_target_pairs={{0,14},{1,15},{2,12},{3,13},{4,10},{5,11},{6,8},{7,9}} | collective-permute-start | bytes 196616 | tf_op jit(solution)/shard_map/ppermute | solution.py:216
  13.7 1.5 %collective-permute-start.13 = (bf16[64,512]{1,0:T(8,128)(2,1)S(1)}, bf16[64,512]{1,0:T(8,128)(2,1)S(1)}, u32[]{:S(2)}, u32[]{:S(2)}) collective-permute-start(bf16[64,512]{1,0:T(8,128)(2,1)S(1)} %late_tile.4.refs_0_), channel_id=1, source_target_pairs={{0,8},{1,9},{2,10},{3,11},{4,12},{5,13},{6,14},{7,15}} | collective-permute-start | bytes 196616 | tf_op jit(solution)/shard_map/ppermute | solution.py:216
  14.5 1.3 %collective-permute-start.8 = (bf16[64,512]{1,0:T(8,128)(2,1)S(1)}, bf16[64,512]{1,0:T(8,128)(2,1)S(1)}, u32[]{:S(2)}, u32[]{:S(2)}) collective-permute-start(bf16[64,512]{1,0:T(8,128)(2,1)S(1)} %collective-permute-done.7.refs_0_), channel_id=1, source_target_pairs={{0,1},{1,0},{2,3},{3,2},{4,5},{5,4},{6,7},{7,6},{8,9},{9,8},{10,11... | collective-permute-start | bytes 196616 | tf_op jit(solution)/shard_map/ppermute | solution.py:205
  16.5 9.3 %collective-permute-start.15 = (bf16[64,512]{1,0:T(8,128)(2,1)S(1)}, bf16[64,512]{1,0:T(8,128)(2,1)S(1)}, u32[]{:S(2)}, u32[]{:S(2)}) collective-permute-start(bf16[64,512]{1,0:T(8,128)(2,1)S(1)} %late_tile.5.refs_0_), channel_id=1, source_target_pairs={{8,20},{9,21},{10,22},{11,23},{12,16},{13,17},{14,18},{15,19},{16,... | collective-permute-start | bytes 196616 | tf_op jit(solution)/shard_map/ppermute | solution.py:216
  23.6 2.8 %collective-permute-start.17 = (bf16[64,512]{1,0:T(8,128)(2,1)S(1)}, bf16[64,512]{1,0:T(8,128)(2,1)S(1)}, u32[]{:S(2)}, u32[]{:S(2)}) collective-permute-start(bf16[64,512]{1,0:T(8,128)(2,1)S(1)} %late_tile.5.refs_0_), channel_id=1, source_target_pairs={{8,18},{9,19},{10,16},{11,17},{12,22},{13,23},{14,20},{15,21}} | collective-permute-start | bytes 196616 | tf_op jit(solution)/shard_map/ppermute | solution.py:216
  24.3 2.2 %collective-permute-start.19 = (bf16[64,512]{1,0:T(8,128)(2,1)S(1)}, bf16[64,512]{1,0:T(8,128)(2,1)S(1)}, u32[]{:S(2)}, u32[]{:S(2)}) collective-permute-start(bf16[64,512]{1,0:T(8,128)(2,1)S(1)} %late_tile.5.refs_0_), channel_id=1, source_target_pairs={{8,22},{9,23},{10,20},{11,21},{12,18},{13,19},{14,16},{15,17}} | collective-permute-start | bytes 196616 | tf_op jit(solution)/shard_map/ppermute | solution.py:216
  24.9 2.0 %collective-permute-start.21 = (bf16[64,512]{1,0:T(8,128)(2,1)S(1)}, bf16[64,512]{1,0:T(8,128)(2,1)S(1)}, u32[]{:S(2)}, u32[]{:S(2)}) collective-permute-start(bf16[64,512]{1,0:T(8,128)(2,1)S(1)} %late_tile.5.refs_0_), channel_id=1, source_target_pairs={{8,16},{9,17},{10,18},{11,19},{12,20},{13,21},{14,22},{15,23}} | collective-permute-start | bytes 196616 | tf_op jit(solution)/shard_map/ppermute | solution.py:216
  25.7 1.6 %collective-permute-start.16 = (bf16[64,512]{1,0:T(8,128)(2,1)S(1)}, bf16[64,512]{1,0:T(8,128)(2,1)S(1)}, u32[]{:S(2)}, u32[]{:S(2)}) collective-permute-start(bf16[64,512]{1,0:T(8,128)(2,1)S(1)} %collective-permute-done.15.refs_0_), channel_id=1, source_target_pairs={{0,1},{1,0},{2,3},{3,2},{4,5},{5,4},{6,7},{7,6},{8,9},{9,8},{10,11... | collective-permute-start | bytes 196616 | tf_op jit(solution)/shard_map/ppermute | solution.py:205
  26.5 1.3 %collective-permute-start.20 = (bf16[64,512]{1,0:T(8,128)(2,1)S(1)}, bf16[64,512]{1,0:T(8,128)(2,1)S(1)}, u32[]{:S(2)}, u32[]{:S(2)}) collective-permute-start(bf16[64,512]{1,0:T(8,128)(2,1)S(1)} %collective-permute-done.19.refs_1_), channel_id=1, source_target_pairs={{0,1},{1,0},{2,3},{3,2},{4,5},{5,4},{6,7},{7,6},{8,9},{9,8},{10,11... | collective-permute-start | bytes 196616 | tf_op jit(solution)/shard_map/ppermute | solution.py:205
  28.2 10.8 %collective-permute-start.23 = (bf16[64,512]{1,0:T(8,128)(2,1)S(1)}, bf16[64,512]{1,0:T(8,128)(2,1)S(1)}, u32[]{:S(2)}, u32[]{:S(2)}) collective-permute-start(bf16[64,512]{1,0:T(8,128)(2,1)S(1)} %late_tile.6.refs_0_), channel_id=1, source_target_pairs={{16,28},{17,29},{18,30},{19,31},{20,24},{21,25},{22,26},{23,27},{2... | collective-permute-start | bytes 196616 | tf_op jit(solution)/shard_map/ppermute | solution.py:216
  28.2 12.0 %collective-permute-start.25 = (bf16[64,512]{1,0:T(8,128)(2,1)S(1)}, bf16[64,512]{1,0:T(8,128)(2,1)S(1)}, u32[]{:S(2)}, u32[]{:S(2)}) collective-permute-start(bf16[64,512]{1,0:T(8,128)(2,1)S(1)} %late_tile.6.refs_0_), channel_id=1, source_target_pairs={{16,26},{17,27},{18,24},{19,25},{20,30},{21,31},{22,28},{23,29}} | collective-permute-start | bytes 196616 | tf_op jit(solution)/shard_map/ppermute | solution.py:216
  29.5 12.2 %collective-permute-start.27 = (bf16[64,512]{1,0:T(8,128)(2,1)S(1)}, bf16[64,512]{1,0:T(8,128)(2,1)S(1)}, u32[]{:S(2)}, u32[]{:S(2)}) collective-permute-start(bf16[64,512]{1,0:T(8,128)(2,1)S(1)} %late_tile.6.refs_0_), channel_id=1, source_target_pairs={{16,30},{17,31},{18,28},{19,29},{20,26},{21,27},{22,24},{23,25},{2... | collective-permute-start | bytes 196616 | tf_op jit(solution)/shard_map/ppermute | solution.py:216
  33.6 8.8 %collective-permute-start.29 = (bf16[64,512]{1,0:T(8,128)(2,1)S(1)}, bf16[64,512]{1,0:T(8,128)(2,1)S(1)}, u32[]{:S(2)}, u32[]{:S(2)}) collective-permute-start(bf16[64,512]{1,0:T(8,128)(2,1)S(1)} %late_tile.6.refs_0_), channel_id=1, source_target_pairs={{16,24},{17,25},{18,26},{19,27},{20,28},{21,29},{22,30},{23,31},{2... | collective-permute-start | bytes 196616 | tf_op jit(solution)/shard_map/ppermute | solution.py:216
  39.0 3.6 %collective-permute-start.24 = (bf16[64,512]{1,0:T(8,128)(2,1)S(1)}, bf16[64,512]{1,0:T(8,128)(2,1)S(1)}, u32[]{:S(2)}, u32[]{:S(2)}) collective-permute-start(bf16[64,512]{1,0:T(8,128)(2,1)S(1)} %collective-permute-done.23.refs_0_), channel_id=1, source_target_pairs={{0,1},{1,0},{2,3},{3,2},{4,5},{5,4},{6,7},{7,6},{8,9},{9,8},{10,11... | collective-permute-start | bytes 196616 | tf_op jit(solution)/shard_map/ppermute | solution.py:205
  40.2 2.8 %collective-permute-start.26 = (bf16[64,512]{1,0:T(8,128)(2,1)S(1)}, bf16[64,512]{1,0:T(8,128)(2,1)S(1)}, u32[]{:S(2)}, u32[]{:S(2)}) collective-permute-start(bf16[64,512]{1,0:T(8,128)(2,1)S(1)} %collective-permute-done.25.refs_2_), channel_id=1, source_target_pairs={{0,1},{1,0},{2,3},{3,2},{4,5},{5,4},{6,7},{7,6},{8,9},{9,8},{10,11... | collective-permute-start | bytes 196616 | tf_op jit(solution)/shard_map/ppermute | solution.py:205
  41.6 1.7 %collective-permute-start.28 = (bf16[64,512]{1,0:T(8,128)(2,1)S(1)}, bf16[64,512]{1,0:T(8,128)(2,1)S(1)}, u32[]{:S(2)}, u32[]{:S(2)}) collective-permute-start(bf16[64,512]{1,0:T(8,128)(2,1)S(1)} %collective-permute-done.27.refs_1_), channel_id=1, source_target_pairs={{0,1},{1,0},{2,3},{3,2},{4,5},{5,4},{6,7},{7,6},{8,9},{9,8},{10,11... | collective-permute-start | bytes 196616 | tf_op jit(solution)/shard_map/ppermute | solution.py:205
  (9 other events, 16.8 us)

commit v7 on v6

--- a/solution.py
+++ b/solution.py
@@ -43,36 +43,36 @@
     return spot < positions, jnp.where(spot < positions, spot, spot - positions)
 
 
-def place_kernel(chips, cols_ref, count_ref, greens_ref, solve_in, source_in, spots_ref, placed_ref, solve_ref, source_ref, sems):
-    slots, positions = greens_ref.shape[2], placed_ref.shape[0]
-    for slot in range(slots):
-        position = position_of(slot, chips, cols_ref)
-        spots_ref[slot] = jnp.where(slot < count_ref[0, 0], position, position + positions)
-
-    @pl.when(lax.axis_index("slab") == 0)
-    def _():
-        copies = [
-            pltpu.make_async_copy(solve_in.at[0, 0], solve_ref, sems.at[slots]),
-            pltpu.make_async_copy(source_in, source_ref, sems.at[slots + 1]),
-        ]
+def place_kernel(chips, cols_in, count_ref, greens_ref, solve_in, source_in, *refs):
+    spots_ref, slots_ref, held_ref, solve_ref, source_ref, cols_ref, sems = refs
+    slots, positions = greens_ref.shape[2], slots_ref.shape[0]
+    table = pltpu.make_async_copy(cols_in, cols_ref, sems.at[0])
+    copies = [
+        pltpu.make_async_copy(greens_ref.at[0, 0], held_ref, sems.at[1]),
+        pltpu.make_async_copy(solve_in.at[0, 0], solve_ref, sems.at[2]),
+        pltpu.make_async_copy(source_in, source_ref, sems.at[3]),
+    ]
+    first = lax.axis_index("slab") == 0
+    table.start()
+
+    @pl.when(first)
+    def _():
         for copy in copies:
             copy.start()
-        if positions > slots:
-            placed_ref[...] = jnp.zeros_like(placed_ref)
-        moves = []
-        for slot in range(slots):
-            used, position = spot_of(spots_ref, slot, positions)
-            move = pltpu.make_async_copy(greens_ref.at[0, 0, slot], placed_ref.at[position], sems.at[slot])
-            moves.append((used, move))
-            pl.when(used)(move.start)
-            if positions == slots:
-
-                @pl.when(jnp.logical_not(used))
-                def _():
-                    placed_ref[position] = jnp.zeros(placed_ref.shape[1:], placed_ref.dtype)
-
-        for used, move in moves:
-            pl.when(used)(move.wait)
+
+    for position in range(positions):
+        slots_ref[position] = -1
+    table.wait()
+    for slot in range(slots):
+        position, used = position_of(slot, chips, cols_ref), slot < count_ref[0, 0]
+        spots_ref[slot] = jnp.where(used, position, position + positions)
+
+        @pl.when(used)
+        def _():
+            slots_ref[position] = slot
+
+    @pl.when(first)
+    def _():
         for copy in copies:
             copy.wait()
 
@@ -83,13 +83,17 @@
         functools.partial(place_kernel, chips),
         out_shape=(
             pltpu.SMEM((slots,), jnp.int32),
-            pltpu.VMEM((chips * CORES, rows, depth), greens.dtype),
+            pltpu.SMEM((chips * CORES,), jnp.int32),
+            pltpu.VMEM((slots, rows, depth), greens.dtype),
             pltpu.VMEM(solve.shape[2:], solve.dtype),
             pltpu.VMEM(source.shape, source.dtype),
         ),
-        in_specs=[IN_SMEM] * 2 + [ANYWHERE] * 3,
-        out_specs=(IN_SMEM,) + (IN_VMEM,) * 3,
-        scratch_shapes=[pltpu.SemaphoreType.DMA((slots + 2,))],
+        in_specs=[ANYWHERE, IN_SMEM] + [ANYWHERE] * 3,
+        out_specs=(IN_SMEM,) * 2 + (IN_VMEM,) * 3,
+        scratch_shapes=[
+            pltpu.SMEM(cols.shape, cols.dtype),
+            pltpu.SemaphoreType.DMA((4,)),
+        ],
         compiler_params=params(),
         cost_estimate=pl.CostEstimate(flops=0, bytes_accessed=2 * greens.size * 2, transcendentals=0),
         name="place",
@@ -149,56 +153,66 @@
     )(spots, greens, solve, source)
 
 
-def products(tiles, positions, placed_ref, folded, total):
+def products(tiles, positions, placed_ref, slots_ref, total):
     for tile, position in zip(tiles, positions):
-        dims = LAST_FIRST if folded else LAST_LAST
-        total += lax.dot_general(tile[...], placed_ref[position], dims, preferred_element_type=jnp.float32)
+        if slots_ref is None:
+            total += jnp.dot(tile[...], placed_ref[position], preferred_element_type=jnp.float32)
+        else:
+            slot = slots_ref[position]
+            used = jnp.where(slot >= 0, tile[...], jnp.zeros_like(tile))
+            total += lax.dot_general(
+                used, placed_ref[jnp.maximum(slot, 0)], LAST_LAST, preferred_element_type=jnp.float32
+            )
     return total
 
 
-def early_kernel(section, positions, placed_ref, before_ref, *refs):
-    tiles, total_ref = refs[:-1], refs[-1]
+def early_kernel(section, positions, *refs):
+    slots_ref, refs = (refs[0], refs[1:]) if section == 0 else (None, refs)
+    placed_ref, before_ref, tiles, total_ref = refs[0], refs[1], refs[2:-1], refs[-1]
 
     @pl.when(lax.axis_index("slab") == section)
     def _():
         before = before_ref[...].astype(jnp.float32)
-        total_ref[...] = products(tiles, positions, placed_ref, section > 0, before)
-
-
-def early(section, positions, placed, before, tiles):
+        total_ref[...] = products(tiles, positions, placed_ref, slots_ref, before)
+
+
+def early(section, positions, slots, placed, before, tiles):
+    scalars = [slots] if section == 0 else []
     return pl.pallas_call(
         functools.partial(early_kernel, section, positions),
         out_shape=pltpu.VMEM(before.shape, jnp.float32),
-        in_specs=[IN_VMEM] * (2 + len(tiles)),
+        in_specs=[IN_SMEM] * len(scalars) + [IN_VMEM] * (2 + len(tiles)),
         out_specs=IN_VMEM,
         compiler_params=params(),
         name="early_tiles",
-    )(placed, before, *tiles)
-
-
-def late_kernel(section, position, placed_ref, total_ref, tile_ref, *refs):
-    solve_ref, trace_ref = refs[0], refs[-1]
+    )(*scalars, placed, before, *tiles)
+
+
+def late_kernel(section, position, *refs):
+    slots_ref, refs = (refs[0], refs[1:]) if section == 0 else (None, refs)
+    placed_ref, total_ref, tile_ref, solve_ref, trace_ref = *refs[:3], refs[3], refs[-1]
 
     @pl.when(lax.axis_index("slab") == section)
     def _():
-        total = products([tile_ref], [position], placed_ref, section > 0, total_ref[...])
+        total = products([tile_ref], [position], placed_ref, slots_ref, total_ref[...])
         if section == 0:
             coupled = total.astype(jnp.bfloat16)
             total = lax.dot_general(coupled, solve_ref[...], LAST_LAST, preferred_element_type=jnp.float32)
         trace_ref[...] = total.astype(trace_ref.dtype)
 
 
-def late(section, position, placed, total, tile, solve, trace):
-    operands = (placed, total, tile, solve, trace) if section == 0 else (placed, total, tile, trace)
+def late(section, position, slots, placed, total, tile, solve, trace):
+    scalars = [slots] if section == 0 else []
+    operands = [placed, total, tile, *([solve] if section == 0 else []), trace]
     return pl.pallas_call(
         functools.partial(late_kernel, section, position),
         out_shape=pltpu.VMEM(trace.shape, trace.dtype),
-        in_specs=[IN_VMEM] * len(operands),
+        in_specs=[IN_SMEM] * len(scalars) + [IN_VMEM] * len(operands),
         out_specs=IN_VMEM,
-        input_output_aliases={len(operands) - 1: 0},
+        input_output_aliases={len(scalars) + len(operands) - 1: 0},
         compiler_params=params(),
         name="late_tile",
-    )(*operands)
+    )(*scalars, *operands)
 
 
 def swapped(tile, rows):
@@ -231,10 +245,10 @@
     chips, last = rows // CORES, slabs - 1
     steps = [step_of(order, chips) for order in range(chips)]
     entering, source = inflow.T, forcing[0].T
-    greens, self_solve, source = (
-        pltpu.with_memory_space_constraint(array, pltpu.HBM) for array in (greens, self_solve, source)
+    kept_cols, greens, self_solve, source = (
+        pltpu.with_memory_space_constraint(array, pltpu.HBM) for array in (kept_cols, greens, self_solve, source)
     )
-    spots, placed, solve, base = place(chips, kept_cols, counts, greens, self_solve, source)
+    spots, slots, placed, solve, base = place(chips, kept_cols, counts, greens, self_solve, source)
     given = (rows, spots, greens, self_solve, source)
     ready = fold(last, *given) if last > 0 else ()
     trace = jnp.zeros(entering.shape, jnp.bfloat16)
@@ -255,14 +269,14 @@
                 placed, base = ready
         if section == 0:
             other = [swapped(tile, rows) for tile in own[:-1]]
-            held = [(own[0], orders[0]), (other[0], chips + orders[0])] + [(own[i], orders[i]) for i in range(1, chips - 1)]
+            held = [(own[0], orders[0]), (other[0], chips + orders[0])]
             tiles, positions = zip(*held)
-            total = early(section, positions, placed, base, tiles)
-            own[-1], total = lax.optimization_barrier((own[-1], total))
+            total = early(section, positions, slots, placed, base, tiles)
+            own[1], total = lax.optimization_barrier((own[1], total))
             other.append(swapped(own[-1], rows))
-            held = [(other[i], chips + orders[i]) for i in range(1, chips - 1)] + [(own[-1], orders[-1])]
+            held = [(own[i], orders[i]) for i in range(1, chips)] + [(other[i], chips + orders[i]) for i in range(1, chips - 1)]
             tiles, positions = zip(*held)
-            total = early(section, positions, placed, total, tiles)
+            total = early(section, positions, slots, placed, total, tiles)
             arriving = [(None, chips + orders[-1])]
         else:
             other = [swapped(tile, rows) for tile in own]
@@ -272,8 +286,8 @@
             total = base
             for first in [0, *range(3, len(arriving) - 1, 2)]:
                 tiles, positions = zip(*arriving[first : first + 3 if first == 0 else first + 2])
-                total = early(section, positions, placed, total, tiles)
-        trace = late(section, arriving[-1][1], placed, total, other[-1], solve, trace)
+                total = early(section, positions, slots, placed, total, tiles)
+        trace = late(section, arriving[-1][1], slots, placed, total, other[-1], solve, trace)
     return trace.T[None]
 
 

time: 44.7 us -> 44.5 us (level)
  local copies, waits for them, and re-layouts: 1.29 us -> 0.65 us
    ppermute x16, starting transfers between devices: 6.27 us -> 5.56 us  [swapped(): return lax.ppermute(tile, 'row', [(r, r ^ 1) for r in range(rows)])]
    unnamed x5 -> x3, local copies, waits for them, and re-layouts: 1.29 us -> 0.64 us
    ppermute x15, starting transfers between devices: 20.3 us -> 20.9 us  [sent(): return lax.ppermute(tile, ('slab', 'row'), pairs)]
  transfers between devices with their start and end apart: 31 -> 31, of which waited for: 13 -> 14; matrix products, arithmetic and copies ran while one was open for 0% -> 0% of each run, Pallas kernels for 19% -> 19%
where the time goes in v7:
time: 44.5 us; the launch traced here: 44.2 us
  starting transfers between devices  26.4 us (59%)
  Pallas kernels  8.77 us (20%)
  waiting for transfers between devices  7.53 us (17%)
  between operations  0.86 us (2%)
  local copies, waits for them, and re-layouts  0.65 us (1%)
    ppermute x15, starting transfers between devices, sent(): return lax.ppermute(tile, ('slab', 'row'), pairs)  20.9 us
    pallas_call x3, Pallas kernels, fold(): pl.pallas_call(functools.partial(fold_kernel, section), out_shape=(pltpu....  6.76 us
    ppermute x16, starting transfers between devices, swapped(): return lax.ppermute(tile, 'row', [(r, r ^ 1) for r in range(rows)])  5.56 us
    ppermute x15, waiting for transfers between devices, sent(): return lax.ppermute(tile, ('slab', 'row'), pairs)  4.56 us
    ppermute x16, waiting for transfers between devices, swapped(): return lax.ppermute(tile, 'row', [(r, r ^ 1) for r in range(rows)])  2.97 us
    pallas_call x11, Pallas kernels, early(): pl.pallas_call(functools.partial(early_kernel, section, positions), out_s...  1 us
  transfers between devices with their start and end apart: 31, of which 14 were waited for; matrix products, arithmetic and copies ran while one was open for 0% of the time, Pallas kernels for 19%

profile of v7, /device:TPU:7, one launch (start us, length us, event | category | flops | bytes accessed | tf_op | source)
XLA Modules:
  0.0 44.2 jit_solution(14462367964190879175)
XLA Ops:
  0.0 0.7 %collective-permute-start = (bf16[64,512]{1,0:T(8,128)(2,1)}, bf16[64,512]{1,0:T(8,128)(2,1)S(1)}, u32[]{:S(2)}, u32[]{:S(2)}) collective-permute-start(bf16[64,512]{1,0:T(8,128)(2,1)} %bitcast.8), channel_id=1, source_target_pairs={{0,4},{1,5},{2,6},{3,7},{4,0},{5,1},{6,2},{7,3},{8,9},{9,8},{10,11... | collective-permute-start | bytes 196616 | tf_op jit(solution)/shard_map/ppermute | solution.py:230
  0.7 0.5 %collective-permute-start.2 = (bf16[64,512]{1,0:T(8,128)(2,1)}, bf16[64,512]{1,0:T(8,128)(2,1)S(1)}, u32[]{:S(2)}, u32[]{:S(2)}) collective-permute-start(bf16[64,512]{1,0:T(8,128)(2,1)} %bitcast.10), channel_id=1, source_target_pairs={{0,2},{1,3},{2,0},{3,1},{4,6},{5,7},{6,4},{7,5},{8,9},{9,8},{10,11... | collective-permute-start | bytes 196616 | tf_op jit(solution)/shard_map/ppermute | solution.py:230
  1.8 0.8 %place.1 = (s32[8]{0:T(128)S(4)}, s32[8]{0:T(128)S(4)}, bf16[8,512,512]{2,1,0:T(8,128)(2,1)S(1)}, bf16[512,512]{1,0:T(8,128)(2,1)S(1)}, bf16[64,512]{1,0:T(8,128)(2,1)S(1)}) custom-call(s32[1,1,8]{2,1,0:T(1,128)} %cols_in.1, s32[1,1]{1,0:T(1,128)S(6)} %copy.16.count_ref, bf16[1,1,8,512,512]{4,3,2,1,0:T(8,128)(2,1)} %greens_ref.7, ...), custom_call_target="tpu_custom_call" | custom-call | bytes 8388608 | tf_op jit(solution)/shard_map/place/pallas_call | solution.py:82
  2.7 6.5 %fold.3 = (bf16[8,512,512]{2,1,0:T(8,128)(2,1)S(1)}, f32[64,512]{1,0:T(8,128)S(1)}) custom-call(s32[8]{0:T(128)S(4)} %get-tuple-element.33.spots_ref, bf16[1,1,8,512,512]{4,3,2,1,0:T(8,128)(2,1)} %greens_ref.7, bf16[1,1,512,512]{3,2,1,0:T(8,128)(2,1)} %solve_in.7, bf16[64,512]{1,0:T(8,128)(2,1)} %bitcast.14), custom_call_target="tpu_custom_call" | custom-call | flops 2147483648 | bytes 8388608 | tf_op jit(solution)/shard_map/fold/pallas_call | solution.py:134
  9.2 0.6 %collective-permute-start.4 = (bf16[64,512]{1,0:T(8,128)(2,1)S(1)}, bf16[64,512]{1,0:T(8,128)(2,1)S(1)}, u32[]{:S(2)}, u32[]{:S(2)}) collective-permute-start(bf16[64,512]{1,0:T(8,128)(2,1)S(1)} %collective-permute-done.refs_3_), channel_id=1, source_target_pairs={{0,1},{1,0},{2,3},{3,2},{4,5},{5,4},{6,7},{7,6},{8,9},{9,8},{10,11... | collective-permute-start | bytes 196616 | tf_op jit(solution)/shard_map/ppermute | solution.py:219
  9.9 0.4 collective-permute-start.6
  11.6 0.7 %collective-permute-start.9 = (bf16[64,512]{1,0:T(8,128)(2,1)S(1)}, bf16[64,512]{1,0:T(8,128)(2,1)S(1)}, u32[]{:S(2)}, u32[]{:S(2)}) collective-permute-start(bf16[64,512]{1,0:T(8,128)(2,1)S(1)} %late_tile.4.refs_3_), channel_id=1, source_target_pairs={{0,10},{1,11},{2,8},{3,9},{4,14},{5,15},{6,12},{7,13}} | collective-permute-start | bytes 196616 | tf_op jit(solution)/shard_map/ppermute | solution.py:230
  12.3 0.7 %collective-permute-start.11 = (bf16[64,512]{1,0:T(8,128)(2,1)S(1)}, bf16[64,512]{1,0:T(8,128)(2,1)S(1)}, u32[]{:S(2)}, u32[]{:S(2)}) collective-permute-start(bf16[64,512]{1,0:T(8,128)(2,1)S(1)} %late_tile.4.refs_3_), channel_id=1, source_target_pairs={{0,14},{1,15},{2,12},{3,13},{4,10},{5,11},{6,8},{7,9}} | collective-permute-start | bytes 196616 | tf_op jit(solution)/shard_map/ppermute | solution.py:230
  13.0 0.7 %collective-permute-start.13 = (bf16[64,512]{1,0:T(8,128)(2,1)S(1)}, bf16[64,512]{1,0:T(8,128)(2,1)S(1)}, u32[]{:S(2)}, u32[]{:S(2)}) collective-permute-start(bf16[64,512]{1,0:T(8,128)(2,1)S(1)} %late_tile.4.refs_3_), channel_id=1, source_target_pairs={{0,8},{1,9},{2,10},{3,11},{4,12},{5,13},{6,14},{7,15}} | collective-permute-start | bytes 196616 | tf_op jit(solution)/shard_map/ppermute | solution.py:230
  15.8 7.5 %collective-permute-start.15 = (bf16[64,512]{1,0:T(8,128)(2,1)S(1)}, bf16[64,512]{1,0:T(8,128)(2,1)S(1)}, u32[]{:S(2)}, u32[]{:S(2)}) collective-permute-start(bf16[64,512]{1,0:T(8,128)(2,1)S(1)} %late_tile.5.refs_3_), channel_id=1, source_target_pairs={{8,20},{9,21},{10,22},{11,23},{12,16},{13,17},{14,18},{15,19},{16,... | collective-permute-start | bytes 196616 | tf_op jit(solution)/shard_map/ppermute | solution.py:230
  23.2 0.7 %collective-permute-start.17 = (bf16[64,512]{1,0:T(8,128)(2,1)S(1)}, bf16[64,512]{1,0:T(8,128)(2,1)S(1)}, u32[]{:S(2)}, u32[]{:S(2)}) collective-permute-start(bf16[64,512]{1,0:T(8,128)(2,1)S(1)} %late_tile.5.refs_3_), channel_id=1, source_target_pairs={{8,18},{9,19},{10,16},{11,17},{12,22},{13,23},{14,20},{15,21}} | collective-permute-start | bytes 196616 | tf_op jit(solution)/shard_map/ppermute | solution.py:230
  23.9 0.7 %collective-permute-start.19 = (bf16[64,512]{1,0:T(8,128)(2,1)S(1)}, bf16[64,512]{1,0:T(8,128)(2,1)S(1)}, u32[]{:S(2)}, u32[]{:S(2)}) collective-permute-start(bf16[64,512]{1,0:T(8,128)(2,1)S(1)} %late_tile.5.refs_3_), channel_id=1, source_target_pairs={{8,22},{9,23},{10,20},{11,21},{12,18},{13,19},{14,16},{15,17}} | collective-permute-start | bytes 196616 | tf_op jit(solution)/shard_map/ppermute | solution.py:230
  24.6 0.7 %collective-permute-start.21 = (bf16[64,512]{1,0:T(8,128)(2,1)S(1)}, bf16[64,512]{1,0:T(8,128)(2,1)S(1)}, u32[]{:S(2)}, u32[]{:S(2)}) collective-permute-start(bf16[64,512]{1,0:T(8,128)(2,1)S(1)} %late_tile.5.refs_3_), channel_id=1, source_target_pairs={{8,16},{9,17},{10,18},{11,19},{12,20},{13,21},{14,22},{15,23}} | collective-permute-start | bytes 196616 | tf_op jit(solution)/shard_map/ppermute | solution.py:230
  25.4 0.5 %collective-permute-start.16 = (bf16[64,512]{1,0:T(8,128)(2,1)S(1)}, bf16[64,512]{1,0:T(8,128)(2,1)S(1)}, u32[]{:S(2)}, u32[]{:S(2)}) collective-permute-start(bf16[64,512]{1,0:T(8,128)(2,1)S(1)} %collective-permute-done.15.refs_2_), channel_id=1, source_target_pairs={{0,1},{1,0},{2,3},{3,2},{4,5},{5,4},{6,7},{7,6},{8,9},{9,8},{10,11... | collective-permute-start | bytes 196616 | tf_op jit(solution)/shard_map/ppermute | solution.py:219
  26.0 0.4 collective-permute-start.20
  27.7 1.3 %collective-permute-start.25 = (bf16[64,512]{1,0:T(8,128)(2,1)S(1)}, bf16[64,512]{1,0:T(8,128)(2,1)S(1)}, u32[]{:S(2)}, u32[]{:S(2)}) collective-permute-start(bf16[64,512]{1,0:T(8,128)(2,1)S(1)} %late_tile.6.refs_3_), channel_id=1, source_target_pairs={{16,26},{17,27},{18,24},{19,25},{20,30},{21,31},{22,28},{23,29}} | collective-permute-start | bytes 196616 | tf_op jit(solution)/shard_map/ppermute | solution.py:230
  29.0 3.8 %collective-permute-start.27 = (bf16[64,512]{1,0:T(8,128)(2,1)S(1)}, bf16[64,512]{1,0:T(8,128)(2,1)S(1)}, u32[]{:S(2)}, u32[]{:S(2)}) collective-permute-start(bf16[64,512]{1,0:T(8,128)(2,1)S(1)} %late_tile.6.refs_3_), channel_id=1, source_target_pairs={{16,30},{17,31},{18,28},{19,29},{20,26},{21,27},{22,24},{23,25},{2... | collective-permute-start | bytes 196616 | tf_op jit(solution)/shard_map/ppermute | solution.py:230
  32.8 2.7 %collective-permute-start.29 = (bf16[64,512]{1,0:T(8,128)(2,1)S(1)}, bf16[64,512]{1,0:T(8,128)(2,1)S(1)}, u32[]{:S(2)}, u32[]{:S(2)}) collective-permute-start(bf16[64,512]{1,0:T(8,128)(2,1)S(1)} %late_tile.6.refs_3_), channel_id=1, source_target_pairs={{16,24},{17,25},{18,26},{19,27},{20,28},{21,29},{22,30},{23,31},{2... | collective-permute-start | bytes 196616 | tf_op jit(solution)/shard_map/ppermute | solution.py:230
  35.5 3.2 %collective-permute-done.23.refs_2_ = bf16[64,512]{1,0:T(8,128)(2,1)S(1)} collective-permute-done((bf16[64,512]{1,0:T(8,128)(2,1)S(1)}, bf16[64,512]{1,0:T(8,128)(2,1)S(1)}, u32[]{:S(2)}, u32[]{:S(2)}) %collective-permute-start.23) | collective-permute-done | bytes 65568 | tf_op jit(solution)/shard_map/ppermute | solution.py:230
  38.7 1.0 %collective-permute-start.24 = (bf16[64,512]{1,0:T(8,128)(2,1)S(1)}, bf16[64,512]{1,0:T(8,128)(2,1)S(1)}, u32[]{:S(2)}, u32[]{:S(2)}) collective-permute-start(bf16[64,512]{1,0:T(8,128)(2,1)S(1)} %collective-permute-done.23.refs_2_), channel_id=1, source_target_pairs={{0,1},{1,0},{2,3},{3,2},{4,5},{5,4},{6,7},{7,6},{8,9},{9,8},{10,11... | collective-permute-start | bytes 196616 | tf_op jit(solution)/shard_map/ppermute | solution.py:219
  39.7 1.3 %collective-permute-done.27.refs_3_ = bf16[64,512]{1,0:T(8,128)(2,1)S(1)} collective-permute-done((bf16[64,512]{1,0:T(8,128)(2,1)S(1)}, bf16[64,512]{1,0:T(8,128)(2,1)S(1)}, u32[]{:S(2)}, u32[]{:S(2)}) %collective-permute-start.27) | collective-permute-done | bytes 65568 | tf_op jit(solution)/shard_map/ppermute | solution.py:230
  40.9 0.7 %collective-permute-start.28 = (bf16[64,512]{1,0:T(8,128)(2,1)S(1)}, bf16[64,512]{1,0:T(8,128)(2,1)S(1)}, u32[]{:S(2)}, u32[]{:S(2)}) collective-permute-start(bf16[64,512]{1,0:T(8,128)(2,1)S(1)} %collective-permute-done.27.refs_3_), channel_id=1, source_target_pairs={{0,1},{1,0},{2,3},{3,2},{4,5},{5,4},{6,7},{7,6},{8,9},{9,8},{10,11... | collective-permute-start | bytes 196616 | tf_op jit(solution)/shard_map/ppermute | solution.py:219
  41.8 0.5 %collective-permute-start.30 = (bf16[64,512]{1,0:T(8,128)(2,1)S(1)}, bf16[64,512]{1,0:T(8,128)(2,1)S(1)}, u32[]{:S(2)}, u32[]{:S(2)}) collective-permute-start(bf16[64,512]{1,0:T(8,128)(2,1)S(1)} %collective-permute-done.29.refs_3_), channel_id=1, source_target_pairs={{0,1},{1,0},{2,3},{3,2},{4,5},{5,4},{6,7},{7,6},{8,9},{9,8},{10,11... | collective-permute-start | bytes 196616 | tf_op jit(solution)/shard_map/ppermute | solution.py:219
  43.6 0.6 %copy.15 = bf16[1,512,64]{1,2,0:T(8,128)(2,1)} copy(bf16[1,512,64]{1,2,0:T(8,128)(2,1)S(1)} %bitcast.7) | data formatting | bytes 131072
  (61 shorter events, 6.3 us)
Async XLA Ops:
  0.0 9.2 %collective-permute-start = (bf16[64,512]{1,0:T(8,128)(2,1)}, bf16[64,512]{1,0:T(8,128)(2,1)S(1)}, u32[]{:S(2)}, u32[]{:S(2)}) collective-permute-start(bf16[64,512]{1,0:T(8,128)(2,1)} %bitcast.8), channel_id=1, source_target_pairs={{0,4},{1,5},{2,6},{3,7},{4,0},{5,1},{6,2},{7,3},{8,9},{9,8},{10,11... | collective-permute-start | bytes 196616 | tf_op jit(solution)/shard_map/ppermute | solution.py:230
  0.7 9.6 %collective-permute-start.1 = (bf16[64,512]{1,0:T(8,128)(2,1)}, bf16[64,512]{1,0:T(8,128)(2,1)S(1)}, u32[]{:S(2)}, u32[]{:S(2)}) collective-permute-start(bf16[64,512]{1,0:T(8,128)(2,1)} %bitcast.9), channel_id=1, source_target_pairs={{0,1},{1,0},{2,3},{3,2},{4,5},{5,4},{6,7},{7,6},{8,9},{9,8},{10,11... | collective-permute-start | bytes 196616 | tf_op jit(solution)/shard_map/ppermute | solution.py:219
  0.7 9.1 %collective-permute-start.2 = (bf16[64,512]{1,0:T(8,128)(2,1)}, bf16[64,512]{1,0:T(8,128)(2,1)S(1)}, u32[]{:S(2)}, u32[]{:S(2)}) collective-permute-start(bf16[64,512]{1,0:T(8,128)(2,1)} %bitcast.10), channel_id=1, source_target_pairs={{0,2},{1,3},{2,0},{3,1},{4,6},{5,7},{6,4},{7,5},{8,9},{9,8},{10,11... | collective-permute-start | bytes 196616 | tf_op jit(solution)/shard_map/ppermute | solution.py:230
  1.2 8.7 %collective-permute-start.3 = (bf16[64,512]{1,0:T(8,128)(2,1)}, bf16[64,512]{1,0:T(8,128)(2,1)S(1)}, u32[]{:S(2)}, u32[]{:S(2)}) collective-permute-start(bf16[64,512]{1,0:T(8,128)(2,1)} %bitcast.11), channel_id=1, source_target_pairs={{0,6},{1,7},{2,4},{3,5},{4,2},{5,3},{6,0},{7,1},{8,9},{9,8},{10,11... | collective-permute-start | bytes 196616 | tf_op jit(solution)/shard_map/ppermute | solution.py:230
  9.2 1.5 %collective-permute-start.4 = (bf16[64,512]{1,0:T(8,128)(2,1)S(1)}, bf16[64,512]{1,0:T(8,128)(2,1)S(1)}, u32[]{:S(2)}, u32[]{:S(2)}) collective-permute-start(bf16[64,512]{1,0:T(8,128)(2,1)S(1)} %collective-permute-done.refs_3_), channel_id=1, source_target_pairs={{0,1},{1,0},{2,3},{3,2},{4,5},{5,4},{6,7},{7,6},{8,9},{9,8},{10,11... | collective-permute-start | bytes 196616 | tf_op jit(solution)/shard_map/ppermute | solution.py:219
  9.9 1.3 %collective-permute-start.6 = (bf16[64,512]{1,0:T(8,128)(2,1)S(1)}, bf16[64,512]{1,0:T(8,128)(2,1)S(1)}, u32[]{:S(2)}, u32[]{:S(2)}) collective-permute-start(bf16[64,512]{1,0:T(8,128)(2,1)S(1)} %collective-permute-done.3.refs_5_), channel_id=1, source_target_pairs={{0,1},{1,0},{2,3},{3,2},{4,5},{5,4},{6,7},{7,6},{8,9},{9,8},{10,11... | collective-permute-start | bytes 196616 | tf_op jit(solution)/shard_map/ppermute | solution.py:219
  11.2 2.5 %collective-permute-start.7 = (bf16[64,512]{1,0:T(8,128)(2,1)S(1)}, bf16[64,512]{1,0:T(8,128)(2,1)S(1)}, u32[]{:S(2)}, u32[]{:S(2)}) collective-permute-start(bf16[64,512]{1,0:T(8,128)(2,1)S(1)} %late_tile.4.refs_3_), channel_id=1, source_target_pairs={{0,12},{1,13},{2,14},{3,15},{4,8},{5,9},{6,10},{7,11},{8,16},{9,17... | collective-permute-start | bytes 196616 | tf_op jit(solution)/shard_map/ppermute | solution.py:230
  11.6 2.3 %collective-permute-start.9 = (bf16[64,512]{1,0:T(8,128)(2,1)S(1)}, bf16[64,512]{1,0:T(8,128)(2,1)S(1)}, u32[]{:S(2)}, u32[]{:S(2)}) collective-permute-start(bf16[64,512]{1,0:T(8,128)(2,1)S(1)} %late_tile.4.refs_3_), channel_id=1, source_target_pairs={{0,10},{1,11},{2,8},{3,9},{4,14},{5,15},{6,12},{7,13}} | collective-permute-start | bytes 196616 | tf_op jit(solution)/shard_map/ppermute | solution.py:230
  12.3 2.1 %collective-permute-start.11 = (bf16[64,512]{1,0:T(8,128)(2,1)S(1)}, bf16[64,512]{1,0:T(8,128)(2,1)S(1)}, u32[]{:S(2)}, u32[]{:S(2)}) collective-permute-start(bf16[64,512]{1,0:T(8,128)(2,1)S(1)} %late_tile.4.refs_3_), channel_id=1, source_target_pairs={{0,14},{1,15},{2,12},{3,13},{4,10},{5,11},{6,8},{7,9}} | collective-permute-start | bytes 196616 | tf_op jit(solution)/shard_map/ppermute | solution.py:230
  13.0 1.5 %collective-permute-start.13 = (bf16[64,512]{1,0:T(8,128)(2,1)S(1)}, bf16[64,512]{1,0:T(8,128)(2,1)S(1)}, u32[]{:S(2)}, u32[]{:S(2)}) collective-permute-start(bf16[64,512]{1,0:T(8,128)(2,1)S(1)} %late_tile.4.refs_3_), channel_id=1, source_target_pairs={{0,8},{1,9},{2,10},{3,11},{4,12},{5,13},{6,14},{7,15}} | collective-permute-start | bytes 196616 | tf_op jit(solution)/shard_map/ppermute | solution.py:230
  15.8 9.6 %collective-permute-start.15 = (bf16[64,512]{1,0:T(8,128)(2,1)S(1)}, bf16[64,512]{1,0:T(8,128)(2,1)S(1)}, u32[]{:S(2)}, u32[]{:S(2)}) collective-permute-start(bf16[64,512]{1,0:T(8,128)(2,1)S(1)} %late_tile.5.refs_3_), channel_id=1, source_target_pairs={{8,20},{9,21},{10,22},{11,23},{12,16},{13,17},{14,18},{15,19},{16,... | collective-permute-start | bytes 196616 | tf_op jit(solution)/shard_map/ppermute | solution.py:230
  23.2 2.7 %collective-permute-start.17 = (bf16[64,512]{1,0:T(8,128)(2,1)S(1)}, bf16[64,512]{1,0:T(8,128)(2,1)S(1)}, u32[]{:S(2)}, u32[]{:S(2)}) collective-permute-start(bf16[64,512]{1,0:T(8,128)(2,1)S(1)} %late_tile.5.refs_3_), channel_id=1, source_target_pairs={{8,18},{9,19},{10,16},{11,17},{12,22},{13,23},{14,20},{15,21}} | collective-permute-start | bytes 196616 | tf_op jit(solution)/shard_map/ppermute | solution.py:230
  23.9 2.1 %collective-permute-start.19 = (bf16[64,512]{1,0:T(8,128)(2,1)S(1)}, bf16[64,512]{1,0:T(8,128)(2,1)S(1)}, u32[]{:S(2)}, u32[]{:S(2)}) collective-permute-start(bf16[64,512]{1,0:T(8,128)(2,1)S(1)} %late_tile.5.refs_3_), channel_id=1, source_target_pairs={{8,22},{9,23},{10,20},{11,21},{12,18},{13,19},{14,16},{15,17}} | collective-permute-start | bytes 196616 | tf_op jit(solution)/shard_map/ppermute | solution.py:230
  24.6 1.9 %collective-permute-start.21 = (bf16[64,512]{1,0:T(8,128)(2,1)S(1)}, bf16[64,512]{1,0:T(8,128)(2,1)S(1)}, u32[]{:S(2)}, u32[]{:S(2)}) collective-permute-start(bf16[64,512]{1,0:T(8,128)(2,1)S(1)} %late_tile.5.refs_3_), channel_id=1, source_target_pairs={{8,16},{9,17},{10,18},{11,19},{12,20},{13,21},{14,22},{15,23}} | collective-permute-start | bytes 196616 | tf_op jit(solution)/shard_map/ppermute | solution.py:230
  25.4 1.4 %collective-permute-start.16 = (bf16[64,512]{1,0:T(8,128)(2,1)S(1)}, bf16[64,512]{1,0:T(8,128)(2,1)S(1)}, u32[]{:S(2)}, u32[]{:S(2)}) collective-permute-start(bf16[64,512]{1,0:T(8,128)(2,1)S(1)} %collective-permute-done.15.refs_2_), channel_id=1, source_target_pairs={{0,1},{1,0},{2,3},{3,2},{4,5},{5,4},{6,7},{7,6},{8,9},{9,8},{10,11... | collective-permute-start | bytes 196616 | tf_op jit(solution)/shard_map/ppermute | solution.py:219
  26.0 1.3 %collective-permute-start.20 = (bf16[64,512]{1,0:T(8,128)(2,1)S(1)}, bf16[64,512]{1,0:T(8,128)(2,1)S(1)}, u32[]{:S(2)}, u32[]{:S(2)}) collective-permute-start(bf16[64,512]{1,0:T(8,128)(2,1)S(1)} %collective-permute-done.19.refs_3_), channel_id=1, source_target_pairs={{0,1},{1,0},{2,3},{3,2},{4,5},{5,4},{6,7},{7,6},{8,9},{9,8},{10,11... | collective-permute-start | bytes 196616 | tf_op jit(solution)/shard_map/ppermute | solution.py:219
  27.7 11.0 %collective-permute-start.23 = (bf16[64,512]{1,0:T(8,128)(2,1)S(1)}, bf16[64,512]{1,0:T(8,128)(2,1)S(1)}, u32[]{:S(2)}, u32[]{:S(2)}) collective-permute-start(bf16[64,512]{1,0:T(8,128)(2,1)S(1)} %late_tile.6.refs_3_), channel_id=1, source_target_pairs={{16,28},{17,29},{18,30},{19,31},{20,24},{21,25},{22,26},{23,27},{2... | collective-permute-start | bytes 196616 | tf_op jit(solution)/shard_map/ppermute | solution.py:230
  27.7 12.0 %collective-permute-start.25 = (bf16[64,512]{1,0:T(8,128)(2,1)S(1)}, bf16[64,512]{1,0:T(8,128)(2,1)S(1)}, u32[]{:S(2)}, u32[]{:S(2)}) collective-permute-start(bf16[64,512]{1,0:T(8,128)(2,1)S(1)} %late_tile.6.refs_3_), channel_id=1, source_target_pairs={{16,26},{17,27},{18,24},{19,25},{20,30},{21,31},{22,28},{23,29}} | collective-permute-start | bytes 196616 | tf_op jit(solution)/shard_map/ppermute | solution.py:230
  29.0 12.0 %collective-permute-start.27 = (bf16[64,512]{1,0:T(8,128)(2,1)S(1)}, bf16[64,512]{1,0:T(8,128)(2,1)S(1)}, u32[]{:S(2)}, u32[]{:S(2)}) collective-permute-start(bf16[64,512]{1,0:T(8,128)(2,1)S(1)} %late_tile.6.refs_3_), channel_id=1, source_target_pairs={{16,30},{17,31},{18,28},{19,29},{20,26},{21,27},{22,24},{23,25},{2... | collective-permute-start | bytes 196616 | tf_op jit(solution)/shard_map/ppermute | solution.py:230
  32.8 9.0 %collective-permute-start.29 = (bf16[64,512]{1,0:T(8,128)(2,1)S(1)}, bf16[64,512]{1,0:T(8,128)(2,1)S(1)}, u32[]{:S(2)}, u32[]{:S(2)}) collective-permute-start(bf16[64,512]{1,0:T(8,128)(2,1)S(1)} %late_tile.6.refs_3_), channel_id=1, source_target_pairs={{16,24},{17,25},{18,26},{19,27},{20,28},{21,29},{22,30},{23,31},{2... | collective-permute-start | bytes 196616 | tf_op jit(solution)/shard_map/ppermute | solution.py:230
  38.7 3.6 %collective-permute-start.24 = (bf16[64,512]{1,0:T(8,128)(2,1)S(1)}, bf16[64,512]{1,0:T(8,128)(2,1)S(1)}, u32[]{:S(2)}, u32[]{:S(2)}) collective-permute-start(bf16[64,512]{1,0:T(8,128)(2,1)S(1)} %collective-permute-done.23.refs_2_), channel_id=1, source_target_pairs={{0,1},{1,0},{2,3},{3,2},{4,5},{5,4},{6,7},{7,6},{8,9},{9,8},{10,11... | collective-permute-start | bytes 196616 | tf_op jit(solution)/shard_map/ppermute | solution.py:219
  39.7 3.0 %collective-permute-start.26 = (bf16[64,512]{1,0:T(8,128)(2,1)S(1)}, bf16[64,512]{1,0:T(8,128)(2,1)S(1)}, u32[]{:S(2)}, u32[]{:S(2)}) collective-permute-start(bf16[64,512]{1,0:T(8,128)(2,1)S(1)} %collective-permute-done.25.refs_4_), channel_id=1, source_target_pairs={{0,1},{1,0},{2,3},{3,2},{4,5},{5,4},{6,7},{7,6},{8,9},{9,8},{10,11... | collective-permute-start | bytes 196616 | tf_op jit(solution)/shard_map/ppermute | solution.py:219
  40.9 2.1 %collective-permute-start.28 = (bf16[64,512]{1,0:T(8,128)(2,1)S(1)}, bf16[64,512]{1,0:T(8,128)(2,1)S(1)}, u32[]{:S(2)}, u32[]{:S(2)}) collective-permute-start(bf16[64,512]{1,0:T(8,128)(2,1)S(1)} %collective-permute-done.27.refs_3_), channel_id=1, source_target_pairs={{0,1},{1,0},{2,3},{3,2},{4,5},{5,4},{6,7},{7,6},{8,9},{9,8},{10,11... | collective-permute-start | bytes 196616 | tf_op jit(solution)/shard_map/ppermute | solution.py:219
  41.8 1.6 %collective-permute-start.30 = (bf16[64,512]{1,0:T(8,128)(2,1)S(1)}, bf16[64,512]{1,0:T(8,128)(2,1)S(1)}, u32[]{:S(2)}, u32[]{:S(2)}) collective-permute-start(bf16[64,512]{1,0:T(8,128)(2,1)S(1)} %collective-permute-done.29.refs_3_), channel_id=1, source_target_pairs={{0,1},{1,0},{2,3},{3,2},{4,5},{5,4},{6,7},{7,6},{8,9},{9,8},{10,11... | collective-permute-start | bytes 196616 | tf_op jit(solution)/shard_map/ppermute | solution.py:219
  (8 other events, 16.6 us)

commit v8 on v7

--- a/solution.py
+++ b/solution.py
@@ -38,13 +38,8 @@
     return jnp.where(column % CORES == core, 0, chips) + order_of(chip ^ (column // CORES), chips)
 
 
-def spot_of(spots_ref, slot, positions):
-    spot = spots_ref[slot]
-    return spot < positions, jnp.where(spot < positions, spot, spot - positions)
-
-
 def place_kernel(chips, cols_in, count_ref, greens_ref, solve_in, source_in, *refs):
-    spots_ref, slots_ref, held_ref, solve_ref, source_ref, cols_ref, sems = refs
+    slots_ref, held_ref, solve_ref, source_ref, cols_ref, sems = refs
     slots, positions = greens_ref.shape[2], slots_ref.shape[0]
     table = pltpu.make_async_copy(cols_in, cols_ref, sems.at[0])
     copies = [
@@ -64,12 +59,10 @@
         slots_ref[position] = -1
     table.wait()
     for slot in range(slots):
-        position, used = position_of(slot, chips, cols_ref), slot < count_ref[0, 0]
-        spots_ref[slot] = jnp.where(used, position, position + positions)
-
-        @pl.when(used)
+
+        @pl.when(slot < count_ref[0, 0])
         def _():
-            slots_ref[position] = slot
+            slots_ref[position_of(slot, chips, cols_ref)] = slot
 
     @pl.when(first)
     def _():
@@ -82,14 +75,13 @@
     return pl.pallas_call(
         functools.partial(place_kernel, chips),
         out_shape=(
-            pltpu.SMEM((slots,), jnp.int32),
             pltpu.SMEM((chips * CORES,), jnp.int32),
             pltpu.VMEM((slots, rows, depth), greens.dtype),
             pltpu.VMEM(solve.shape[2:], solve.dtype),
             pltpu.VMEM(source.shape, source.dtype),
         ),
         in_specs=[ANYWHERE, IN_SMEM] + [ANYWHERE] * 3,
-        out_specs=(IN_SMEM,) * 2 + (IN_VMEM,) * 3,
+        out_specs=(IN_SMEM,) + (IN_VMEM,) * 3,
         scratch_shapes=[
             pltpu.SMEM(cols.shape, cols.dtype),
             pltpu.SemaphoreType.DMA((4,)),
@@ -100,57 +92,50 @@
     )(cols, count, greens, solve, source)
 
 
-def fold_kernel(section, spots_ref, greens_ref, solve_in, source_in, folded_ref, base_ref, held_ref, solve_ref, source_ref, sems):
-    slots, positions = greens_ref.shape[2], folded_ref.shape[0]
-
+def fold_kernel(section, slots_ref, greens_ref, solve_in, source_in, folded_ref, base_ref, held_ref, solve_ref, source_ref, sems):
     @pl.when(lax.axis_index("slab") == section)
     def _():
         copies = [
-            pltpu.make_async_copy(solve_in.at[0, 0], solve_ref, sems.at[slots]),
-            pltpu.make_async_copy(source_in, source_ref, sems.at[slots + 1]),
-        ]
-        copies += [
-            pltpu.make_async_copy(greens_ref.at[0, 0, slot], held_ref.at[slot], sems.at[slot]) for slot in range(slots)
+            pltpu.make_async_copy(greens_ref.at[0, 0], held_ref, sems.at[0]),
+            pltpu.make_async_copy(solve_in.at[0, 0], solve_ref, sems.at[1]),
+            pltpu.make_async_copy(source_in, source_ref, sems.at[2]),
         ]
         for copy in copies:
             copy.start()
-        if positions > slots:
-            folded_ref[...] = jnp.zeros_like(folded_ref)
         for copy in copies:
             copy.wait()
         base_ref[...] = lax.dot_general(source_ref[...], solve_ref[...], LAST_LAST, preferred_element_type=jnp.float32)
 
-        def fold_slot(slot, carry):
-            solved = lax.dot_general(held_ref[slot], solve_ref[...], FIRST_LAST, preferred_element_type=jnp.float32)
-            used, position = spot_of(spots_ref, slot, positions)
-            folded_ref[position] = jnp.where(used, solved, jnp.zeros_like(solved)).astype(folded_ref.dtype)
-            return carry
-
-        lax.fori_loop(0, slots, fold_slot, 0)
-
-
-def fold(section, positions, spots, greens, solve, source):
-    slots, rows, depth = greens.shape[2:]
+        for position in range(folded_ref.shape[0]):
+            slot = slots_ref[position]
+            solved = lax.dot_general(
+                held_ref[jnp.maximum(slot, 0)], solve_ref[...], FIRST_LAST, preferred_element_type=jnp.float32
+            )
+            folded_ref[position] = jnp.where(slot >= 0, solved, jnp.zeros_like(solved)).astype(folded_ref.dtype)
+
+
+def fold(section, slots, greens, solve, source):
+    held, rows, depth = greens.shape[2:]
     return pl.pallas_call(
         functools.partial(fold_kernel, section),
         out_shape=(
-            pltpu.VMEM((positions, depth, rows), greens.dtype),
+            pltpu.VMEM((*slots.shape, depth, rows), greens.dtype),
             pltpu.VMEM(source.shape, jnp.float32),
         ),
         in_specs=[IN_SMEM] + [ANYWHERE] * 3,
         out_specs=(IN_VMEM,) * 2,
         scratch_shapes=[
-            pltpu.VMEM((slots, rows, depth), greens.dtype),
+            pltpu.VMEM((held, rows, depth), greens.dtype),
             pltpu.VMEM(solve.shape[2:], solve.dtype),
             pltpu.VMEM(source.shape, source.dtype),
-            pltpu.SemaphoreType.DMA((slots + 2,)),
+            pltpu.SemaphoreType.DMA((3,)),
         ],
         compiler_params=params(),
         cost_estimate=pl.CostEstimate(
             flops=2 * greens.size * rows, bytes_accessed=2 * greens.size * 2, transcendentals=0
         ),
         name="fold",
-    )(spots, greens, solve, source)
+    )(slots, greens, solve, source)
 
 
 def products(tiles, positions, placed_ref, slots_ref, total):
@@ -237,7 +222,7 @@
     free, late = others[0], others[-1]
     if section < slabs - 1:
         return [(free,)] + [None] * (chips - 1)
-    return [(free,)] + [None] * (chips - 3) + [(late, free), ()]
+    return [(free,), (late, free)] + [None] * (chips - 3) + [()]
 
 
 def direct(forcing, inflow, self_solve, greens, kept_cols, counts):
@@ -248,8 +233,8 @@
     kept_cols, greens, self_solve, source = (
         pltpu.with_memory_space_constraint(array, pltpu.HBM) for array in (kept_cols, greens, self_solve, source)
     )
-    spots, slots, placed, solve, base = place(chips, kept_cols, counts, greens, self_solve, source)
-    given = (rows, spots, greens, self_solve, source)
+    slots, placed, solve, base = place(chips, kept_cols, counts, greens, self_solve, source)
+    given = (slots, greens, self_solve, source)
     ready = fold(last, *given) if last > 0 else ()
     trace = jnp.zeros(entering.shape, jnp.bfloat16)
     for section in range(slabs):

time: 44.5 us -> 44.2 us (level)
  starting transfers between devices: 26.4 us -> 29.5 us
  Pallas kernels: 8.77 us -> 7 us
  waiting for transfers between devices: 7.53 us -> 5.93 us
    ppermute x15, starting transfers between devices: 20.9 us -> 23.8 us  [sent(): return lax.ppermute(tile, ('slab', 'row'), pairs)]
    pallas_call x3, Pallas kernels: 6.76 us -> 5 us  [fold(): pl.pallas_call(functools.partial(fold_kernel, section), out_shape=(pltpu....]
    ppermute x15, waiting for transfers between devices: 4.56 us -> 2.97 us  [sent(): return lax.ppermute(tile, ('slab', 'row'), pairs)]
  transfers between devices with their start and end apart: 31 -> 31, of which waited for: 14 -> 13; matrix products, arithmetic and copies ran while one was open for 0% -> 0% of each run, Pallas kernels for 19% -> 15%
where the time goes in v8:
time: 44.2 us; the launch traced here: 43.9 us
  starting transfers between devices  29.5 us (67%)
  Pallas kernels  7 us (16%)
  waiting for transfers between devices  5.93 us (13%)
  between operations  0.86 us (2%)
  local copies, waits for them, and re-layouts  0.65 us (1%)
    ppermute x15, starting transfers between devices, sent(): return lax.ppermute(tile, ('slab', 'row'), pairs)  23.8 us
    ppermute x16, starting transfers between devices, swapped(): return lax.ppermute(tile, 'row', [(r, r ^ 1) for r in range(rows)])  5.67 us
    pallas_call x3, Pallas kernels, fold(): pl.pallas_call(functools.partial(fold_kernel, section), out_shape=(pltpu....  5 us
    ppermute x16, waiting for transfers between devices, swapped(): return lax.ppermute(tile, 'row', [(r, r ^ 1) for r in range(rows)])  2.97 us
    ppermute x15, waiting for transfers between devices, sent(): return lax.ppermute(tile, ('slab', 'row'), pairs)  2.97 us
    pallas_call x11, Pallas kernels, early(): pl.pallas_call(functools.partial(early_kernel, section, positions), out_s...  1 us
  transfers between devices with their start and end apart: 31, of which 13 were waited for; matrix products, arithmetic and copies ran while one was open for 0% of the time, Pallas kernels for 15%

profile of v8, /device:TPU:7, one launch (start us, length us, event | category | flops | bytes accessed | tf_op | source)
XLA Modules:
  0.0 43.9 jit_solution(2522557711277081660)
XLA Ops:
  0.0 0.7 %collective-permute-start = (bf16[64,512]{1,0:T(8,128)(2,1)}, bf16[64,512]{1,0:T(8,128)(2,1)S(1)}, u32[]{:S(2)}, u32[]{:S(2)}) collective-permute-start(bf16[64,512]{1,0:T(8,128)(2,1)} %bitcast.8), channel_id=1, source_target_pairs={{0,4},{1,5},{2,6},{3,7},{4,0},{5,1},{6,2},{7,3},{8,9},{9,8},{10,11... | collective-permute-start | bytes 196616 | tf_op jit(solution)/shard_map/ppermute | solution.py:215
  0.7 0.5 %collective-permute-start.2 = (bf16[64,512]{1,0:T(8,128)(2,1)}, bf16[64,512]{1,0:T(8,128)(2,1)S(1)}, u32[]{:S(2)}, u32[]{:S(2)}) collective-permute-start(bf16[64,512]{1,0:T(8,128)(2,1)} %bitcast.10), channel_id=1, source_target_pairs={{0,2},{1,3},{2,0},{3,1},{4,6},{5,7},{6,4},{7,5},{8,9},{9,8},{10,11... | collective-permute-start | bytes 196616 | tf_op jit(solution)/shard_map/ppermute | solution.py:215
  1.8 0.8 %place.1 = (s32[8]{0:T(128)S(4)}, bf16[8,512,512]{2,1,0:T(8,128)(2,1)S(1)}, bf16[512,512]{1,0:T(8,128)(2,1)S(1)}, bf16[64,512]{1,0:T(8,128)(2,1)S(1)}) custom-call(s32[1,1,8]{2,1,0:T(1,128)} %cols_in.1, s32[1,1]{1,0:T(1,128)S(6)} %copy.16.count_ref, bf16[1,1,8,512,512]{4,3,2,1,0:T(8,128)(2,1)} %greens_ref.7, bf16[1,1,512,512]{3,2,1,0:T(8,128)(2,1)} %solve_in.7, ...), custom_call_target="tpu_custom_call" | custom-call | bytes 8388608 | tf_op jit(solution)/shard_map/place/pallas_call | solution.py:75
  2.6 4.9 %fold.3 = (bf16[8,512,512]{2,1,0:T(8,128)(2,1)S(1)}, f32[64,512]{1,0:T(8,128)S(1)}) custom-call(s32[8]{0:T(128)S(4)} %get-tuple-element.32.slots_ref.refs_0_, bf16[1,1,8,512,512]{4,3,2,1,0:T(8,128)(2,1)} %greens_ref.7, bf16[1,1,512,512]{3,2,1,0:T(8,128)(2,1)} %solve_in.7, bf16[64,512]{1,0:T(8,128)(2,1)} %bitcast.14), custom_call_target="tpu_custom_call" | custom-call | flops 2147483648 | bytes 8388608 | tf_op jit(solution)/shard_map/fold/pallas_call | solution.py:119
  7.6 0.6 %collective-permute-start.4 = (bf16[64,512]{1,0:T(8,128)(2,1)S(1)}, bf16[64,512]{1,0:T(8,128)(2,1)S(1)}, u32[]{:S(2)}, u32[]{:S(2)}) collective-permute-start(bf16[64,512]{1,0:T(8,128)(2,1)S(1)} %collective-permute-done.refs_3_), channel_id=1, source_target_pairs={{0,1},{1,0},{2,3},{3,2},{4,5},{5,4},{6,7},{7,6},{8,9},{9,8},{10,11... | collective-permute-start | bytes 196616 | tf_op jit(solution)/shard_map/ppermute | solution.py:204
  8.2 0.4 collective-permute-start.6
  9.6 0.4 collective-permute-start.7
  10.0 0.7 %collective-permute-start.9 = (bf16[64,512]{1,0:T(8,128)(2,1)S(1)}, bf16[64,512]{1,0:T(8,128)(2,1)S(1)}, u32[]{:S(2)}, u32[]{:S(2)}) collective-permute-start(bf16[64,512]{1,0:T(8,128)(2,1)S(1)} %late_tile.4.refs_3_), channel_id=1, source_target_pairs={{0,10},{1,11},{2,8},{3,9},{4,14},{5,15},{6,12},{7,13}} | collective-permute-start | bytes 196616 | tf_op jit(solution)/shard_map/ppermute | solution.py:215
  10.6 0.7 %collective-permute-start.11 = (bf16[64,512]{1,0:T(8,128)(2,1)S(1)}, bf16[64,512]{1,0:T(8,128)(2,1)S(1)}, u32[]{:S(2)}, u32[]{:S(2)}) collective-permute-start(bf16[64,512]{1,0:T(8,128)(2,1)S(1)} %late_tile.4.refs_3_), channel_id=1, source_target_pairs={{0,14},{1,15},{2,12},{3,13},{4,10},{5,11},{6,8},{7,9}} | collective-permute-start | bytes 196616 | tf_op jit(solution)/shard_map/ppermute | solution.py:215
  11.3 0.7 %collective-permute-start.13 = (bf16[64,512]{1,0:T(8,128)(2,1)S(1)}, bf16[64,512]{1,0:T(8,128)(2,1)S(1)}, u32[]{:S(2)}, u32[]{:S(2)}) collective-permute-start(bf16[64,512]{1,0:T(8,128)(2,1)S(1)} %late_tile.4.refs_3_), channel_id=1, source_target_pairs={{0,8},{1,9},{2,10},{3,11},{4,12},{5,13},{6,14},{7,15}} | collective-permute-start | bytes 196616 | tf_op jit(solution)/shard_map/ppermute | solution.py:215
  14.1 9.2 %collective-permute-start.15 = (bf16[64,512]{1,0:T(8,128)(2,1)S(1)}, bf16[64,512]{1,0:T(8,128)(2,1)S(1)}, u32[]{:S(2)}, u32[]{:S(2)}) collective-permute-start(bf16[64,512]{1,0:T(8,128)(2,1)S(1)} %late_tile.5.refs_3_), channel_id=1, source_target_pairs={{8,20},{9,21},{10,22},{11,23},{12,16},{13,17},{14,18},{15,19},{16,... | collective-permute-start | bytes 196616 | tf_op jit(solution)/shard_map/ppermute | solution.py:215
  23.2 0.7 %collective-permute-start.17 = (bf16[64,512]{1,0:T(8,128)(2,1)S(1)}, bf16[64,512]{1,0:T(8,128)(2,1)S(1)}, u32[]{:S(2)}, u32[]{:S(2)}) collective-permute-start(bf16[64,512]{1,0:T(8,128)(2,1)S(1)} %late_tile.5.refs_3_), channel_id=1, source_target_pairs={{8,18},{9,19},{10,16},{11,17},{12,22},{13,23},{14,20},{15,21}} | collective-permute-start | bytes 196616 | tf_op jit(solution)/shard_map/ppermute | solution.py:215
  23.9 0.7 %collective-permute-start.19 = (bf16[64,512]{1,0:T(8,128)(2,1)S(1)}, bf16[64,512]{1,0:T(8,128)(2,1)S(1)}, u32[]{:S(2)}, u32[]{:S(2)}) collective-permute-start(bf16[64,512]{1,0:T(8,128)(2,1)S(1)} %late_tile.5.refs_3_), channel_id=1, source_target_pairs={{8,22},{9,23},{10,20},{11,21},{12,18},{13,19},{14,16},{15,17}} | collective-permute-start | bytes 196616 | tf_op jit(solution)/shard_map/ppermute | solution.py:215
  24.6 0.7 %collective-permute-start.21 = (bf16[64,512]{1,0:T(8,128)(2,1)S(1)}, bf16[64,512]{1,0:T(8,128)(2,1)S(1)}, u32[]{:S(2)}, u32[]{:S(2)}) collective-permute-start(bf16[64,512]{1,0:T(8,128)(2,1)S(1)} %late_tile.5.refs_3_), channel_id=1, source_target_pairs={{8,16},{9,17},{10,18},{11,19},{12,20},{13,21},{14,22},{15,23}} | collective-permute-start | bytes 196616 | tf_op jit(solution)/shard_map/ppermute | solution.py:215
  25.3 0.5 %collective-permute-start.16 = (bf16[64,512]{1,0:T(8,128)(2,1)S(1)}, bf16[64,512]{1,0:T(8,128)(2,1)S(1)}, u32[]{:S(2)}, u32[]{:S(2)}) collective-permute-start(bf16[64,512]{1,0:T(8,128)(2,1)S(1)} %collective-permute-done.15.refs_2_), channel_id=1, source_target_pairs={{0,1},{1,0},{2,3},{3,2},{4,5},{5,4},{6,7},{7,6},{8,9},{9,8},{10,11... | collective-permute-start | bytes 196616 | tf_op jit(solution)/shard_map/ppermute | solution.py:204
  25.9 0.4 collective-permute-start.20
  27.6 4.5 %collective-permute-start.25 = (bf16[64,512]{1,0:T(8,128)(2,1)S(1)}, bf16[64,512]{1,0:T(8,128)(2,1)S(1)}, u32[]{:S(2)}, u32[]{:S(2)}) collective-permute-start(bf16[64,512]{1,0:T(8,128)(2,1)S(1)} %late_tile.6.refs_3_), channel_id=1, source_target_pairs={{16,26},{17,27},{18,24},{19,25},{20,30},{21,31},{22,28},{23,29},{2... | collective-permute-start | bytes 196616 | tf_op jit(solution)/shard_map/ppermute | solution.py:215
  32.1 1.3 %collective-permute-start.27 = (bf16[64,512]{1,0:T(8,128)(2,1)S(1)}, bf16[64,512]{1,0:T(8,128)(2,1)S(1)}, u32[]{:S(2)}, u32[]{:S(2)}) collective-permute-start(bf16[64,512]{1,0:T(8,128)(2,1)S(1)} %late_tile.6.refs_3_), channel_id=1, source_target_pairs={{16,30},{17,31},{18,28},{19,29},{20,26},{21,27},{22,24},{23,25}} | collective-permute-start | bytes 196616 | tf_op jit(solution)/shard_map/ppermute | solution.py:215
  33.4 3.3 %collective-permute-start.29 = (bf16[64,512]{1,0:T(8,128)(2,1)S(1)}, bf16[64,512]{1,0:T(8,128)(2,1)S(1)}, u32[]{:S(2)}, u32[]{:S(2)}) collective-permute-start(bf16[64,512]{1,0:T(8,128)(2,1)S(1)} %late_tile.6.refs_3_), channel_id=1, source_target_pairs={{16,24},{17,25},{18,26},{19,27},{20,28},{21,29},{22,30},{23,31},{2... | collective-permute-start | bytes 196616 | tf_op jit(solution)/shard_map/ppermute | solution.py:215
  36.7 2.0 %collective-permute-done.23.refs_2_ = bf16[64,512]{1,0:T(8,128)(2,1)S(1)} collective-permute-done((bf16[64,512]{1,0:T(8,128)(2,1)S(1)}, bf16[64,512]{1,0:T(8,128)(2,1)S(1)}, u32[]{:S(2)}, u32[]{:S(2)}) %collective-permute-start.23) | collective-permute-done | bytes 65568 | tf_op jit(solution)/shard_map/ppermute | solution.py:215
  38.7 0.9 %collective-permute-start.24 = (bf16[64,512]{1,0:T(8,128)(2,1)S(1)}, bf16[64,512]{1,0:T(8,128)(2,1)S(1)}, u32[]{:S(2)}, u32[]{:S(2)}) collective-permute-start(bf16[64,512]{1,0:T(8,128)(2,1)S(1)} %collective-permute-done.23.refs_2_), channel_id=1, source_target_pairs={{0,1},{1,0},{2,3},{3,2},{4,5},{5,4},{6,7},{7,6},{8,9},{9,8},{10,11... | collective-permute-start | bytes 196616 | tf_op jit(solution)/shard_map/ppermute | solution.py:204
  39.6 1.0 %collective-permute-done.27.refs_3_ = bf16[64,512]{1,0:T(8,128)(2,1)S(1)} collective-permute-done((bf16[64,512]{1,0:T(8,128)(2,1)S(1)}, bf16[64,512]{1,0:T(8,128)(2,1)S(1)}, u32[]{:S(2)}, u32[]{:S(2)}) %collective-permute-start.27) | collective-permute-done | bytes 65568 | tf_op jit(solution)/shard_map/ppermute | solution.py:215
  40.6 1.1 %collective-permute-start.28 = (bf16[64,512]{1,0:T(8,128)(2,1)S(1)}, bf16[64,512]{1,0:T(8,128)(2,1)S(1)}, u32[]{:S(2)}, u32[]{:S(2)}) collective-permute-start(bf16[64,512]{1,0:T(8,128)(2,1)S(1)} %collective-permute-done.27.refs_3_), channel_id=1, source_target_pairs={{0,1},{1,0},{2,3},{3,2},{4,5},{5,4},{6,7},{7,6},{8,9},{9,8},{10,11... | collective-permute-start | bytes 196616 | tf_op jit(solution)/shard_map/ppermute | solution.py:204
  43.3 0.6 %copy.15 = bf16[1,512,64]{1,2,0:T(8,128)(2,1)} copy(bf16[1,512,64]{1,2,0:T(8,128)(2,1)S(1)} %bitcast.7) | data formatting | bytes 131072
  (61 shorter events, 6.0 us)
Async XLA Ops:
  0.0 7.6 %collective-permute-start = (bf16[64,512]{1,0:T(8,128)(2,1)}, bf16[64,512]{1,0:T(8,128)(2,1)S(1)}, u32[]{:S(2)}, u32[]{:S(2)}) collective-permute-start(bf16[64,512]{1,0:T(8,128)(2,1)} %bitcast.8), channel_id=1, source_target_pairs={{0,4},{1,5},{2,6},{3,7},{4,0},{5,1},{6,2},{7,3},{8,9},{9,8},{10,11... | collective-permute-start | bytes 196616 | tf_op jit(solution)/shard_map/ppermute | solution.py:215
  0.7 8.0 %collective-permute-start.1 = (bf16[64,512]{1,0:T(8,128)(2,1)}, bf16[64,512]{1,0:T(8,128)(2,1)S(1)}, u32[]{:S(2)}, u32[]{:S(2)}) collective-permute-start(bf16[64,512]{1,0:T(8,128)(2,1)} %bitcast.9), channel_id=1, source_target_pairs={{0,1},{1,0},{2,3},{3,2},{4,5},{5,4},{6,7},{7,6},{8,9},{9,8},{10,11... | collective-permute-start | bytes 196616 | tf_op jit(solution)/shard_map/ppermute | solution.py:204
  0.7 7.5 %collective-permute-start.2 = (bf16[64,512]{1,0:T(8,128)(2,1)}, bf16[64,512]{1,0:T(8,128)(2,1)S(1)}, u32[]{:S(2)}, u32[]{:S(2)}) collective-permute-start(bf16[64,512]{1,0:T(8,128)(2,1)} %bitcast.10), channel_id=1, source_target_pairs={{0,2},{1,3},{2,0},{3,1},{4,6},{5,7},{6,4},{7,5},{8,9},{9,8},{10,11... | collective-permute-start | bytes 196616 | tf_op jit(solution)/shard_map/ppermute | solution.py:215
  1.2 7.1 %collective-permute-start.3 = (bf16[64,512]{1,0:T(8,128)(2,1)}, bf16[64,512]{1,0:T(8,128)(2,1)S(1)}, u32[]{:S(2)}, u32[]{:S(2)}) collective-permute-start(bf16[64,512]{1,0:T(8,128)(2,1)} %bitcast.11), channel_id=1, source_target_pairs={{0,6},{1,7},{2,4},{3,5},{4,2},{5,3},{6,0},{7,1},{8,9},{9,8},{10,11... | collective-permute-start | bytes 196616 | tf_op jit(solution)/shard_map/ppermute | solution.py:215
  7.6 1.5 %collective-permute-start.4 = (bf16[64,512]{1,0:T(8,128)(2,1)S(1)}, bf16[64,512]{1,0:T(8,128)(2,1)S(1)}, u32[]{:S(2)}, u32[]{:S(2)}) collective-permute-start(bf16[64,512]{1,0:T(8,128)(2,1)S(1)} %collective-permute-done.refs_3_), channel_id=1, source_target_pairs={{0,1},{1,0},{2,3},{3,2},{4,5},{5,4},{6,7},{7,6},{8,9},{9,8},{10,11... | collective-permute-start | bytes 196616 | tf_op jit(solution)/shard_map/ppermute | solution.py:204
  8.2 1.3 %collective-permute-start.6 = (bf16[64,512]{1,0:T(8,128)(2,1)S(1)}, bf16[64,512]{1,0:T(8,128)(2,1)S(1)}, u32[]{:S(2)}, u32[]{:S(2)}) collective-permute-start(bf16[64,512]{1,0:T(8,128)(2,1)S(1)} %collective-permute-done.3.refs_5_), channel_id=1, source_target_pairs={{0,1},{1,0},{2,3},{3,2},{4,5},{5,4},{6,7},{7,6},{8,9},{9,8},{10,11... | collective-permute-start | bytes 196616 | tf_op jit(solution)/shard_map/ppermute | solution.py:204
  9.6 2.5 %collective-permute-start.7 = (bf16[64,512]{1,0:T(8,128)(2,1)S(1)}, bf16[64,512]{1,0:T(8,128)(2,1)S(1)}, u32[]{:S(2)}, u32[]{:S(2)}) collective-permute-start(bf16[64,512]{1,0:T(8,128)(2,1)S(1)} %late_tile.4.refs_3_), channel_id=1, source_target_pairs={{0,12},{1,13},{2,14},{3,15},{4,8},{5,9},{6,10},{7,11},{8,16},{9,17... | collective-permute-start | bytes 196616 | tf_op jit(solution)/shard_map/ppermute | solution.py:215
  10.0 2.3 %collective-permute-start.9 = (bf16[64,512]{1,0:T(8,128)(2,1)S(1)}, bf16[64,512]{1,0:T(8,128)(2,1)S(1)}, u32[]{:S(2)}, u32[]{:S(2)}) collective-permute-start(bf16[64,512]{1,0:T(8,128)(2,1)S(1)} %late_tile.4.refs_3_), channel_id=1, source_target_pairs={{0,10},{1,11},{2,8},{3,9},{4,14},{5,15},{6,12},{7,13}} | collective-permute-start | bytes 196616 | tf_op jit(solution)/shard_map/ppermute | solution.py:215
  10.6 2.0 %collective-permute-start.11 = (bf16[64,512]{1,0:T(8,128)(2,1)S(1)}, bf16[64,512]{1,0:T(8,128)(2,1)S(1)}, u32[]{:S(2)}, u32[]{:S(2)}) collective-permute-start(bf16[64,512]{1,0:T(8,128)(2,1)S(1)} %late_tile.4.refs_3_), channel_id=1, source_target_pairs={{0,14},{1,15},{2,12},{3,13},{4,10},{5,11},{6,8},{7,9}} | collective-permute-start | bytes 196616 | tf_op jit(solution)/shard_map/ppermute | solution.py:215
  11.3 1.5 %collective-permute-start.13 = (bf16[64,512]{1,0:T(8,128)(2,1)S(1)}, bf16[64,512]{1,0:T(8,128)(2,1)S(1)}, u32[]{:S(2)}, u32[]{:S(2)}) collective-permute-start(bf16[64,512]{1,0:T(8,128)(2,1)S(1)} %late_tile.4.refs_3_), channel_id=1, source_target_pairs={{0,8},{1,9},{2,10},{3,11},{4,12},{5,13},{6,14},{7,15}} | collective-permute-start | bytes 196616 | tf_op jit(solution)/shard_map/ppermute | solution.py:215
  14.1 11.2 %collective-permute-start.15 = (bf16[64,512]{1,0:T(8,128)(2,1)S(1)}, bf16[64,512]{1,0:T(8,128)(2,1)S(1)}, u32[]{:S(2)}, u32[]{:S(2)}) collective-permute-start(bf16[64,512]{1,0:T(8,128)(2,1)S(1)} %late_tile.5.refs_3_), channel_id=1, source_target_pairs={{8,20},{9,21},{10,22},{11,23},{12,16},{13,17},{14,18},{15,19},{16,... | collective-permute-start | bytes 196616 | tf_op jit(solution)/shard_map/ppermute | solution.py:215
  23.2 2.6 %collective-permute-start.17 = (bf16[64,512]{1,0:T(8,128)(2,1)S(1)}, bf16[64,512]{1,0:T(8,128)(2,1)S(1)}, u32[]{:S(2)}, u32[]{:S(2)}) collective-permute-start(bf16[64,512]{1,0:T(8,128)(2,1)S(1)} %late_tile.5.refs_3_), channel_id=1, source_target_pairs={{8,18},{9,19},{10,16},{11,17},{12,22},{13,23},{14,20},{15,21}} | collective-permute-start | bytes 196616 | tf_op jit(solution)/shard_map/ppermute | solution.py:215
  23.9 2.0 %collective-permute-start.19 = (bf16[64,512]{1,0:T(8,128)(2,1)S(1)}, bf16[64,512]{1,0:T(8,128)(2,1)S(1)}, u32[]{:S(2)}, u32[]{:S(2)}) collective-permute-start(bf16[64,512]{1,0:T(8,128)(2,1)S(1)} %late_tile.5.refs_3_), channel_id=1, source_target_pairs={{8,22},{9,23},{10,20},{11,21},{12,18},{13,19},{14,16},{15,17}} | collective-permute-start | bytes 196616 | tf_op jit(solution)/shard_map/ppermute | solution.py:215
  24.6 1.8 %collective-permute-start.21 = (bf16[64,512]{1,0:T(8,128)(2,1)S(1)}, bf16[64,512]{1,0:T(8,128)(2,1)S(1)}, u32[]{:S(2)}, u32[]{:S(2)}) collective-permute-start(bf16[64,512]{1,0:T(8,128)(2,1)S(1)} %late_tile.5.refs_3_), channel_id=1, source_target_pairs={{8,16},{9,17},{10,18},{11,19},{12,20},{13,21},{14,22},{15,23}} | collective-permute-start | bytes 196616 | tf_op jit(solution)/shard_map/ppermute | solution.py:215
  25.3 1.4 %collective-permute-start.16 = (bf16[64,512]{1,0:T(8,128)(2,1)S(1)}, bf16[64,512]{1,0:T(8,128)(2,1)S(1)}, u32[]{:S(2)}, u32[]{:S(2)}) collective-permute-start(bf16[64,512]{1,0:T(8,128)(2,1)S(1)} %collective-permute-done.15.refs_2_), channel_id=1, source_target_pairs={{0,1},{1,0},{2,3},{3,2},{4,5},{5,4},{6,7},{7,6},{8,9},{9,8},{10,11... | collective-permute-start | bytes 196616 | tf_op jit(solution)/shard_map/ppermute | solution.py:204
  25.9 1.3 %collective-permute-start.20 = (bf16[64,512]{1,0:T(8,128)(2,1)S(1)}, bf16[64,512]{1,0:T(8,128)(2,1)S(1)}, u32[]{:S(2)}, u32[]{:S(2)}) collective-permute-start(bf16[64,512]{1,0:T(8,128)(2,1)S(1)} %collective-permute-done.19.refs_3_), channel_id=1, source_target_pairs={{0,1},{1,0},{2,3},{3,2},{4,5},{5,4},{6,7},{7,6},{8,9},{9,8},{10,11... | collective-permute-start | bytes 196616 | tf_op jit(solution)/shard_map/ppermute | solution.py:204
  27.6 11.1 %collective-permute-start.23 = (bf16[64,512]{1,0:T(8,128)(2,1)S(1)}, bf16[64,512]{1,0:T(8,128)(2,1)S(1)}, u32[]{:S(2)}, u32[]{:S(2)}) collective-permute-start(bf16[64,512]{1,0:T(8,128)(2,1)S(1)} %late_tile.6.refs_3_), channel_id=1, source_target_pairs={{16,28},{17,29},{18,30},{19,31},{20,24},{21,25},{22,26},{23,27},{2... | collective-permute-start | bytes 196616 | tf_op jit(solution)/shard_map/ppermute | solution.py:215
  27.6 12.0 %collective-permute-start.25 = (bf16[64,512]{1,0:T(8,128)(2,1)S(1)}, bf16[64,512]{1,0:T(8,128)(2,1)S(1)}, u32[]{:S(2)}, u32[]{:S(2)}) collective-permute-start(bf16[64,512]{1,0:T(8,128)(2,1)S(1)} %late_tile.6.refs_3_), channel_id=1, source_target_pairs={{16,26},{17,27},{18,24},{19,25},{20,30},{21,31},{22,28},{23,29},{2... | collective-permute-start | bytes 196616 | tf_op jit(solution)/shard_map/ppermute | solution.py:215
  32.1 8.5 %collective-permute-start.27 = (bf16[64,512]{1,0:T(8,128)(2,1)S(1)}, bf16[64,512]{1,0:T(8,128)(2,1)S(1)}, u32[]{:S(2)}, u32[]{:S(2)}) collective-permute-start(bf16[64,512]{1,0:T(8,128)(2,1)S(1)} %late_tile.6.refs_3_), channel_id=1, source_target_pairs={{16,30},{17,31},{18,28},{19,29},{20,26},{21,27},{22,24},{23,25}} | collective-permute-start | bytes 196616 | tf_op jit(solution)/shard_map/ppermute | solution.py:215
  33.4 8.3 %collective-permute-start.29 = (bf16[64,512]{1,0:T(8,128)(2,1)S(1)}, bf16[64,512]{1,0:T(8,128)(2,1)S(1)}, u32[]{:S(2)}, u32[]{:S(2)}) collective-permute-start(bf16[64,512]{1,0:T(8,128)(2,1)S(1)} %late_tile.6.refs_3_), channel_id=1, source_target_pairs={{16,24},{17,25},{18,26},{19,27},{20,28},{21,29},{22,30},{23,31},{2... | collective-permute-start | bytes 196616 | tf_op jit(solution)/shard_map/ppermute | solution.py:215
  38.7 3.3 %collective-permute-start.24 = (bf16[64,512]{1,0:T(8,128)(2,1)S(1)}, bf16[64,512]{1,0:T(8,128)(2,1)S(1)}, u32[]{:S(2)}, u32[]{:S(2)}) collective-permute-start(bf16[64,512]{1,0:T(8,128)(2,1)S(1)} %collective-permute-done.23.refs_2_), channel_id=1, source_target_pairs={{0,1},{1,0},{2,3},{3,2},{4,5},{5,4},{6,7},{7,6},{8,9},{9,8},{10,11... | collective-permute-start | bytes 196616 | tf_op jit(solution)/shard_map/ppermute | solution.py:204
  39.6 2.8 %collective-permute-start.26 = (bf16[64,512]{1,0:T(8,128)(2,1)S(1)}, bf16[64,512]{1,0:T(8,128)(2,1)S(1)}, u32[]{:S(2)}, u32[]{:S(2)}) collective-permute-start(bf16[64,512]{1,0:T(8,128)(2,1)S(1)} %collective-permute-done.25.refs_4_), channel_id=1, source_target_pairs={{0,1},{1,0},{2,3},{3,2},{4,5},{5,4},{6,7},{7,6},{8,9},{9,8},{10,11... | collective-permute-start | bytes 196616 | tf_op jit(solution)/shard_map/ppermute | solution.py:204
  40.6 2.1 %collective-permute-start.28 = (bf16[64,512]{1,0:T(8,128)(2,1)S(1)}, bf16[64,512]{1,0:T(8,128)(2,1)S(1)}, u32[]{:S(2)}, u32[]{:S(2)}) collective-permute-start(bf16[64,512]{1,0:T(8,128)(2,1)S(1)} %collective-permute-done.27.refs_3_), channel_id=1, source_target_pairs={{0,1},{1,0},{2,3},{3,2},{4,5},{5,4},{6,7},{7,6},{8,9},{9,8},{10,11... | collective-permute-start | bytes 196616 | tf_op jit(solution)/shard_map/ppermute | solution.py:204
  41.7 1.4 %collective-permute-start.30 = (bf16[64,512]{1,0:T(8,128)(2,1)S(1)}, bf16[64,512]{1,0:T(8,128)(2,1)S(1)}, u32[]{:S(2)}, u32[]{:S(2)}) collective-permute-start(bf16[64,512]{1,0:T(8,128)(2,1)S(1)} %collective-permute-done.29.refs_3_), channel_id=1, source_target_pairs={{0,1},{1,0},{2,3},{3,2},{4,5},{5,4},{6,7},{7,6},{8,9},{9,8},{10,11... | collective-permute-start | bytes 196616 | tf_op jit(solution)/shard_map/ppermute | solution.py:204
  (8 other events, 14.9 us)

commit v9 on v8

--- a/solution.py
+++ b/solution.py
@@ -106,12 +106,15 @@
             copy.wait()
         base_ref[...] = lax.dot_general(source_ref[...], solve_ref[...], LAST_LAST, preferred_element_type=jnp.float32)
 
-        for position in range(folded_ref.shape[0]):
+        def fold_one(position, carry):
             slot = slots_ref[position]
             solved = lax.dot_general(
                 held_ref[jnp.maximum(slot, 0)], solve_ref[...], FIRST_LAST, preferred_element_type=jnp.float32
             )
             folded_ref[position] = jnp.where(slot >= 0, solved, jnp.zeros_like(solved)).astype(folded_ref.dtype)
+            return carry
+
+        lax.fori_loop(0, folded_ref.shape[0], fold_one, 0, unroll=section != lax.axis_size("slab") - 1)
 
 
 def fold(section, slots, greens, solve, source):

time: 44.2 us -> 44.2 us (level)
  starting transfers between devices: 29.5 us -> 27.9 us
  Pallas kernels: 7 us -> 8.55 us
    pallas_call x3, Pallas kernels: 5 us -> 6.55 us  [fold(): pl.pallas_call(functools.partial(fold_kernel, section), out_shape=(pltpu....]
    ppermute x15, starting transfers between devices: 23.8 us -> 22.3 us  [sent(): return lax.ppermute(tile, ('slab', 'row'), pairs)]
  transfers between devices with their start and end apart: 31 -> 31, of which waited for: 13 -> 13; matrix products, arithmetic and copies ran while one was open for 0% -> 0% of each run, Pallas kernels for 15% -> 19%
where the time goes in v9:
time: 44.2 us; the launch traced here: 43.9 us
  starting transfers between devices  27.9 us (63%)
  Pallas kernels  8.55 us (19%)
  waiting for transfers between devices  5.93 us (13%)
  between operations  0.86 us (2%)
  local copies, waits for them, and re-layouts  0.65 us (1%)
    ppermute x15, starting transfers between devices, sent(): return lax.ppermute(tile, ('slab', 'row'), pairs)  22.3 us
    pallas_call x3, Pallas kernels, fold(): pl.pallas_call(functools.partial(fold_kernel, section), out_shape=(pltpu....  6.55 us
    ppermute x16, starting transfers between devices, swapped(): return lax.ppermute(tile, 'row', [(r, r ^ 1) for r in range(rows)])  5.67 us
    ppermute x16, waiting for transfers between devices, swapped(): return lax.ppermute(tile, 'row', [(r, r ^ 1) for r in range(rows)])  2.97 us
    ppermute x15, waiting for transfers between devices, sent(): return lax.ppermute(tile, ('slab', 'row'), pairs)  2.97 us
    pallas_call x11, Pallas kernels, early(): pl.pallas_call(functools.partial(early_kernel, section, positions), out_s...  1 us
  transfers between devices with their start and end apart: 31, of which 13 were waited for; matrix products, arithmetic and copies ran while one was open for 0% of the time, Pallas kernels for 19%

profile of v9, /device:TPU:7, one launch (start us, length us, event | category | flops | bytes accessed | tf_op | source)
XLA Modules:
  0.0 43.9 jit_solution(344588689522169724)
XLA Ops:
  0.0 0.7 %collective-permute-start = (bf16[64,512]{1,0:T(8,128)(2,1)}, bf16[64,512]{1,0:T(8,128)(2,1)S(1)}, u32[]{:S(2)}, u32[]{:S(2)}) collective-permute-start(bf16[64,512]{1,0:T(8,128)(2,1)} %bitcast.8), channel_id=1, source_target_pairs={{0,4},{1,5},{2,6},{3,7},{4,0},{5,1},{6,2},{7,3},{8,9},{9,8},{10,11... | collective-permute-start | bytes 196616 | tf_op jit(solution)/shard_map/ppermute | solution.py:218
  0.7 0.5 %collective-permute-start.2 = (bf16[64,512]{1,0:T(8,128)(2,1)}, bf16[64,512]{1,0:T(8,128)(2,1)S(1)}, u32[]{:S(2)}, u32[]{:S(2)}) collective-permute-start(bf16[64,512]{1,0:T(8,128)(2,1)} %bitcast.10), channel_id=1, source_target_pairs={{0,2},{1,3},{2,0},{3,1},{4,6},{5,7},{6,4},{7,5},{8,9},{9,8},{10,11... | collective-permute-start | bytes 196616 | tf_op jit(solution)/shard_map/ppermute | solution.py:218
  1.8 0.8 %place.1 = (s32[8]{0:T(128)S(4)}, bf16[8,512,512]{2,1,0:T(8,128)(2,1)S(1)}, bf16[512,512]{1,0:T(8,128)(2,1)S(1)}, bf16[64,512]{1,0:T(8,128)(2,1)S(1)}) custom-call(s32[1,1,8]{2,1,0:T(1,128)} %cols_in.1, s32[1,1]{1,0:T(1,128)S(6)} %copy.16.count_ref, bf16[1,1,8,512,512]{4,3,2,1,0:T(8,128)(2,1)} %greens_ref.7, bf16[1,1,512,512]{3,2,1,0:T(8,128)(2,1)} %solve_in.7, ...), custom_call_target="tpu_custom_call" | custom-call | bytes 8388608 | tf_op jit(solution)/shard_map/place/pallas_call | solution.py:75
  2.6 6.5 %fold.3 = (bf16[8,512,512]{2,1,0:T(8,128)(2,1)S(1)}, f32[64,512]{1,0:T(8,128)S(1)}) custom-call(s32[8]{0:T(128)S(4)} %get-tuple-element.32.slots_ref.refs_0_, bf16[1,1,8,512,512]{4,3,2,1,0:T(8,128)(2,1)} %greens_ref.7, bf16[1,1,512,512]{3,2,1,0:T(8,128)(2,1)} %solve_in.7, bf16[64,512]{1,0:T(8,128)(2,1)} %bitcast.14), custom_call_target="tpu_custom_call" | custom-call | flops 2147483648 | bytes 8388608 | tf_op jit(solution)/shard_map/fold/pallas_call | solution.py:122
  9.1 0.6 %collective-permute-start.4 = (bf16[64,512]{1,0:T(8,128)(2,1)S(1)}, bf16[64,512]{1,0:T(8,128)(2,1)S(1)}, u32[]{:S(2)}, u32[]{:S(2)}) collective-permute-start(bf16[64,512]{1,0:T(8,128)(2,1)S(1)} %collective-permute-done.refs_3_), channel_id=1, source_target_pairs={{0,1},{1,0},{2,3},{3,2},{4,5},{5,4},{6,7},{7,6},{8,9},{9,8},{10,11... | collective-permute-start | bytes 196616 | tf_op jit(solution)/shard_map/ppermute | solution.py:207
  9.8 0.4 collective-permute-start.6
  11.1 0.4 collective-permute-start.7
  11.5 0.7 %collective-permute-start.9 = (bf16[64,512]{1,0:T(8,128)(2,1)S(1)}, bf16[64,512]{1,0:T(8,128)(2,1)S(1)}, u32[]{:S(2)}, u32[]{:S(2)}) collective-permute-start(bf16[64,512]{1,0:T(8,128)(2,1)S(1)} %late_tile.4.refs_3_), channel_id=1, source_target_pairs={{0,10},{1,11},{2,8},{3,9},{4,14},{5,15},{6,12},{7,13}} | collective-permute-start | bytes 196616 | tf_op jit(solution)/shard_map/ppermute | solution.py:218
  12.2 0.7 %collective-permute-start.11 = (bf16[64,512]{1,0:T(8,128)(2,1)S(1)}, bf16[64,512]{1,0:T(8,128)(2,1)S(1)}, u32[]{:S(2)}, u32[]{:S(2)}) collective-permute-start(bf16[64,512]{1,0:T(8,128)(2,1)S(1)} %late_tile.4.refs_3_), channel_id=1, source_target_pairs={{0,14},{1,15},{2,12},{3,13},{4,10},{5,11},{6,8},{7,9}} | collective-permute-start | bytes 196616 | tf_op jit(solution)/shard_map/ppermute | solution.py:218
  12.9 0.7 %collective-permute-start.13 = (bf16[64,512]{1,0:T(8,128)(2,1)S(1)}, bf16[64,512]{1,0:T(8,128)(2,1)S(1)}, u32[]{:S(2)}, u32[]{:S(2)}) collective-permute-start(bf16[64,512]{1,0:T(8,128)(2,1)S(1)} %late_tile.4.refs_3_), channel_id=1, source_target_pairs={{0,8},{1,9},{2,10},{3,11},{4,12},{5,13},{6,14},{7,15}} | collective-permute-start | bytes 196616 | tf_op jit(solution)/shard_map/ppermute | solution.py:218
  15.6 7.6 %collective-permute-start.15 = (bf16[64,512]{1,0:T(8,128)(2,1)S(1)}, bf16[64,512]{1,0:T(8,128)(2,1)S(1)}, u32[]{:S(2)}, u32[]{:S(2)}) collective-permute-start(bf16[64,512]{1,0:T(8,128)(2,1)S(1)} %late_tile.5.refs_3_), channel_id=1, source_target_pairs={{8,20},{9,21},{10,22},{11,23},{12,16},{13,17},{14,18},{15,19},{16,... | collective-permute-start | bytes 196616 | tf_op jit(solution)/shard_map/ppermute | solution.py:218
  23.2 0.7 %collective-permute-start.17 = (bf16[64,512]{1,0:T(8,128)(2,1)S(1)}, bf16[64,512]{1,0:T(8,128)(2,1)S(1)}, u32[]{:S(2)}, u32[]{:S(2)}) collective-permute-start(bf16[64,512]{1,0:T(8,128)(2,1)S(1)} %late_tile.5.refs_3_), channel_id=1, source_target_pairs={{8,18},{9,19},{10,16},{11,17},{12,22},{13,23},{14,20},{15,21}} | collective-permute-start | bytes 196616 | tf_op jit(solution)/shard_map/ppermute | solution.py:218
  23.9 0.7 %collective-permute-start.19 = (bf16[64,512]{1,0:T(8,128)(2,1)S(1)}, bf16[64,512]{1,0:T(8,128)(2,1)S(1)}, u32[]{:S(2)}, u32[]{:S(2)}) collective-permute-start(bf16[64,512]{1,0:T(8,128)(2,1)S(1)} %late_tile.5.refs_3_), channel_id=1, source_target_pairs={{8,22},{9,23},{10,20},{11,21},{12,18},{13,19},{14,16},{15,17}} | collective-permute-start | bytes 196616 | tf_op jit(solution)/shard_map/ppermute | solution.py:218
  24.6 0.7 %collective-permute-start.21 = (bf16[64,512]{1,0:T(8,128)(2,1)S(1)}, bf16[64,512]{1,0:T(8,128)(2,1)S(1)}, u32[]{:S(2)}, u32[]{:S(2)}) collective-permute-start(bf16[64,512]{1,0:T(8,128)(2,1)S(1)} %late_tile.5.refs_3_), channel_id=1, source_target_pairs={{8,16},{9,17},{10,18},{11,19},{12,20},{13,21},{14,22},{15,23}} | collective-permute-start | bytes 196616 | tf_op jit(solution)/shard_map/ppermute | solution.py:218
  25.3 0.5 %collective-permute-start.16 = (bf16[64,512]{1,0:T(8,128)(2,1)S(1)}, bf16[64,512]{1,0:T(8,128)(2,1)S(1)}, u32[]{:S(2)}, u32[]{:S(2)}) collective-permute-start(bf16[64,512]{1,0:T(8,128)(2,1)S(1)} %collective-permute-done.15.refs_2_), channel_id=1, source_target_pairs={{0,1},{1,0},{2,3},{3,2},{4,5},{5,4},{6,7},{7,6},{8,9},{9,8},{10,11... | collective-permute-start | bytes 196616 | tf_op jit(solution)/shard_map/ppermute | solution.py:207
  25.9 0.4 collective-permute-start.20
  27.6 4.5 %collective-permute-start.25 = (bf16[64,512]{1,0:T(8,128)(2,1)S(1)}, bf16[64,512]{1,0:T(8,128)(2,1)S(1)}, u32[]{:S(2)}, u32[]{:S(2)}) collective-permute-start(bf16[64,512]{1,0:T(8,128)(2,1)S(1)} %late_tile.6.refs_3_), channel_id=1, source_target_pairs={{16,26},{17,27},{18,24},{19,25},{20,30},{21,31},{22,28},{23,29},{2... | collective-permute-start | bytes 196616 | tf_op jit(solution)/shard_map/ppermute | solution.py:218
  32.1 1.3 %collective-permute-start.27 = (bf16[64,512]{1,0:T(8,128)(2,1)S(1)}, bf16[64,512]{1,0:T(8,128)(2,1)S(1)}, u32[]{:S(2)}, u32[]{:S(2)}) collective-permute-start(bf16[64,512]{1,0:T(8,128)(2,1)S(1)} %late_tile.6.refs_3_), channel_id=1, source_target_pairs={{16,30},{17,31},{18,28},{19,29},{20,26},{21,27},{22,24},{23,25}} | collective-permute-start | bytes 196616 | tf_op jit(solution)/shard_map/ppermute | solution.py:218
  33.4 3.3 %collective-permute-start.29 = (bf16[64,512]{1,0:T(8,128)(2,1)S(1)}, bf16[64,512]{1,0:T(8,128)(2,1)S(1)}, u32[]{:S(2)}, u32[]{:S(2)}) collective-permute-start(bf16[64,512]{1,0:T(8,128)(2,1)S(1)} %late_tile.6.refs_3_), channel_id=1, source_target_pairs={{16,24},{17,25},{18,26},{19,27},{20,28},{21,29},{22,30},{23,31},{2... | collective-permute-start | bytes 196616 | tf_op jit(solution)/shard_map/ppermute | solution.py:218
  36.7 2.0 %collective-permute-done.23.refs_2_ = bf16[64,512]{1,0:T(8,128)(2,1)S(1)} collective-permute-done((bf16[64,512]{1,0:T(8,128)(2,1)S(1)}, bf16[64,512]{1,0:T(8,128)(2,1)S(1)}, u32[]{:S(2)}, u32[]{:S(2)}) %collective-permute-start.23) | collective-permute-done | bytes 65568 | tf_op jit(solution)/shard_map/ppermute | solution.py:218
  38.7 0.9 %collective-permute-start.24 = (bf16[64,512]{1,0:T(8,128)(2,1)S(1)}, bf16[64,512]{1,0:T(8,128)(2,1)S(1)}, u32[]{:S(2)}, u32[]{:S(2)}) collective-permute-start(bf16[64,512]{1,0:T(8,128)(2,1)S(1)} %collective-permute-done.23.refs_2_), channel_id=1, source_target_pairs={{0,1},{1,0},{2,3},{3,2},{4,5},{5,4},{6,7},{7,6},{8,9},{9,8},{10,11... | collective-permute-start | bytes 196616 | tf_op jit(solution)/shard_map/ppermute | solution.py:207
  39.6 1.0 %collective-permute-done.27.refs_3_ = bf16[64,512]{1,0:T(8,128)(2,1)S(1)} collective-permute-done((bf16[64,512]{1,0:T(8,128)(2,1)S(1)}, bf16[64,512]{1,0:T(8,128)(2,1)S(1)}, u32[]{:S(2)}, u32[]{:S(2)}) %collective-permute-start.27) | collective-permute-done | bytes 65568 | tf_op jit(solution)/shard_map/ppermute | solution.py:218
  40.6 1.1 %collective-permute-start.28 = (bf16[64,512]{1,0:T(8,128)(2,1)S(1)}, bf16[64,512]{1,0:T(8,128)(2,1)S(1)}, u32[]{:S(2)}, u32[]{:S(2)}) collective-permute-start(bf16[64,512]{1,0:T(8,128)(2,1)S(1)} %collective-permute-done.27.refs_3_), channel_id=1, source_target_pairs={{0,1},{1,0},{2,3},{3,2},{4,5},{5,4},{6,7},{7,6},{8,9},{9,8},{10,11... | collective-permute-start | bytes 196616 | tf_op jit(solution)/shard_map/ppermute | solution.py:207
  43.3 0.6 %copy.15 = bf16[1,512,64]{1,2,0:T(8,128)(2,1)} copy(bf16[1,512,64]{1,2,0:T(8,128)(2,1)S(1)} %bitcast.7) | data formatting | bytes 131072
  (61 shorter events, 6.0 us)
Async XLA Ops:
  0.0 9.1 %collective-permute-start = (bf16[64,512]{1,0:T(8,128)(2,1)}, bf16[64,512]{1,0:T(8,128)(2,1)S(1)}, u32[]{:S(2)}, u32[]{:S(2)}) collective-permute-start(bf16[64,512]{1,0:T(8,128)(2,1)} %bitcast.8), channel_id=1, source_target_pairs={{0,4},{1,5},{2,6},{3,7},{4,0},{5,1},{6,2},{7,3},{8,9},{9,8},{10,11... | collective-permute-start | bytes 196616 | tf_op jit(solution)/shard_map/ppermute | solution.py:218
  0.7 9.5 %collective-permute-start.1 = (bf16[64,512]{1,0:T(8,128)(2,1)}, bf16[64,512]{1,0:T(8,128)(2,1)S(1)}, u32[]{:S(2)}, u32[]{:S(2)}) collective-permute-start(bf16[64,512]{1,0:T(8,128)(2,1)} %bitcast.9), channel_id=1, source_target_pairs={{0,1},{1,0},{2,3},{3,2},{4,5},{5,4},{6,7},{7,6},{8,9},{9,8},{10,11... | collective-permute-start | bytes 196616 | tf_op jit(solution)/shard_map/ppermute | solution.py:207
  0.7 9.0 %collective-permute-start.2 = (bf16[64,512]{1,0:T(8,128)(2,1)}, bf16[64,512]{1,0:T(8,128)(2,1)S(1)}, u32[]{:S(2)}, u32[]{:S(2)}) collective-permute-start(bf16[64,512]{1,0:T(8,128)(2,1)} %bitcast.10), channel_id=1, source_target_pairs={{0,2},{1,3},{2,0},{3,1},{4,6},{5,7},{6,4},{7,5},{8,9},{9,8},{10,11... | collective-permute-start | bytes 196616 | tf_op jit(solution)/shard_map/ppermute | solution.py:218
  1.2 8.6 %collective-permute-start.3 = (bf16[64,512]{1,0:T(8,128)(2,1)}, bf16[64,512]{1,0:T(8,128)(2,1)S(1)}, u32[]{:S(2)}, u32[]{:S(2)}) collective-permute-start(bf16[64,512]{1,0:T(8,128)(2,1)} %bitcast.11), channel_id=1, source_target_pairs={{0,6},{1,7},{2,4},{3,5},{4,2},{5,3},{6,0},{7,1},{8,9},{9,8},{10,11... | collective-permute-start | bytes 196616 | tf_op jit(solution)/shard_map/ppermute | solution.py:218
  9.1 1.5 %collective-permute-start.4 = (bf16[64,512]{1,0:T(8,128)(2,1)S(1)}, bf16[64,512]{1,0:T(8,128)(2,1)S(1)}, u32[]{:S(2)}, u32[]{:S(2)}) collective-permute-start(bf16[64,512]{1,0:T(8,128)(2,1)S(1)} %collective-permute-done.refs_3_), channel_id=1, source_target_pairs={{0,1},{1,0},{2,3},{3,2},{4,5},{5,4},{6,7},{7,6},{8,9},{9,8},{10,11... | collective-permute-start | bytes 196616 | tf_op jit(solution)/shard_map/ppermute | solution.py:207
  9.8 1.3 %collective-permute-start.6 = (bf16[64,512]{1,0:T(8,128)(2,1)S(1)}, bf16[64,512]{1,0:T(8,128)(2,1)S(1)}, u32[]{:S(2)}, u32[]{:S(2)}) collective-permute-start(bf16[64,512]{1,0:T(8,128)(2,1)S(1)} %collective-permute-done.3.refs_5_), channel_id=1, source_target_pairs={{0,1},{1,0},{2,3},{3,2},{4,5},{5,4},{6,7},{7,6},{8,9},{9,8},{10,11... | collective-permute-start | bytes 196616 | tf_op jit(solution)/shard_map/ppermute | solution.py:207
  11.1 2.5 %collective-permute-start.7 = (bf16[64,512]{1,0:T(8,128)(2,1)S(1)}, bf16[64,512]{1,0:T(8,128)(2,1)S(1)}, u32[]{:S(2)}, u32[]{:S(2)}) collective-permute-start(bf16[64,512]{1,0:T(8,128)(2,1)S(1)} %late_tile.4.refs_3_), channel_id=1, source_target_pairs={{0,12},{1,13},{2,14},{3,15},{4,8},{5,9},{6,10},{7,11},{8,16},{9,17... | collective-permute-start | bytes 196616 | tf_op jit(solution)/shard_map/ppermute | solution.py:218
  11.5 2.3 %collective-permute-start.9 = (bf16[64,512]{1,0:T(8,128)(2,1)S(1)}, bf16[64,512]{1,0:T(8,128)(2,1)S(1)}, u32[]{:S(2)}, u32[]{:S(2)}) collective-permute-start(bf16[64,512]{1,0:T(8,128)(2,1)S(1)} %late_tile.4.refs_3_), channel_id=1, source_target_pairs={{0,10},{1,11},{2,8},{3,9},{4,14},{5,15},{6,12},{7,13}} | collective-permute-start | bytes 196616 | tf_op jit(solution)/shard_map/ppermute | solution.py:218
  12.2 2.0 %collective-permute-start.11 = (bf16[64,512]{1,0:T(8,128)(2,1)S(1)}, bf16[64,512]{1,0:T(8,128)(2,1)S(1)}, u32[]{:S(2)}, u32[]{:S(2)}) collective-permute-start(bf16[64,512]{1,0:T(8,128)(2,1)S(1)} %late_tile.4.refs_3_), channel_id=1, source_target_pairs={{0,14},{1,15},{2,12},{3,13},{4,10},{5,11},{6,8},{7,9}} | collective-permute-start | bytes 196616 | tf_op jit(solution)/shard_map/ppermute | solution.py:218
  12.9 1.5 %collective-permute-start.13 = (bf16[64,512]{1,0:T(8,128)(2,1)S(1)}, bf16[64,512]{1,0:T(8,128)(2,1)S(1)}, u32[]{:S(2)}, u32[]{:S(2)}) collective-permute-start(bf16[64,512]{1,0:T(8,128)(2,1)S(1)} %late_tile.4.refs_3_), channel_id=1, source_target_pairs={{0,8},{1,9},{2,10},{3,11},{4,12},{5,13},{6,14},{7,15}} | collective-permute-start | bytes 196616 | tf_op jit(solution)/shard_map/ppermute | solution.py:218
  15.6 9.7 %collective-permute-start.15 = (bf16[64,512]{1,0:T(8,128)(2,1)S(1)}, bf16[64,512]{1,0:T(8,128)(2,1)S(1)}, u32[]{:S(2)}, u32[]{:S(2)}) collective-permute-start(bf16[64,512]{1,0:T(8,128)(2,1)S(1)} %late_tile.5.refs_3_), channel_id=1, source_target_pairs={{8,20},{9,21},{10,22},{11,23},{12,16},{13,17},{14,18},{15,19},{16,... | collective-permute-start | bytes 196616 | tf_op jit(solution)/shard_map/ppermute | solution.py:218
  23.2 2.6 %collective-permute-start.17 = (bf16[64,512]{1,0:T(8,128)(2,1)S(1)}, bf16[64,512]{1,0:T(8,128)(2,1)S(1)}, u32[]{:S(2)}, u32[]{:S(2)}) collective-permute-start(bf16[64,512]{1,0:T(8,128)(2,1)S(1)} %late_tile.5.refs_3_), channel_id=1, source_target_pairs={{8,18},{9,19},{10,16},{11,17},{12,22},{13,23},{14,20},{15,21}} | collective-permute-start | bytes 196616 | tf_op jit(solution)/shard_map/ppermute | solution.py:218
  23.9 2.0 %collective-permute-start.19 = (bf16[64,512]{1,0:T(8,128)(2,1)S(1)}, bf16[64,512]{1,0:T(8,128)(2,1)S(1)}, u32[]{:S(2)}, u32[]{:S(2)}) collective-permute-start(bf16[64,512]{1,0:T(8,128)(2,1)S(1)} %late_tile.5.refs_3_), channel_id=1, source_target_pairs={{8,22},{9,23},{10,20},{11,21},{12,18},{13,19},{14,16},{15,17}} | collective-permute-start | bytes 196616 | tf_op jit(solution)/shard_map/ppermute | solution.py:218
  24.6 1.8 %collective-permute-start.21 = (bf16[64,512]{1,0:T(8,128)(2,1)S(1)}, bf16[64,512]{1,0:T(8,128)(2,1)S(1)}, u32[]{:S(2)}, u32[]{:S(2)}) collective-permute-start(bf16[64,512]{1,0:T(8,128)(2,1)S(1)} %late_tile.5.refs_3_), channel_id=1, source_target_pairs={{8,16},{9,17},{10,18},{11,19},{12,20},{13,21},{14,22},{15,23}} | collective-permute-start | bytes 196616 | tf_op jit(solution)/shard_map/ppermute | solution.py:218
  25.3 1.4 %collective-permute-start.16 = (bf16[64,512]{1,0:T(8,128)(2,1)S(1)}, bf16[64,512]{1,0:T(8,128)(2,1)S(1)}, u32[]{:S(2)}, u32[]{:S(2)}) collective-permute-start(bf16[64,512]{1,0:T(8,128)(2,1)S(1)} %collective-permute-done.15.refs_2_), channel_id=1, source_target_pairs={{0,1},{1,0},{2,3},{3,2},{4,5},{5,4},{6,7},{7,6},{8,9},{9,8},{10,11... | collective-permute-start | bytes 196616 | tf_op jit(solution)/shard_map/ppermute | solution.py:207
  25.9 1.3 %collective-permute-start.20 = (bf16[64,512]{1,0:T(8,128)(2,1)S(1)}, bf16[64,512]{1,0:T(8,128)(2,1)S(1)}, u32[]{:S(2)}, u32[]{:S(2)}) collective-permute-start(bf16[64,512]{1,0:T(8,128)(2,1)S(1)} %collective-permute-done.19.refs_3_), channel_id=1, source_target_pairs={{0,1},{1,0},{2,3},{3,2},{4,5},{5,4},{6,7},{7,6},{8,9},{9,8},{10,11... | collective-permute-start | bytes 196616 | tf_op jit(solution)/shard_map/ppermute | solution.py:207
  27.6 11.1 %collective-permute-start.23 = (bf16[64,512]{1,0:T(8,128)(2,1)S(1)}, bf16[64,512]{1,0:T(8,128)(2,1)S(1)}, u32[]{:S(2)}, u32[]{:S(2)}) collective-permute-start(bf16[64,512]{1,0:T(8,128)(2,1)S(1)} %late_tile.6.refs_3_), channel_id=1, source_target_pairs={{16,28},{17,29},{18,30},{19,31},{20,24},{21,25},{22,26},{23,27},{2... | collective-permute-start | bytes 196616 | tf_op jit(solution)/shard_map/ppermute | solution.py:218
  27.6 12.0 %collective-permute-start.25 = (bf16[64,512]{1,0:T(8,128)(2,1)S(1)}, bf16[64,512]{1,0:T(8,128)(2,1)S(1)}, u32[]{:S(2)}, u32[]{:S(2)}) collective-permute-start(bf16[64,512]{1,0:T(8,128)(2,1)S(1)} %late_tile.6.refs_3_), channel_id=1, source_target_pairs={{16,26},{17,27},{18,24},{19,25},{20,30},{21,31},{22,28},{23,29},{2... | collective-permute-start | bytes 196616 | tf_op jit(solution)/shard_map/ppermute | solution.py:218
  32.1 8.5 %collective-permute-start.27 = (bf16[64,512]{1,0:T(8,128)(2,1)S(1)}, bf16[64,512]{1,0:T(8,128)(2,1)S(1)}, u32[]{:S(2)}, u32[]{:S(2)}) collective-permute-start(bf16[64,512]{1,0:T(8,128)(2,1)S(1)} %late_tile.6.refs_3_), channel_id=1, source_target_pairs={{16,30},{17,31},{18,28},{19,29},{20,26},{21,27},{22,24},{23,25}} | collective-permute-start | bytes 196616 | tf_op jit(solution)/shard_map/ppermute | solution.py:218
  33.4 8.3 %collective-permute-start.29 = (bf16[64,512]{1,0:T(8,128)(2,1)S(1)}, bf16[64,512]{1,0:T(8,128)(2,1)S(1)}, u32[]{:S(2)}, u32[]{:S(2)}) collective-permute-start(bf16[64,512]{1,0:T(8,128)(2,1)S(1)} %late_tile.6.refs_3_), channel_id=1, source_target_pairs={{16,24},{17,25},{18,26},{19,27},{20,28},{21,29},{22,30},{23,31},{2... | collective-permute-start | bytes 196616 | tf_op jit(solution)/shard_map/ppermute | solution.py:218
  38.7 3.3 %collective-permute-start.24 = (bf16[64,512]{1,0:T(8,128)(2,1)S(1)}, bf16[64,512]{1,0:T(8,128)(2,1)S(1)}, u32[]{:S(2)}, u32[]{:S(2)}) collective-permute-start(bf16[64,512]{1,0:T(8,128)(2,1)S(1)} %collective-permute-done.23.refs_2_), channel_id=1, source_target_pairs={{0,1},{1,0},{2,3},{3,2},{4,5},{5,4},{6,7},{7,6},{8,9},{9,8},{10,11... | collective-permute-start | bytes 196616 | tf_op jit(solution)/shard_map/ppermute | solution.py:207
  39.6 2.8 %collective-permute-start.26 = (bf16[64,512]{1,0:T(8,128)(2,1)S(1)}, bf16[64,512]{1,0:T(8,128)(2,1)S(1)}, u32[]{:S(2)}, u32[]{:S(2)}) collective-permute-start(bf16[64,512]{1,0:T(8,128)(2,1)S(1)} %collective-permute-done.25.refs_4_), channel_id=1, source_target_pairs={{0,1},{1,0},{2,3},{3,2},{4,5},{5,4},{6,7},{7,6},{8,9},{9,8},{10,11... | collective-permute-start | bytes 196616 | tf_op jit(solution)/shard_map/ppermute | solution.py:207
  40.6 2.1 %collective-permute-start.28 = (bf16[64,512]{1,0:T(8,128)(2,1)S(1)}, bf16[64,512]{1,0:T(8,128)(2,1)S(1)}, u32[]{:S(2)}, u32[]{:S(2)}) collective-permute-start(bf16[64,512]{1,0:T(8,128)(2,1)S(1)} %collective-permute-done.27.refs_3_), channel_id=1, source_target_pairs={{0,1},{1,0},{2,3},{3,2},{4,5},{5,4},{6,7},{7,6},{8,9},{9,8},{10,11... | collective-permute-start | bytes 196616 | tf_op jit(solution)/shard_map/ppermute | solution.py:207
  41.7 1.4 %collective-permute-start.30 = (bf16[64,512]{1,0:T(8,128)(2,1)S(1)}, bf16[64,512]{1,0:T(8,128)(2,1)S(1)}, u32[]{:S(2)}, u32[]{:S(2)}) collective-permute-start(bf16[64,512]{1,0:T(8,128)(2,1)S(1)} %collective-permute-done.29.refs_3_), channel_id=1, source_target_pairs={{0,1},{1,0},{2,3},{3,2},{4,5},{5,4},{6,7},{7,6},{8,9},{9,8},{10,11... | collective-permute-start | bytes 196616 | tf_op jit(solution)/shard_map/ppermute | solution.py:207
  (8 other events, 16.5 us)
